TPU v7x, 128 devices: a whole 4x4x4 slice. The times are simulated.
128 devices in a mesh: sect: 8 (over z, core), rows: 16 (over x, y).
Axes of the slice: x: 4, y: 4, z: 4, core: 2. Of those that a mesh axis runs over, the one named last changes fastest.
Arguments:
- a_tiles: bfloat16 [2048, 27, 128, 128], P(('sect', 'rows')), may hold values from -0.109375 to 0.109375
- a_cols: int32 [2048, 27], P(('sect', 'rows')), may hold values from 0 to 2047, as said below
- a_count: int32 [2048], P(('sect', 'rows')), may hold values from 1 to 27, as said below
- p_tiles: bfloat16 [2048, 128, 128], P(('sect', 'rows')), may hold values from -0.125 to 0.125
- coarse_map: int32 [2048], P(('sect', 'rows')), may hold values from 0 to 127, as said below
- p_coarse: float32 [16384, 256], P(('sect', 'rows')), may hold values from -0.046875 to 0.046875
Outputs:
- coarse_one: float32 [16384, 2048], P(('sect', 'rows'))
- coarsest: float32 [256, 256], replicated
Inputs may be any that keep to these rules, and one draw needn't show every extreme that they name: `a_cols`: slot 0 of each block row names its own block; every column block lies on the same device as its row or on the device one before or after it along rows, in the same section. `a_count`: some block row of every device uses all 27 slots. `coarse_map`: fine block row i of section s aggregates into one of the coarse blocks s * 16 to s * 16 + 15.
All inputs are finite; a program needn't handle non-finite values.
Results may differ from a plain program's by a relative error of at most 0.0029.
Values may be sent and summed in bfloat16 or wider, within the bound.
No kernel may reach another device: no remote copies, remote signals or barrier semaphores. Data moves between devices by JAX's collectives and lax.ppermute only.
A program may use at most 128 MiB of HBM per device.

v0:
```python
import jax
import jax.numpy as jnp
from jax import lax
from jax.sharding import PartitionSpec as P

CBS = 16


def extended(cells, sides, width):
    for axis, dim in sides:
        count = lax.axis_size(axis)
        ends = count - 1
        head = lax.slice_in_dim(cells, 0, width, axis=dim)
        tail = lax.slice_in_dim(cells, cells.shape[dim] - width, cells.shape[dim], axis=dim)
        cells = jnp.concatenate(
            [
                lax.ppermute(tail, axis, [(i, (i + 1) % count) for i in range(ends)]),
                cells,
                lax.ppermute(head, axis, [((i + 1) % count, i) for i in range(ends)]),
            ],
            axis=dim,
        )
    return cells


def per_device(a_tiles, a_cols, a_count, p_tiles, coarse_map, p_coarse):
    block_rows = a_tiles.shape[0]
    slot_count = a_tiles.shape[1]
    tile_size = a_tiles.shape[2]
    row_devices = lax.axis_size("rows")
    section = lax.axis_index("sect")
    position = lax.axis_index("rows")
    tables = (
        extended(p_tiles, (("rows", 0),), block_rows),
        extended(coarse_map, (("rows", 0),), block_rows),
    )
    offsets = a_cols - (section * row_devices + position - 1) * block_rows
    picked = jnp.take(tables[0], offsets, axis=0, mode="clip")
    picked_map = jnp.take(tables[1], offsets, axis=0, mode="clip")
    in_use = jnp.arange(slot_count, dtype=jnp.int32)[None, :] < a_count[:, None]
    products = jnp.einsum("lkij,lkjy->lkiy", a_tiles, picked, preferred_element_type=jnp.float32)
    coarse_tiles = jnp.where(in_use[:, :, None, None], products, 0.0).astype(jnp.bfloat16)
    block_ids = jnp.arange(CBS, dtype=jnp.int32)
    row_onehot = ((coarse_map - section * CBS)[:, None] == block_ids).astype(jnp.float32)
    col_onehot = ((picked_map - section * CBS)[:, :, None] == block_ids).astype(jnp.bfloat16)
    grouped = jnp.einsum(
        "lkb,lkiy->lbiy", col_onehot, coarse_tiles, preferred_element_type=jnp.float32
    )
    projected = jnp.einsum(
        "lix,lbiy->lbxy", p_tiles.astype(jnp.float32), grouped, precision=lax.Precision.HIGHEST
    )
    width = CBS * tile_size
    partial_sum = jnp.einsum(
        "la,lbxy->axby", row_onehot, projected, precision=lax.Precision.HIGHEST
    ).reshape(width, width)
    section_prolong = lax.all_gather(p_coarse, "rows", axis=0, tiled=True)
    owned_rows = lax.psum_scatter(partial_sum, "rows", scatter_dimension=0, tiled=True)
    applied = jnp.dot(owned_rows, section_prolong, precision=lax.Precision.HIGHEST)
    own_term = jnp.dot(p_coarse.T, applied, precision=lax.Precision.HIGHEST)
    coarsest = lax.psum(own_term, ("sect", "rows"))
    return (owned_rows, coarsest)


def solution(mesh):
    placed = (
        P(("sect", "rows"), None, None, None),
        P(("sect", "rows"), None),
        P(("sect", "rows")),
        P(("sect", "rows"), None, None),
        P(("sect", "rows")),
        P(("sect", "rows"), None),
    )
    return jax.shard_map(
        per_device,
        mesh=mesh,
        in_specs=placed,
        out_specs=(P(("sect", "rows"), None), P()),
        check_vma=False,
    )
```

profile of v0, /device:TPU:1, one launch (start us, length us, event | category | flops | bytes accessed | tf_op | source)
XLA Modules:
  0.0 457.8 jit_solution(12774928957819170570)
XLA Ops:
  7.2 0.0 all-gather.2.cloned.1.call-start
  7.2 4.0 collective-permute-start
  11.2 1.3 collective-permute-start.1
  12.5 4.0 collective-permute-start.2
  16.6 1.3 collective-permute-start.3
  17.9 0.0 all-gather.2.cloned.1.call-update
  17.9 0.0 reduce-scatter.2.cloned.1.call-start
  18.0 0.7 iota_compare_fusion.2
  18.7 0.7 broadcast_subtract_fusion
  19.4 0.7 broadcast_subtract_fusion.2
  20.0 0.1 reshape.35
  20.1 0.0 collective-permute-done
  20.2 0.0 collective-permute-done.1
  20.2 0.7 pad_add_fusion
  20.9 3.0 gather_fusion
  23.9 0.1 reshape.54
  24.0 2.8 collective-permute-done.2
  26.8 3.8 collective-permute-done.3
  30.6 1.2 pad_maximum_fusion
  31.8 13.2 %gather_fusion.1 = bf16[432,128,128]{2,1,0:T(8,128)(2,1)} fusion(bf16[48,128,128]{2,1,0:T(8,128)(2,1)S(1)} %pad_maximum_fusion, s32[1024]{0:T(1024)S(1)} %pad_clamp_fusion), kind=kCustom, calls=%fused_computation.1 | custom fusion | bytes 28313280 | tf_op jit(solution)/shard_map/jit(_take)/gather | solution.py:38
  45.0 20.4 %fusion.4 = bf16[16,27,128,128]{2,3,1,0:T(8,128)(2,1)} fusion(pred[16,27]{1,0:T(8,128)(4,1)S(1)} %iota_compare_fusion.2, bf16[16,27,128,128]{3,2,1,0:T(8,128)(2,1)} %bitcast.39, bf16[16,27,128,128]{3,2,1,0:T(8,128)(2,1)} %param.6), kind=kOutput, calls=%fused_computation.8 | convolution fusion | flops 1826095104 | bytes 42467760 | tf_op jit(solution)/shard_map/lkij,lkjy->lkiy/dot_general | solution.py:41
  65.4 24.5 %copy.12 = bf16[16,27,128,128]{3,1,2,0:T(8,128)(2,1)} copy(bf16[16,27,128,128]{2,3,1,0:T(8,128)(2,1)} %fusion.4) | data formatting | bytes 28311552 | tf_op jit(solution)/shard_map/convert_element_type | solution.py:42
  89.9 0.0 copy-start
  89.9 10.6 %fusion.10 = f32[16,16,128,128]{3,1,2,0:T(8,128)} fusion(bf16[16,27,128,128]{3,1,2,0:T(8,128)(2,1)} %copy.12, s32[16,27]{1,0:T(8,128)S(1)} %reshape.54), kind=kOutput, calls=%fused_computation.15 | convolution fusion | flops 226499328 | bytes 30934720 | tf_op jit(solution)/shard_map/lkb,lkiy->lbiy/dot_general | solution.py:46
  100.5 0.0 copy-done
  100.5 24.3 %fusion.2 = f32[16,16,128,128]{3,2,1,0:T(8,128)} fusion(f32[16,16,128,128]{3,1,2,0:T(8,128)} %fusion.10, bf16[16,128,128]{2,1,0:T(8,128)(2,1)S(1)} %copy-done), kind=kOutput, calls=%fused_computation.6 | convolution fusion | flops 6442450944 | bytes 34078720 | tf_op jit(solution)/shard_map/lix,lbiy->lbxy/dot_general | solution.py:49
  124.8 17.6 %copy.15 = f32[16,16,128,128]{2,0,3,1:T(8,128)} copy(f32[16,16,128,128]{3,2,1,0:T(8,128)} %fusion.2) | data formatting | bytes 33554432 | tf_op jit(solution)/shard_map/lix,lbiy->lbxy/dot_general | solution.py:49
  142.4 14.9 %fusion.5 = f32[16,128,16,128]{3,0,1,2:T(8,128)} fusion(f32[16,16,128,128]{2,0,3,1:T(8,128)} %copy.15, s32[16]{0:T(128)S(1)} %broadcast_subtract_fusion.2), kind=kOutput, calls=%fused_computation.9 | convolution fusion | flops 805306624 | bytes 33554496 | tf_op jit(solution)/shard_map/la,lbxy->axby/dot_general | solution.py:53
  157.4 15.3 %copy.9 = f32[16,128,16,128]{3,2,1,0:T(8,128)S(1)} copy(f32[16,128,16,128]{3,0,1,2:T(8,128)} %fusion.5) | data formatting | bytes 33554432 | tf_op jit(solution)/shard_map/la,lbxy->axby/transpose | solution.py:53
  172.6 11.2 %copy.21 = f32[256,8,16,128]{3,1,2,0:T(8,128)} copy(f32[256,8,16,128]{3,2,1,0:T(8,128)S(1)} %bitcast.41) | data formatting | bytes 33554432
  183.8 0.0 copy-start.1
  183.8 0.0 reduce-scatter.2.cloned.1.call-update
  183.9 0.0 all-reduce.2.cloned.1.call-start
  183.9 0.0 all-gather.2.cloned.1.call-done
  183.9 118.5 %reduce-scatter.2.cloned.1.call-done = f32[128,2048]{1,0:T(8,128)} async-done(((f32[2048,2048]{1,0:T(8,128)}), f32[128,2048]{1,0:T(8,128)}) %reduce-scatter.2.cloned.1.call-update) | async-done | bytes 1048592 | tf_op jit(solution)/shard_map/reduce_scatter | solution.py:57
  302.5 3.0 fusion.16
  305.5 0.0 copy-done.1
  305.5 1.1 convolution_bitcast_fusion
  306.6 0.0 all-reduce.2.cloned.1.call-update
  306.7 142.8 %all-reduce.2.cloned.1.call-done = f32[256,256]{0,1:T(8,128)} async-done(((f32[256,256]{0,1:T(8,128)}), f32[256,256]{0,1:T(8,128)}) %all-reduce.2.cloned.1.call-update) | async-done | bytes 262160 | tf_op jit(solution)/shard_map/psum | solution.py:60
  449.4 1.8 copy.10
  (2 shorter events, 0.0 us)
Async XLA Ops:
  7.2 176.8 %all-gather.2.cloned.1.call-start = ((), (), s32[]{:S(2)}) async-start(), calls=%async_computation.2 | async-start | bytes 2228224 | tf_op jit(solution)/shard_map/all_gather | solution.py:56
  7.2 12.9 %collective-permute-start = (s32[16]{0:T(128)}, s32[16]{0:T(128)S(1)}, u32[]{:S(2)}, u32[]{:S(2)}) collective-permute-start(s32[16]{0:T(128)} %param.10), channel_id=1, source_target_pairs={{0,1},{1,2},{2,3},{3,4},{4,5},{5,6},{6,7},{7,8},{8,9},{9,10},{10,1... | collective-permute-start | bytes 200 | tf_op jit(solution)/shard_map/ppermute | solution.py:17
  11.2 8.9 %collective-permute-start.1 = (s32[16]{0:T(128)}, s32[16]{0:T(128)S(1)}, u32[]{:S(2)}, u32[]{:S(2)}) collective-permute-start(s32[16]{0:T(128)} %param.10), channel_id=1, source_target_pairs={{1,0},{2,1},{3,2},{4,3},{5,4},{6,5},{7,6},{8,7},{9,8},{10,9},{11,1... | collective-permute-start | bytes 200 | tf_op jit(solution)/shard_map/ppermute | solution.py:19
  12.5 14.3 %collective-permute-start.2 = (bf16[16,128,128]{2,1,0:T(8,128)(2,1)}, bf16[16,128,128]{2,1,0:T(8,128)(2,1)S(1)}, u32[]{:S(2)}, u32[]{:S(2)}) collective-permute-start(bf16[16,128,128]{2,1,0:T(8,128)(2,1)} %param.9), channel_id=1, source_target_pairs={{0,1},{1,2},{2,3},{3,4},{4,5},{5,6},{6,7},{7,8},{8,9},{9,10},{10,1... | collective-permute-start | bytes 1572872 | tf_op jit(solution)/shard_map/ppermute | solution.py:17
  16.6 14.0 %collective-permute-start.3 = (bf16[16,128,128]{2,1,0:T(8,128)(2,1)}, bf16[16,128,128]{2,1,0:T(8,128)(2,1)S(1)}, u32[]{:S(2)}, u32[]{:S(2)}) collective-permute-start(bf16[16,128,128]{2,1,0:T(8,128)(2,1)} %param.9), channel_id=1, source_target_pairs={{1,0},{2,1},{3,2},{4,3},{5,4},{6,5},{7,6},{8,7},{9,8},{10,9},{11,1... | collective-permute-start | bytes 1572872 | tf_op jit(solution)/shard_map/ppermute | solution.py:19
  17.9 284.5 %reduce-scatter.2.cloned.1.call-start = ((), (), s32[]{:S(2)}) async-start(), calls=%async_computation.1 | async-start | bytes 17825792 | tf_op jit(solution)/shard_map/reduce_scatter | solution.py:57
  89.9 10.6 %copy-start = (bf16[16,128,128]{2,1,0:T(8,128)(2,1)S(1)}, bf16[16,128,128]{2,1,0:T(8,128)(2,1)}, u32[]{:S(2)}) copy-start(bf16[16,128,128]{2,1,0:T(8,128)(2,1)} %param.9) | copy-start | bytes 1572868
  183.8 121.7 %copy-start.1 = (f32[128,256]{1,0:T(8,128)S(1)}, f32[128,256]{1,0:T(8,128)}, u32[]{:S(2)}) copy-start(f32[128,256]{1,0:T(8,128)} %param.11) | copy-start | bytes 393220
  183.9 265.6 %all-reduce.2.cloned.1.call-start = ((), (), s32[]{:S(2)}) async-start(), calls=%async_computation.3 | async-start | bytes 524288 | tf_op jit(solution)/shard_map/psum | solution.py:60
Sparse Core Ops, SparseCore 0:
  18.0 49.8 all-gather.1
  184.0 118.4 reduce-scatter.1
  307.8 141.6 all-reduce.1
where the time goes:
time: 459 us; the launch traced here: 458 us
  waiting for transfers between devices  268 us (58%)
  local copies, waits for them, and re-layouts  86.8 us (19%)
  matrix products  74.3 us (16%)
  between operations  13.9 us (3%)
  starting transfers between devices  10.8 us (2%)
    psum x1, waiting for transfers between devices, per_device(): coarsest = lax.psum(own_term, ('sect', 'rows'))  143 us
    reduce_scatter x1, waiting for transfers between devices, per_device(): lax.psum_scatter(partial_sum, 'rows', scatter_dimension=0, tiled=True)  119 us
    convert_element_type x1, local copies, waits for them, and re-layouts, per_device(): jnp.where(in_use[:, :, None, None], products, 0.0).astype(jnp.bfloat16)  24.5 us
    dot_general x1, matrix products, per_device(): jnp.einsum('lix,lbiy->lbxy', p_tiles.astype(jnp.float32), grouped, precis...  24.3 us
    dot_general x1, matrix products, per_device(): jnp.einsum('lkij,lkjy->lkiy', a_tiles, picked, preferred_element_type=jnp...  20.4 us
    dot_general x1, local copies, waits for them, and re-layouts, per_device(): jnp.einsum('lix,lbiy->lbxy', p_tiles.astype(jnp.float32), grouped, precis...  17.6 us
    transpose x1, local copies, waits for them, and re-layouts, per_device(): jnp.einsum('la,lbxy->axby', row_onehot, projected, precision=lax.Precisio...  15.3 us
    dot_general x1, matrix products, per_device(): jnp.einsum('la,lbxy->axby', row_onehot, projected, precision=lax.Precisio...  14.9 us
  transfers between devices with their start and end apart: 7, of which 4 were waited for; matrix products, arithmetic and copies ran while one was open for 35% of the time, Pallas kernels for 0%

commit v1 on v0

v1 whole, which is shorter than its diff:
```python
import functools

import jax
import jax.numpy as jnp
from jax import lax
from jax.experimental import pallas as pl
from jax.experimental.pallas import tpu as pltpu
from jax.sharding import PartitionSpec as P

CBS = 16
TILE = 128
RB = 16
KA = 27
GROUP = 9
SIDE = 4
WIDTH = CBS * TILE
C2 = 256

HALF_A = (2, 1)
HALF_B = (3, 0)
FAR = [2 * SIDE + dv for dv in HALF_A + HALF_B]
NEXT_ALONE = [1 * SIDE + dv for dv in HALF_B] + [3 * SIDE + dv for dv in HALF_A]
OWN = [0 * SIDE + dv for dv in HALF_A + HALF_B]
NEXT_JOINED = [1 * SIDE + dv for dv in HALF_A] + [3 * SIDE + dv for dv in HALF_B]
SEQUENCE = FAR + NEXT_ALONE + NEXT_JOINED + OWN
PAIRS = len(SEQUENCE) // 2
COUNT, ORDER, STARTS, INFO = KA, KA + 1, KA + 2, KA + 3
Q_SCALE = 2.0**20


def cost(microseconds):
    return pl.CostEstimate(flops=0, bytes_accessed=int(microseconds * 3.7e6), transcendentals=0)


def plan_body(cols, counts, own_map, info, table):
    def fill(i, _):
        for k in range(KA):
            table[i, k] = cols[i, k] - info[4]
        table[i, COUNT] = counts[i]
        table[i, INFO] = info[lax.min(i, 7)]
        return 0

    lax.fori_loop(0, RB, fill, 0)
    first_core = info[1] == 0
    names = []
    for i in range(RB):
        block = own_map[i] - info[0]
        high, low = lax.shift_right_logical(block, 2), lax.bitwise_and(block, 3)
        du = lax.bitwise_and(jnp.where(first_core, high, low) - info[2], 3)
        dv = lax.bitwise_and(jnp.where(first_core, low, high) - info[3], 3)
        names.append(du * SIDE + dv)
    n = jnp.int32(0)
    for j, code in enumerate(SEQUENCE):
        table[j, STARTS] = n
        for i in range(RB):
            table[n, ORDER] = jnp.int32(i)
            n = n + (names[i] == code).astype(jnp.int32)
    table[len(SEQUENCE), STARTS] = n


def row_plan(*operands):
    smem = pl.BlockSpec(memory_space=pltpu.SMEM)
    return pl.pallas_call(
        plan_body,
        out_shape=jax.ShapeDtypeStruct((RB + 1, 32), jnp.int32),
        in_specs=[smem] * len(operands),
        out_specs=smem,
        cost_estimate=cost(3),
    )(*operands)


def galerkin_body(table, maps, a_ref, left_ref, own_ref, right_ref, _, *rest):
    outs, (a_buf, tiles, acc, stage, a_sem, p_sem, out_sem) = rest[:PAIRS], rest[PAIRS:]

    def fetch(r):
        slot = lax.rem(r, 2)
        return pltpu.make_async_copy(a_ref.at[table[r, ORDER]], a_buf.at[slot], a_sem.at[slot])

    fetch(0).start()
    loads = [
        pltpu.make_async_copy(src.at[pl.ds(0, RB)], tiles.at[pl.ds(n * RB, RB)], p_sem.at[n])
        for n, src in enumerate((left_ref, own_ref, right_ref))
    ]
    for load in loads:
        load.start()
    acc[...] = jnp.zeros_like(acc)
    for load in loads:
        load.wait()

    def row(r, _):
        @pl.when(r + 1 < RB)
        def _():
            fetch(r + 1).start()

        fetch(r).wait()
        i = table[r, ORDER]
        slot = lax.rem(r, 2)
        count = table[i, COUNT]
        left = tiles[RB + i].T
        for k in range(0, KA, 2):
            products, places = [], []
            for s in range(k, min(k + 2, KA)):
                col = jnp.clip(table[i, s], 0, 3 * RB - 1)
                block = jnp.clip(maps[lax.shift_right_logical(col, 4), lax.bitwise_and(col, RB - 1)], 0, CBS - 1)
                places.append(pl.multiple_of(jnp.where(s < count, block, CBS) * TILE, TILE))
                products.append(
                    jnp.dot(a_buf[slot, s], tiles[col], preferred_element_type=jnp.float32).astype(jnp.bfloat16)
                )
            terms = jnp.dot(left, jnp.concatenate(products, axis=1), preferred_element_type=jnp.float32)
            for n, place in enumerate(places):
                acc[:, pl.ds(place, TILE)] += terms[:, n * TILE:(n + 1) * TILE]
        return 0

    def leave(n, half):
        return pltpu.make_async_copy(stage.at[half], outs[n].at[half], out_sem.at[half])

    def block(t, _):
        pair, half = lax.div(t, 2), lax.rem(t, 2)
        lax.fori_loop(table[t, STARTS], table[t + 1, STARTS], row, 0)

        @pl.when(pair > 0)
        def _():
            leave(0, half).wait()

        for first in range(0, WIDTH, TILE):
            columns = pl.ds(first, TILE)
            stage[half, :, columns] = acc[:, columns].astype(jnp.bfloat16)
            acc[:, columns] = jnp.zeros((TILE, TILE), jnp.float32)
        for n in range(PAIRS):
            @pl.when(pair == n)
            def _(n=n):
                leave(n, half).start()
        return 0

    lax.fori_loop(0, 2 * PAIRS, block, 0)
    for half in range(2):
        leave(0, half).wait()


def galerkin(table, maps, a_tiles, left, own, right, after_this):
    anywhere = pl.BlockSpec(memory_space=pl.ANY)
    return pl.pallas_call(
        galerkin_body,
        out_shape=[jax.ShapeDtypeStruct((2, TILE, WIDTH), jnp.bfloat16)] * PAIRS,
        grid_spec=pltpu.PrefetchScalarGridSpec(
            num_scalar_prefetch=2,
            grid=(1,),
            in_specs=[pl.BlockSpec(memory_space=pltpu.HBM)] + [anywhere] * 4,
            out_specs=[anywhere] * PAIRS,
            scratch_shapes=[
                pltpu.VMEM((2, KA, TILE, TILE), jnp.bfloat16),
                pltpu.VMEM((3 * RB, TILE, TILE), jnp.bfloat16),
                pltpu.VMEM((TILE, WIDTH + TILE), jnp.float32),
                pltpu.VMEM((2, TILE, WIDTH), jnp.bfloat16),
                pltpu.SemaphoreType.DMA((2,)),
                pltpu.SemaphoreType.DMA((3,)),
                pltpu.SemaphoreType.DMA((2,)),
            ],
        ),
        compiler_params=pltpu.CompilerParams(vmem_limit_bytes=52 * 1024 * 1024),
        cost_estimate=cost(20),
    )(table, maps, a_tiles, left, own, right, after_this)


def coarsest_body(table, *refs):
    parts = refs[:PAIRS]
    high_ref, low_ref, out_ref, right, rest = refs[PAIRS:]
    step = pl.program_id(0)

    def block_at(u, v):
        u, v = lax.bitwise_and(table[2, INFO] + u, 3), lax.bitwise_and(table[3, INFO] + v, 3)
        block = jnp.where(table[1, INFO] == 0, u * SIDE + v, v * SIDE + u)
        return pl.ds(pl.multiple_of(block * TILE, TILE), TILE)

    @pl.when(step == 0)
    def _():
        for n in range(CBS):
            right[block_at(n % SIDE, n // SIDE), :] = high_ref[n]
            rest[block_at(n % SIDE, n // SIDE), :] = low_ref[n]
        out_ref[...] = jnp.zeros_like(out_ref)

    for n, part in enumerate(parts):
        @pl.when(step == n)
        def _(n=n, part=part):
            applied = jnp.dot(part[...].reshape(2 * TILE, WIDTH), right[...], preferred_element_type=jnp.float32)
            high = applied.astype(jnp.bfloat16)
            low = (applied - high.astype(jnp.float32)).astype(jnp.bfloat16)
            places = [block_at(code // SIDE, code % SIDE) for code in SEQUENCE[2 * n:2 * n + 2]]
            left_high = jnp.concatenate([right[place, :] for place in places], axis=0).T
            left_low = jnp.concatenate([rest[place, :] for place in places], axis=0).T
            terms = jnp.dot(left_high, jnp.concatenate([high, low], axis=1), preferred_element_type=jnp.float32)
            out_ref[...] += terms[:, :C2] + (
                terms[:, C2:] + jnp.dot(left_low, high, preferred_element_type=jnp.float32)
            )


def coarsest_term(table, parts, high, low):
    whole = pl.BlockSpec((CBS, TILE, C2), lambda j, *_: (0, 0, 0))
    return pl.pallas_call(
        coarsest_body,
        out_shape=jax.ShapeDtypeStruct((C2, C2), jnp.float32),
        grid_spec=pltpu.PrefetchScalarGridSpec(
            num_scalar_prefetch=1,
            grid=(PAIRS,),
            in_specs=[pl.BlockSpec((2, TILE, WIDTH), lambda j, *_: (0, 0, 0))] * PAIRS + [whole, whole],
            out_specs=pl.BlockSpec((C2, C2), lambda j, *_: (0, 0)),
            scratch_shapes=[pltpu.VMEM((WIDTH, C2), jnp.bfloat16)] * 2,
        ),
        compiler_params=pltpu.CompilerParams(vmem_limit_bytes=52 * 1024 * 1024),
        cost_estimate=cost(6),
    )(table, *parts, high, low)


def joined_body(up, from_far_a, down, from_far_b, _, up_out, down_out):
    up_out[...] = (up[...].astype(jnp.float32) + from_far_a[...].astype(jnp.float32)).astype(jnp.bfloat16)
    down_out[...] = (down[...].astype(jnp.float32) + from_far_b[...].astype(jnp.float32)).astype(jnp.bfloat16)


def joined(up, from_far_a, down, from_far_b, after_this):
    rows = 32
    part = pl.BlockSpec((2, rows, WIDTH), lambda j: (0, j, 0))
    return pl.pallas_call(
        joined_body,
        out_shape=[jax.ShapeDtypeStruct(up.shape, jnp.bfloat16)] * 2,
        grid=(TILE // rows,),
        in_specs=[part] * 4 + [pl.BlockSpec(memory_space=pl.ANY)],
        out_specs=[part] * 2,
        compiler_params=pltpu.CompilerParams(vmem_limit_bytes=32 * 1024 * 1024),
        cost_estimate=cost(2),
    )(up, from_far_a, down, from_far_b, after_this)


def torus_steps():
    def pairs(second, target):
        found = []
        for sect in range(8):
            for row in range(SIDE * SIDE):
                at = [row // SIDE, row % SIDE]
                axis = (sect % 2) ^ second
                at[axis] = target(at[axis])
                found.append((sect * 16 + row, sect * 16 + at[0] * SIDE + at[1]))
        return found

    return [{by: pairs(second, lambda at: (at + by) % SIDE) for by in (1, -1, 2)} for second in (0, 1)]


STEPS = torus_steps()


def send(value, second, by):
    return lax.ppermute(value, ("sect", "rows"), STEPS[second][by])


def wide(value):
    return value.astype(jnp.float32)


def share_out(term):
    pieces = term.reshape(32, 8, 2, 128).transpose(0, 2, 1, 3).reshape(128, 4, 128)
    return jnp.sum(lax.all_to_all(pieces, ("sect", "rows"), 0, 0), axis=0)


def bring_back(piece):
    back = lax.all_to_all(jnp.broadcast_to(piece[None], (128,) + piece.shape), ("sect", "rows"), 0, 0)
    return back.reshape(32, 2, 8, 128).transpose(0, 2, 1, 3).reshape(C2, C2)


def around(value, second):
    return jnp.stack([value, send(value, second, -1), send(value, second, 2), send(value, second, 1)])


def reduced_body(own_a, own_b, up_a, up_b, down_a, down_b, _, far, after, before, mine):
    def total(n, *refs):
        value = refs[0][n].astype(jnp.float32)
        for ref in refs[1:]:
            value = value + ref[n].astype(jnp.float32)
        return value

    far[...] = total(0, own_a, up_a, down_a).astype(jnp.bfloat16)
    after[...] = total(1, own_a, up_a, down_a).astype(jnp.bfloat16)
    before[...] = total(0, own_b, up_b, down_b).astype(jnp.bfloat16)
    mine[...] = total(1, own_b, up_b, down_b)


def reduced(own_a, own_b, up_a, up_b, down_a, down_b, after_this):
    rows = 64
    pair = pl.BlockSpec((2, rows, WIDTH), lambda j: (0, j, 0))
    one = pl.BlockSpec((rows, WIDTH), lambda j: (j, 0))
    shape = (TILE, WIDTH)
    return pl.pallas_call(
        reduced_body,
        out_shape=[jax.ShapeDtypeStruct(shape, jnp.bfloat16)] * 3 + [jax.ShapeDtypeStruct(shape, jnp.float32)],
        grid=(TILE // rows,),
        in_specs=[pair] * 6 + [pl.BlockSpec(memory_space=pl.ANY)],
        out_specs=[one] * 4,
        compiler_params=pltpu.CompilerParams(vmem_limit_bytes=32 * 1024 * 1024),
        cost_estimate=cost(3),
    )(own_a, own_b, up_a, up_b, down_a, down_b, after_this)


def per_device(a_tiles, a_cols, a_count, p_tiles, coarse_map, p_coarse):
    section = lax.axis_index("sect")
    position = lax.axis_index("rows")
    core = lax.rem(section, 2)
    x, y = lax.div(position, SIDE), lax.rem(position, SIDE)
    u, v = jnp.where(core == 0, x, y), jnp.where(core == 0, y, x)
    zero = jnp.zeros_like(core)
    first_row = (section * 16 + position - 1) * RB
    info = jnp.stack([section * CBS, core, u, v, first_row, zero, zero, zero]).astype(jnp.int32)
    up = [(i, i + 1) for i in range(15)]
    down = [(i + 1, i) for i in range(15)]
    local_map = coarse_map - section * CBS
    map_tile = jnp.pad(local_map.astype(jnp.bfloat16)[None, None], ((0, 0), (0, TILE - 1), (0, TILE - RB)))
    own = jnp.concatenate([p_tiles, map_tile], axis=0)
    left, right = lax.ppermute(own, "rows", up), lax.ppermute(own, "rows", down)
    maps = jnp.stack([left[RB, 0, :RB].astype(jnp.int32), local_map, right[RB, 0, :RB].astype(jnp.int32)])

    line = around((p_coarse * Q_SCALE).astype(jnp.float16), 0)
    square = around(line, 1)
    prolong = square.reshape(CBS, TILE, C2).astype(jnp.float32) * (1.0 / Q_SCALE)
    prolong_high = lax.reduce_precision(prolong, 8, 7)
    prolong_low = (prolong - prolong_high).astype(jnp.bfloat16)
    prolong_high = prolong_high.astype(jnp.bfloat16)

    table = row_plan(a_cols, a_count, coarse_map, info)
    all_held = jnp.sum(square[1:, 0, :8, :TILE].astype(jnp.float32), axis=0)
    parts = galerkin(table, maps, a_tiles, left, own, right, all_held)
    far_a, far_b, up_b, down_a, up_a, down_b, own_a, own_b = parts
    from_far_a, from_far_b = send(far_a, 0, 1), send(far_b, 0, -1)
    from_up_b, from_down_a = send(up_b, 0, 1), send(down_a, 0, -1)
    own_term = coarsest_term(table, parts, prolong_high, prolong_low)
    up_a, down_b = joined(up_a, from_far_a, down_b, from_far_b, own_term)
    from_up_a, from_down_b = send(up_a, 0, 1), send(down_b, 0, -1)

    own_piece = share_out(own_term)
    far, after, before, mine = reduced(own_a, own_b, from_up_a, from_up_b, from_down_a, from_down_b, own_piece)
    from_far, from_after, from_before = send(far, 1, 2), send(after, 1, 1), send(before, 1, -1)
    coarsest = bring_back(own_piece)
    owned_rows = mine + (wide(from_far) + (wide(from_after) + wide(from_before)))
    return (owned_rows, coarsest)


def solution(mesh):
    placed = (
        P(("sect", "rows"), None, None, None),
        P(("sect", "rows"), None),
        P(("sect", "rows")),
        P(("sect", "rows"), None, None),
        P(("sect", "rows")),
        P(("sect", "rows"), None),
    )
    return jax.shard_map(
        per_device,
        mesh=mesh,
        in_specs=placed,
        out_specs=(P(("sect", "rows"), None), P()),
        check_vma=False,
    )
```

time: 459 us -> 132 us (0.29)
  waiting for transfers between devices: 268 us -> 8.63 us
  local copies, waits for them, and re-layouts: 86.8 us -> 2.07 us
  matrix products: 74.3 us -> 0 us
  Pallas kernels: 0 us -> 40.6 us
  blocking collectives: 0 us -> 37.6 us
  starting transfers between devices: 10.8 us -> 34.1 us
  between operations: 13.9 us -> 0.9 us
    psum x1 -> x0, waiting for transfers between devices: 143 us -> none  [per_device(): coarsest = lax.psum(own_term, ('sect', 'rows'))]
    reduce_scatter x1 -> x0, waiting for transfers between devices: 119 us -> none  [per_device(): lax.psum_scatter(partial_sum, 'rows', scatter_dimension=0, tiled=True)]
    dot_general x6 -> x0, matrix products: 74.3 us -> none  [the longest x1 24.3 us: per_device(): jnp.einsum('lix,lbiy->lbxy', p_tiles.astype(jnp.float32), grouped, precis...]
    pallas_call x0 -> x5, Pallas kernels: none -> 40.6 us  [the longest x1 21.3 us: galerkin(): pl.pallas_call(galerkin_body, out_shape=[jax.ShapeDtypeStruct((2, TILE, W...]
    all_to_all x0 -> x2, blocking collectives: none -> 37.6 us  [the longest x1 20.7 us: share_out(): return jnp.sum(lax.all_to_all(pieces, ('sect', 'rows'), 0, 0), axis=0)]
    convert_element_type x1 -> x0, local copies, waits for them, and re-layouts: 24.5 us -> none  [per_device(): jnp.where(in_use[:, :, None, None], products, 0.0).astype(jnp.bfloat16)]
    ppermute x4 -> x17, starting transfers between devices: 10.6 us -> 34.1 us  [the longest x15 28.8 us: send(): return lax.ppermute(value, ('sect', 'rows'), STEPS[second][by])]
    dot_general x1 -> x0, local copies, waits for them, and re-layouts: 17.6 us -> none  [per_device(): jnp.einsum('lix,lbiy->lbxy', p_tiles.astype(jnp.float32), grouped, precis...]
  transfers between devices with their start and end apart: 7 -> 17, of which waited for: 4 -> 2; matrix products, arithmetic and copies ran while one was open for 35% -> 4% of each run, Pallas kernels for 0% -> 13%
where the time goes in v1:
time: 132 us; the launch traced here: 131 us
  Pallas kernels  40.6 us (31%)
  blocking collectives  37.6 us (28%)
  starting transfers between devices  34.1 us (26%)
  waiting for transfers between devices  8.63 us (7%)
  other arithmetic  7.26 us (6%)
  local copies, waits for them, and re-layouts  2.07 us (2%)
    ppermute x15, starting transfers between devices, send(): return lax.ppermute(value, ('sect', 'rows'), STEPS[second][by])  28.8 us
    pallas_call x1, Pallas kernels, galerkin(): pl.pallas_call(galerkin_body, out_shape=[jax.ShapeDtypeStruct((2, TILE, W...  21.3 us
    all_to_all x1, blocking collectives, share_out(): return jnp.sum(lax.all_to_all(pieces, ('sect', 'rows'), 0, 0), axis=0)  20.7 us
    all_to_all x1, blocking collectives, bring_back(): lax.all_to_all(jnp.broadcast_to(piece[None], (128,) + piece.shape), ('sec...  16.9 us
    pallas_call x1, Pallas kernels, coarsest_term(): pl.pallas_call(coarsest_body, out_shape=jax.ShapeDtypeStruct((C2, C2), jn...  11.8 us
    ppermute x15, waiting for transfers between devices, send(): return lax.ppermute(value, ('sect', 'rows'), STEPS[second][by])  8.62 us
    ppermute x1, starting transfers between devices, per_device(): lax.ppermute(own, 'rows', up)  4.02 us
    pallas_call x1, Pallas kernels, row_plan(): pl.pallas_call(plan_body, out_shape=jax.ShapeDtypeStruct((RB + 1, 32), jn...  2.91 us
  transfers between devices with their start and end apart: 17, of which 2 were waited for; matrix products, arithmetic and copies ran while one was open for 4% of the time, Pallas kernels for 13%

profile of v1, /device:TPU:1, one launch (start us, length us, event | category | flops | bytes accessed | tf_op | source)
XLA Modules:
  0.0 131.2 jit_solution(8101924247522784394)
XLA Ops:
  0.6 0.9 multiply_convert_fusion
  1.6 3.8 %collective-permute-start.3 = (f16[128,256]{1,0:T(8,128)(2,1)S(1)}, f16[128,256]{1,0:T(8,128)(2,1)S(1)}, u32[]{:S(2)}, u32[]{:S(2)}) collective-permute-start(f16[128,256]{1,0:T(8,128)(2,1)S(1)} %multiply_convert_fusion), channel_id=1, source_target_pairs={{0,8},{1,9},{2,10},{3,11},{4,12},{5,13},{6,14},{7,15},{8,0},{9,1},... | collective-permute-start | bytes 196616 | tf_op jit(solution)/shard_map/ppermute | solution.py:251
  5.4 0.8 collective-permute-start.2
  6.2 0.7 collective-permute-start.4
  6.8 0.7 subtract_bitcast_fusion
  7.5 1.1 fusion.2.own_ref
  8.6 1.3 collective-permute-start.1
  9.9 4.0 %collective-permute-start = (bf16[17,128,128]{2,1,0:T(8,128)(2,1)S(1)}, bf16[17,128,128]{2,1,0:T(8,128)(2,1)S(1)}, u32[]{:S(2)}, u32[]{:S(2)}) collective-permute-start(bf16[17,128,128]{2,1,0:T(8,128)(2,1)S(1)} %fusion.2.own_ref), channel_id=1, source_target_pairs={{0,1},{1,2},{2,3},{3,4},{4,5},{5,6},{6,7},{7,8},{8,9},{9,10},{10,1... | collective-permute-start | bytes 1671176 | tf_op jit(solution)/shard_map/ppermute | solution.py:315
  13.9 0.9 fusion.6
  14.8 0.0 collective-permute-done.3
  14.9 0.0 collective-permute-done.2
  14.9 0.0 collective-permute-done.4
  14.9 0.1 fusion.5
  15.0 1.8 %collective-permute-start.7 = (f16[4,128,256]{2,1,0:T(8,128)(2,1)S(1)}, f16[4,128,256]{2,1,0:T(8,128)(2,1)S(1)}, u32[]{:S(2)}, u32[]{:S(2)}) collective-permute-start(f16[4,128,256]{2,1,0:T(8,128)(2,1)S(1)} %get-tuple-element.33), channel_id=1, source_target_pairs={{0,1},{1,2},{2,3},{3,0},{4,5},{5,6},{6,7},{7,4},{8,9},{9,10},{10,1... | collective-permute-start | bytes 786440 | tf_op jit(solution)/shard_map/ppermute | solution.py:251
  16.7 2.7 %collective-permute-start.6 = (f16[4,128,256]{2,1,0:T(8,128)(2,1)S(1)}, f16[4,128,256]{2,1,0:T(8,128)(2,1)S(1)}, u32[]{:S(2)}, u32[]{:S(2)}) collective-permute-start(f16[4,128,256]{2,1,0:T(8,128)(2,1)S(1)} %get-tuple-element.33), channel_id=1, source_target_pairs={{0,2},{1,3},{2,0},{3,1},{4,6},{5,7},{6,4},{7,5},{8,10},{9,11},{10,... | collective-permute-start | bytes 786440 | tf_op jit(solution)/shard_map/ppermute | solution.py:251
  19.5 0.9 collective-permute-start.5
  20.3 0.6 stack.63.info
  20.9 2.9 %shard_map.77.table = s32[17,32]{1,0:T(8,128)} custom-call(s32[16,27]{1,0:T(8,128)} %cols.1, s32[16]{0:T(128)} %counts.1, s32[16]{0:T(128)} %own_map.1, s32[8]{0:T(128)} %stack.63.info), custom_call_target="tpu_custom_call" | custom-call | bytes 11100000 | tf_op jit(solution)/shard_map/pallas_call | solution.py:63
  23.9 0.0 collective-permute-done.7
  23.9 2.2 %collective-permute-done.6 = f16[4,128,256]{2,1,0:T(8,128)(2,1)S(1)} collective-permute-done((f16[4,128,256]{2,1,0:T(8,128)(2,1)S(1)}, f16[4,128,256]{2,1,0:T(8,128)(2,1)S(1)}, u32[]{:S(2)}, u32[]{:S(2)}) %collective-permute-start.6) | collective-permute-done | bytes 262176 | tf_op jit(solution)/shard_map/ppermute | solution.py:251
  26.0 6.4 %collective-permute-done.5 = f16[4,128,256]{2,1,0:T(8,128)(2,1)S(1)} collective-permute-done((f16[4,128,256]{2,1,0:T(8,128)(2,1)S(1)}, f16[4,128,256]{2,1,0:T(8,128)(2,1)S(1)}, u32[]{:S(2)}, u32[]{:S(2)}) %collective-permute-start.5) | collective-permute-done | bytes 262176 | tf_op jit(solution)/shard_map/ppermute | solution.py:251
  32.5 0.0 collective-permute-done.1.right_ref
  32.5 0.0 collective-permute-done.left_ref
  32.5 0.0 copy-start.5
  32.5 0.7 copy-done.5
  33.2 21.3 %shard_map.78 = (bf16[2,128,2048]{2,1,0:T(8,128)(2,1)}, bf16[2,128,2048]{2,1,0:T(8,128)(2,1)}, bf16[2,128,2048]{2,1,0:T(8,128)(2,1)}, bf16[2,128,2048]{2,1,0:T(8...) custom-call(s32[17,32]{1,0:T(8,128)S(1)} %copy-done.5, ...), custom_call_target="tpu_custom_call" | custom-call | bytes 74000000 | tf_op jit(solution)/shard_map/pallas_call | solution.py:142
  54.5 0.1 collective-permute-start.8
  54.6 8.2 %collective-permute-start.9 = (bf16[2,128,2048]{2,1,0:T(8,128)(2,1)}, bf16[2,128,2048]{2,1,0:T(8,128)(2,1)S(1)}, u32[]{:S(2)}, u32[]{:S(2)}) collective-permute-start(bf16[2,128,2048]{2,1,0:T(8,128)(2,1)} %get-tuple-element.21.refs_1_), channel_id=1, source_target_pairs={{0,12},{1,13},{2,14},{3,15},{4,0},{5,1},{6,2},{7,3},{8,4},{9,5},{1... | collective-permute-start | bytes 3145736 | tf_op jit(solution)/shard_map/ppermute | solution.py:251
  62.8 0.3 convert_multiply_fusion
  63.1 0.0 copy-start.4
  63.1 1.9 %fusion = (bf16[16,128,256]{2,1,0:T(8,128)(2,1)}, bf16[16,128,256]{2,1,0:T(8,128)(2,1)}) fusion(f32[4,4,128,256]{3,2,1,0:T(8,128)S(1)} %convert_multiply_fusion), kind=kLoop, calls=%fused_computation.2 | loop fusion | flops 2097152 | bytes 4194304 | tf_op jit(solution)/shard_map/convert_element_type | solution.py:322
  65.0 0.0 collective-permute-start.11
  65.0 2.7 %collective-permute-start.12 = (bf16[2,128,2048]{2,1,0:T(8,128)(2,1)}, bf16[2,128,2048]{2,1,0:T(8,128)(2,1)}, u32[]{:S(2)}, u32[]{:S(2)}) collective-permute-start(bf16[2,128,2048]{2,1,0:T(8,128)(2,1)} %get-tuple-element.23.refs_3_), channel_id=1, source_target_pairs={{0,12},{1,13},{2,14},{3,15},{4,0},{5,1},{6,2},{7,3},{8,4},{9,5},{1... | collective-permute-start | bytes 3145736 | tf_op jit(solution)/shard_map/ppermute | solution.py:251
  67.6 0.0 copy-done.4
  67.6 0.0 copy-start
  67.6 0.0 copy-start.1
  67.6 11.8 %shard_map.79._ = f32[256,256]{1,0:T(8,128)S(1)} custom-call(s32[17,32]{1,0:T(8,128)S(1)} %copy-done.5, bf16[2,128,2048]{2,1,0:T(8,128)(2,1)S(1)} %copy-done.4, bf16[2,128,2048]{2,1,0:T(8,128)(2,1)} %get-tuple-element.21.refs_1_, bf16[2,128,2048]{2,1,0:T(8,128)(2,1)} %get-tuple-element.22.refs_2_, bf16[2,128,2048]{2,1,0:T(8,128)(2,1)} %get-tuple-element.23.refs_3_, ...), custom_call_target="tpu_custom_call" | custom-call | bytes 22200000 | tf_op jit(solution)/shard_map/pallas_call | solution.py:199
  79.5 0.0 copy-start.2
  79.5 0.0 copy-start.3
  79.5 0.0 collective-permute-done.8.from_far_a
  79.5 0.0 collective-permute-done.9.from_far_b
  79.5 0.0 copy-done
  79.5 0.0 copy-done.1
  79.5 2.3 %shard_map.80 = (bf16[2,128,2048]{2,1,0:T(8,128)(2,1)}, bf16[2,128,2048]{2,1,0:T(8,128)(2,1)}) custom-call(bf16[2,128,2048]{2,1,0:T(8,128)(2,1)S(1)} %copy-done, bf16[2,128,2048]{2,1,0:T(8,128)(2,1)S(1)} %collective-permute-done.8.from_far_a, bf16[2,128,2048]{2,1,0:T(8,128)(2,1)S(1)} %copy-done.1, ...), custom_call_target="tpu_custom_call" | custom-call | bytes 7400000 | tf_op jit(solution)/shard_map/pallas_call | solution.py:222
  81.8 0.0 collective-permute-start.10
  81.8 2.7 %collective-permute-start.13 = (bf16[2,128,2048]{2,1,0:T(8,128)(2,1)}, bf16[2,128,2048]{2,1,0:T(8,128)(2,1)}, u32[]{:S(2)}, u32[]{:S(2)}) collective-permute-start(bf16[2,128,2048]{2,1,0:T(8,128)(2,1)} %get-tuple-element.25), channel_id=1, source_target_pairs={{0,12},{1,13},{2,14},{3,15},{4,0},{5,1},{6,2},{7,3},{8,4},{9,5},{1... | collective-permute-start | bytes 3145736 | tf_op jit(solution)/shard_map/ppermute | solution.py:251
  84.5 20.7 %all_to_all.10 = f32[128,4,128]{2,1,0:T(4,128)S(1)} all-to-all(f32[128,4,128]{2,1,0:T(4,128)S(1)} %bitcast.42), channel_id=1, replica_groups=mesh['sect'=8,'rows'=16] {'sect','rows'}, dimensions={0} | all-to-all | bytes 524288 | tf_op jit(solution)/shard_map/all_to_all | solution.py:260
  105.2 0.1 reduce_sum.19._
  105.3 0.0 collective-permute-done.11.up_b
  105.3 0.0 collective-permute-done.12.down_a
  105.4 0.0 collective-permute-done.10.up_a
  105.4 0.0 collective-permute-done.13.down_b
  105.4 0.0 copy-done.2
  105.4 0.0 copy-done.3
  105.4 2.4 %shard_map.81 = (bf16[128,2048]{1,0:T(8,128)(2,1)S(1)}, bf16[128,2048]{1,0:T(8,128)(2,1)S(1)}, bf16[128,2048]{1,0:T(8,128)(2,1)S(1)}, f32[128,2048]{1,0:T(8,128)S(1)}) custom-call(bf16[2,128,2048]{2,1,0:T(8,128)(2,1)S(1)} %copy-done.2, bf16[2,128,2048]{2,1,0:T(8,128)(2,1)S(1)} %copy-done.3, bf16[2,128,2048]{2,1,0:T(8,128)(2,1)} %collective-permute-done.10.up_a, ...), custom_call_target="tpu_custom_call" | custom-call | bytes 11100000 | tf_op jit(solution)/shard_map/pallas_call | solution.py:290
  107.8 1.9 %collective-permute-start.14 = (bf16[128,2048]{1,0:T(8,128)(2,1)S(1)}, bf16[128,2048]{1,0:T(8,128)(2,1)S(1)}, u32[]{:S(2)}, u32[]{:S(2)}) collective-permute-start(bf16[128,2048]{1,0:T(8,128)(2,1)S(1)} %get-tuple-element.27), channel_id=1, source_target_pairs={{0,2},{1,3},{2,0},{3,1},{4,6},{5,7},{6,4},{7,5},{8,10},{9,11},{10,... | collective-permute-start | bytes 1572872 | tf_op jit(solution)/shard_map/ppermute | solution.py:251
  109.6 1.3 %collective-permute-start.15 = (bf16[128,2048]{1,0:T(8,128)(2,1)S(1)}, bf16[128,2048]{1,0:T(8,128)(2,1)S(1)}, u32[]{:S(2)}, u32[]{:S(2)}) collective-permute-start(bf16[128,2048]{1,0:T(8,128)(2,1)S(1)} %get-tuple-element.28), channel_id=1, source_target_pairs={{0,1},{1,2},{2,3},{3,0},{4,5},{5,6},{6,7},{7,4},{8,9},{9,10},{10,1... | collective-permute-start | bytes 1572872 | tf_op jit(solution)/shard_map/ppermute | solution.py:251
  111.0 1.4 %collective-permute-start.16 = (bf16[128,2048]{1,0:T(8,128)(2,1)S(1)}, bf16[128,2048]{1,0:T(8,128)(2,1)S(1)}, u32[]{:S(2)}, u32[]{:S(2)}) collective-permute-start(bf16[128,2048]{1,0:T(8,128)(2,1)S(1)} %get-tuple-element.29), channel_id=1, source_target_pairs={{0,3},{1,0},{2,1},{3,2},{4,7},{5,4},{6,5},{7,6},{8,11},{9,8},{10,9... | collective-permute-start | bytes 1572872 | tf_op jit(solution)/shard_map/ppermute | solution.py:251
  112.4 16.9 %all_to_all.11 = f32[128,4,128]{2,1,0:T(4,128)S(1)} all-to-all(f32[128,4,128]{2,1,0:T(4,128)S(1)} %broadcast_in_dim.10), channel_id=1, replica_groups=mesh['sect'=8,'rows'=16] {'sect','rows'}, dimensions={0} | all-to-all | bytes 524288 | tf_op jit(solution)/shard_map/all_to_all | solution.py:264
  129.2 0.0 collective-permute-done.14
  129.2 0.0 collective-permute-done.15
  129.2 0.0 collective-permute-done.16
  129.2 1.2 add_add_fusion
  130.5 0.7 copy.9
  (6 shorter events, 0.1 us)
Async XLA Ops:
  1.6 13.3 %collective-permute-start.3 = (f16[128,256]{1,0:T(8,128)(2,1)S(1)}, f16[128,256]{1,0:T(8,128)(2,1)S(1)}, u32[]{:S(2)}, u32[]{:S(2)}) collective-permute-start(f16[128,256]{1,0:T(8,128)(2,1)S(1)} %multiply_convert_fusion), channel_id=1, source_target_pairs={{0,8},{1,9},{2,10},{3,11},{4,12},{5,13},{6,14},{7,15},{8,0},{9,1},... | collective-permute-start | bytes 196616 | tf_op jit(solution)/shard_map/ppermute | solution.py:251
  5.4 9.5 %collective-permute-start.2 = (f16[128,256]{1,0:T(8,128)(2,1)S(1)}, f16[128,256]{1,0:T(8,128)(2,1)S(1)}, u32[]{:S(2)}, u32[]{:S(2)}) collective-permute-start(f16[128,256]{1,0:T(8,128)(2,1)S(1)} %multiply_convert_fusion), channel_id=1, source_target_pairs={{0,12},{1,13},{2,14},{3,15},{4,0},{5,1},{6,2},{7,3},{8,4},{9,5},{1... | collective-permute-start | bytes 196616 | tf_op jit(solution)/shard_map/ppermute | solution.py:251
  6.2 8.7 %collective-permute-start.4 = (f16[128,256]{1,0:T(8,128)(2,1)S(1)}, f16[128,256]{1,0:T(8,128)(2,1)S(1)}, u32[]{:S(2)}, u32[]{:S(2)}) collective-permute-start(f16[128,256]{1,0:T(8,128)(2,1)S(1)} %multiply_convert_fusion), channel_id=1, source_target_pairs={{0,4},{1,5},{2,6},{3,7},{4,8},{5,9},{6,10},{7,11},{8,12},{9,13},{1... | collective-permute-start | bytes 196616 | tf_op jit(solution)/shard_map/ppermute | solution.py:251
  8.6 23.9 %collective-permute-start.1 = (bf16[17,128,128]{2,1,0:T(8,128)(2,1)S(1)}, bf16[17,128,128]{2,1,0:T(8,128)(2,1)S(1)}, u32[]{:S(2)}, u32[]{:S(2)}) collective-permute-start(bf16[17,128,128]{2,1,0:T(8,128)(2,1)S(1)} %fusion.2.own_ref), channel_id=1, source_target_pairs={{1,0},{2,1},{3,2},{4,3},{5,4},{6,5},{7,6},{8,7},{9,8},{10,9},{11,1... | collective-permute-start | bytes 1671176 | tf_op jit(solution)/shard_map/ppermute | solution.py:315
  9.9 22.6 %collective-permute-start = (bf16[17,128,128]{2,1,0:T(8,128)(2,1)S(1)}, bf16[17,128,128]{2,1,0:T(8,128)(2,1)S(1)}, u32[]{:S(2)}, u32[]{:S(2)}) collective-permute-start(bf16[17,128,128]{2,1,0:T(8,128)(2,1)S(1)} %fusion.2.own_ref), channel_id=1, source_target_pairs={{0,1},{1,2},{2,3},{3,4},{4,5},{5,6},{6,7},{7,8},{8,9},{9,10},{10,1... | collective-permute-start | bytes 1671176 | tf_op jit(solution)/shard_map/ppermute | solution.py:315
  15.0 8.9 %collective-permute-start.7 = (f16[4,128,256]{2,1,0:T(8,128)(2,1)S(1)}, f16[4,128,256]{2,1,0:T(8,128)(2,1)S(1)}, u32[]{:S(2)}, u32[]{:S(2)}) collective-permute-start(f16[4,128,256]{2,1,0:T(8,128)(2,1)S(1)} %get-tuple-element.33), channel_id=1, source_target_pairs={{0,1},{1,2},{2,3},{3,0},{4,5},{5,6},{6,7},{7,4},{8,9},{9,10},{10,1... | collective-permute-start | bytes 786440 | tf_op jit(solution)/shard_map/ppermute | solution.py:251
  16.7 9.3 %collective-permute-start.6 = (f16[4,128,256]{2,1,0:T(8,128)(2,1)S(1)}, f16[4,128,256]{2,1,0:T(8,128)(2,1)S(1)}, u32[]{:S(2)}, u32[]{:S(2)}) collective-permute-start(f16[4,128,256]{2,1,0:T(8,128)(2,1)S(1)} %get-tuple-element.33), channel_id=1, source_target_pairs={{0,2},{1,3},{2,0},{3,1},{4,6},{5,7},{6,4},{7,5},{8,10},{9,11},{10,... | collective-permute-start | bytes 786440 | tf_op jit(solution)/shard_map/ppermute | solution.py:251
  19.5 13.0 %collective-permute-start.5 = (f16[4,128,256]{2,1,0:T(8,128)(2,1)S(1)}, f16[4,128,256]{2,1,0:T(8,128)(2,1)S(1)}, u32[]{:S(2)}, u32[]{:S(2)}) collective-permute-start(f16[4,128,256]{2,1,0:T(8,128)(2,1)S(1)} %get-tuple-element.33), channel_id=1, source_target_pairs={{0,3},{1,0},{2,1},{3,2},{4,7},{5,4},{6,5},{7,6},{8,11},{9,8},{10,9... | collective-permute-start | bytes 786440 | tf_op jit(solution)/shard_map/ppermute | solution.py:251
  32.5 0.7 copy-start.5
  54.5 25.0 %collective-permute-start.8 = (bf16[2,128,2048]{2,1,0:T(8,128)(2,1)}, bf16[2,128,2048]{2,1,0:T(8,128)(2,1)S(1)}, u32[]{:S(2)}, u32[]{:S(2)}) collective-permute-start(bf16[2,128,2048]{2,1,0:T(8,128)(2,1)} %get-tuple-element.19.refs_0_), channel_id=1, source_target_pairs={{0,4},{1,5},{2,6},{3,7},{4,8},{5,9},{6,10},{7,11},{8,12},{9,13},{1... | collective-permute-start | bytes 3145736 | tf_op jit(solution)/shard_map/ppermute | solution.py:251
  54.6 24.9 %collective-permute-start.9 = (bf16[2,128,2048]{2,1,0:T(8,128)(2,1)}, bf16[2,128,2048]{2,1,0:T(8,128)(2,1)S(1)}, u32[]{:S(2)}, u32[]{:S(2)}) collective-permute-start(bf16[2,128,2048]{2,1,0:T(8,128)(2,1)} %get-tuple-element.21.refs_1_), channel_id=1, source_target_pairs={{0,12},{1,13},{2,14},{3,15},{4,0},{5,1},{6,2},{7,3},{8,4},{9,5},{1... | collective-permute-start | bytes 3145736 | tf_op jit(solution)/shard_map/ppermute | solution.py:251
  63.1 4.5 %copy-start.4 = (bf16[2,128,2048]{2,1,0:T(8,128)(2,1)S(1)}, bf16[2,128,2048]{2,1,0:T(8,128)(2,1)}, u32[]{:S(2)}) copy-start(bf16[2,128,2048]{2,1,0:T(8,128)(2,1)} %get-tuple-element.19.refs_0_) | copy-start | bytes 3145732
  65.0 40.4 %collective-permute-start.11 = (bf16[2,128,2048]{2,1,0:T(8,128)(2,1)}, bf16[2,128,2048]{2,1,0:T(8,128)(2,1)S(1)}, u32[]{:S(2)}, u32[]{:S(2)}) collective-permute-start(bf16[2,128,2048]{2,1,0:T(8,128)(2,1)} %get-tuple-element.22.refs_2_), channel_id=1, source_target_pairs={{0,4},{1,5},{2,6},{3,7},{4,8},{5,9},{6,10},{7,11},{8,12},{9,13},{1... | collective-permute-start | bytes 3145736 | tf_op jit(solution)/shard_map/ppermute | solution.py:251
  65.0 40.4 %collective-permute-start.12 = (bf16[2,128,2048]{2,1,0:T(8,128)(2,1)}, bf16[2,128,2048]{2,1,0:T(8,128)(2,1)}, u32[]{:S(2)}, u32[]{:S(2)}) collective-permute-start(bf16[2,128,2048]{2,1,0:T(8,128)(2,1)} %get-tuple-element.23.refs_3_), channel_id=1, source_target_pairs={{0,12},{1,13},{2,14},{3,15},{4,0},{5,1},{6,2},{7,3},{8,4},{9,5},{1... | collective-permute-start | bytes 3145736 | tf_op jit(solution)/shard_map/ppermute | solution.py:251
  67.6 11.9 %copy-start = (bf16[2,128,2048]{2,1,0:T(8,128)(2,1)S(1)}, bf16[2,128,2048]{2,1,0:T(8,128)(2,1)}, u32[]{:S(2)}) copy-start(bf16[2,128,2048]{2,1,0:T(8,128)(2,1)} %get-tuple-element.18.refs_4_.up) | copy-start | bytes 3145732
  67.6 11.9 %copy-start.1 = (bf16[2,128,2048]{2,1,0:T(8,128)(2,1)S(1)}, bf16[2,128,2048]{2,1,0:T(8,128)(2,1)}, u32[]{:S(2)}) copy-start(bf16[2,128,2048]{2,1,0:T(8,128)(2,1)} %get-tuple-element.20.refs_5_.down) | copy-start | bytes 3145732
  79.5 25.9 %copy-start.2 = (bf16[2,128,2048]{2,1,0:T(8,128)(2,1)S(1)}, bf16[2,128,2048]{2,1,0:T(8,128)(2,1)}, u32[]{:S(2)}) copy-start(bf16[2,128,2048]{2,1,0:T(8,128)(2,1)} %get-tuple-element.16.refs_6_.own_a) | copy-start | bytes 3145732
  79.5 25.9 %copy-start.3 = (bf16[2,128,2048]{2,1,0:T(8,128)(2,1)S(1)}, bf16[2,128,2048]{2,1,0:T(8,128)(2,1)}, u32[]{:S(2)}) copy-start(bf16[2,128,2048]{2,1,0:T(8,128)(2,1)} %get-tuple-element.17.refs_7_.own_b) | copy-start | bytes 3145732
  81.8 23.5 %collective-permute-start.10 = (bf16[2,128,2048]{2,1,0:T(8,128)(2,1)}, bf16[2,128,2048]{2,1,0:T(8,128)(2,1)}, u32[]{:S(2)}, u32[]{:S(2)}) collective-permute-start(bf16[2,128,2048]{2,1,0:T(8,128)(2,1)} %get-tuple-element.24), channel_id=1, source_target_pairs={{0,4},{1,5},{2,6},{3,7},{4,8},{5,9},{6,10},{7,11},{8,12},{9,13},{1... | collective-permute-start | bytes 3145736 | tf_op jit(solution)/shard_map/ppermute | solution.py:251
  81.8 23.5 %collective-permute-start.13 = (bf16[2,128,2048]{2,1,0:T(8,128)(2,1)}, bf16[2,128,2048]{2,1,0:T(8,128)(2,1)}, u32[]{:S(2)}, u32[]{:S(2)}) collective-permute-start(bf16[2,128,2048]{2,1,0:T(8,128)(2,1)} %get-tuple-element.25), channel_id=1, source_target_pairs={{0,12},{1,13},{2,14},{3,15},{4,0},{5,1},{6,2},{7,3},{8,4},{9,5},{1... | collective-permute-start | bytes 3145736 | tf_op jit(solution)/shard_map/ppermute | solution.py:251
  107.8 21.5 %collective-permute-start.14 = (bf16[128,2048]{1,0:T(8,128)(2,1)S(1)}, bf16[128,2048]{1,0:T(8,128)(2,1)S(1)}, u32[]{:S(2)}, u32[]{:S(2)}) collective-permute-start(bf16[128,2048]{1,0:T(8,128)(2,1)S(1)} %get-tuple-element.27), channel_id=1, source_target_pairs={{0,2},{1,3},{2,0},{3,1},{4,6},{5,7},{6,4},{7,5},{8,10},{9,11},{10,... | collective-permute-start | bytes 1572872 | tf_op jit(solution)/shard_map/ppermute | solution.py:251
  109.6 19.6 %collective-permute-start.15 = (bf16[128,2048]{1,0:T(8,128)(2,1)S(1)}, bf16[128,2048]{1,0:T(8,128)(2,1)S(1)}, u32[]{:S(2)}, u32[]{:S(2)}) collective-permute-start(bf16[128,2048]{1,0:T(8,128)(2,1)S(1)} %get-tuple-element.28), channel_id=1, source_target_pairs={{0,1},{1,2},{2,3},{3,0},{4,5},{5,6},{6,7},{7,4},{8,9},{9,10},{10,1... | collective-permute-start | bytes 1572872 | tf_op jit(solution)/shard_map/ppermute | solution.py:251
  111.0 18.3 %collective-permute-start.16 = (bf16[128,2048]{1,0:T(8,128)(2,1)S(1)}, bf16[128,2048]{1,0:T(8,128)(2,1)S(1)}, u32[]{:S(2)}, u32[]{:S(2)}) collective-permute-start(bf16[128,2048]{1,0:T(8,128)(2,1)S(1)} %get-tuple-element.29), channel_id=1, source_target_pairs={{0,3},{1,0},{2,1},{3,2},{4,7},{5,4},{6,5},{7,6},{8,11},{9,8},{10,9... | collective-permute-start | bytes 1572872 | tf_op jit(solution)/shard_map/ppermute | solution.py:251

commit v2 on v1

--- a/solution.py
+++ b/solution.py
@@ -69,8 +69,9 @@
     )(*operands)
 
 
-def galerkin_body(table, maps, a_ref, left_ref, own_ref, right_ref, _, *rest):
-    outs, (a_buf, tiles, acc, stage, a_sem, p_sem, out_sem) = rest[:PAIRS], rest[PAIRS:]
+def galerkin_body(table, maps, a_ref, left_ref, own_ref, right_ref, *rest):
+    outs, (scale_ref, a_buf, tiles, acc, stage, a_sem, p_sem, out_sem) = rest[:PAIRS], rest[PAIRS:]
+    scale_ref[...] = jnp.full(scale_ref.shape, 1.0 / Q_SCALE, jnp.float32)
 
     def fetch(r):
         slot = lax.rem(r, 2)
@@ -137,16 +138,17 @@
         leave(0, half).wait()
 
 
-def galerkin(table, maps, a_tiles, left, own, right, after_this):
+def galerkin(table, maps, a_tiles, left, own, right):
     anywhere = pl.BlockSpec(memory_space=pl.ANY)
     return pl.pallas_call(
         galerkin_body,
-        out_shape=[jax.ShapeDtypeStruct((2, TILE, WIDTH), jnp.bfloat16)] * PAIRS,
+        out_shape=[jax.ShapeDtypeStruct((2, TILE, WIDTH), jnp.bfloat16)] * PAIRS
+        + [jax.ShapeDtypeStruct((1, TILE), jnp.float32)],
         grid_spec=pltpu.PrefetchScalarGridSpec(
             num_scalar_prefetch=2,
             grid=(1,),
-            in_specs=[pl.BlockSpec(memory_space=pltpu.HBM)] + [anywhere] * 4,
-            out_specs=[anywhere] * PAIRS,
+            in_specs=[pl.BlockSpec(memory_space=pltpu.HBM)] + [anywhere] * 3,
+            out_specs=[anywhere] * PAIRS + [pl.BlockSpec((1, TILE), lambda j, *_: (0, 0))],
             scratch_shapes=[
                 pltpu.VMEM((2, KA, TILE, TILE), jnp.bfloat16),
                 pltpu.VMEM((3 * RB, TILE, TILE), jnp.bfloat16),
@@ -159,56 +161,81 @@
         ),
         compiler_params=pltpu.CompilerParams(vmem_limit_bytes=52 * 1024 * 1024),
         cost_estimate=cost(20),
-    )(table, maps, a_tiles, left, own, right, after_this)
+    )(table, maps, a_tiles, left, own, right)
 
 
 def coarsest_body(table, *refs):
     parts = refs[:PAIRS]
-    high_ref, low_ref, out_ref, right, rest = refs[PAIRS:]
-    step = pl.program_id(0)
+    high_ref, low_ref, out_ref, right, rest, held, q_sem, part_sem = refs[PAIRS:]
 
     def block_at(u, v):
         u, v = lax.bitwise_and(table[2, INFO] + u, 3), lax.bitwise_and(table[3, INFO] + v, 3)
         block = jnp.where(table[1, INFO] == 0, u * SIDE + v, v * SIDE + u)
         return pl.ds(pl.multiple_of(block * TILE, TILE), TILE)
 
-    @pl.when(step == 0)
-    def _():
-        for n in range(CBS):
-            right[block_at(n % SIDE, n // SIDE), :] = high_ref[n]
-            rest[block_at(n % SIDE, n // SIDE), :] = low_ref[n]
-        out_ref[...] = jnp.zeros_like(out_ref)
-
-    for n, part in enumerate(parts):
-        @pl.when(step == n)
-        def _(n=n, part=part):
-            applied = jnp.dot(part[...].reshape(2 * TILE, WIDTH), right[...], preferred_element_type=jnp.float32)
-            high = applied.astype(jnp.bfloat16)
-            low = (applied - high.astype(jnp.float32)).astype(jnp.bfloat16)
-            places = [block_at(code // SIDE, code % SIDE) for code in SEQUENCE[2 * n:2 * n + 2]]
-            left_high = jnp.concatenate([right[place, :] for place in places], axis=0).T
-            left_low = jnp.concatenate([rest[place, :] for place in places], axis=0).T
-            terms = jnp.dot(left_high, jnp.concatenate([high, low], axis=1), preferred_element_type=jnp.float32)
-            out_ref[...] += terms[:, :C2] + (
-                terms[:, C2:] + jnp.dot(left_low, high, preferred_element_type=jnp.float32)
-            )
+    factors = [
+        pltpu.make_async_copy(src.at[n], dst.at[block_at(n % SIDE, n // SIDE)], q_sem.at[m])
+        for m, (src, dst) in enumerate(((high_ref, right), (low_ref, rest)))
+        for n in range(CBS)
+    ]
+    loads = [
+        pltpu.make_async_copy(part, held.at[pl.ds(2 * n, 2)], part_sem.at[n]) for n, part in enumerate(parts)
+    ]
+    for copy in factors[:CBS] + loads[:2] + factors[CBS:] + loads[2:]:
+        copy.start()
+    for m, (src, dst) in enumerate(((high_ref, right), (low_ref, rest))):
+        pltpu.make_async_copy(src, dst.reshape(CBS, TILE, C2), q_sem.at[m]).wait()
+    total = None
+    for n in range(0, PAIRS, 2):
+        loads[n].wait()
+        loads[n + 1].wait()
+        rows = held[2 * n:2 * n + 4].reshape(4 * TILE, WIDTH)
+        applied = jnp.dot(rows, right[...], preferred_element_type=jnp.float32)
+        high = applied.astype(jnp.bfloat16)
+        low = (applied - high.astype(jnp.float32)).astype(jnp.bfloat16)
+        places = [block_at(code // SIDE, code % SIDE) for code in SEQUENCE[2 * n:2 * n + 4]]
+        left_high = jnp.concatenate([right[place, :] for place in places], axis=0).T
+        left_low = jnp.concatenate([rest[place, :] for place in places], axis=0).T
+        terms = jnp.dot(left_high, jnp.concatenate([high, low], axis=1), preferred_element_type=jnp.float32)
+        term = terms[:, :C2] + (terms[:, C2:] + jnp.dot(left_low, high, preferred_element_type=jnp.float32))
+        if n == 0:
+            out_ref[...] = term
+        else:
+            out_ref[...] += term
 
 
 def coarsest_term(table, parts, high, low):
-    whole = pl.BlockSpec((CBS, TILE, C2), lambda j, *_: (0, 0, 0))
     return pl.pallas_call(
         coarsest_body,
         out_shape=jax.ShapeDtypeStruct((C2, C2), jnp.float32),
         grid_spec=pltpu.PrefetchScalarGridSpec(
             num_scalar_prefetch=1,
-            grid=(PAIRS,),
-            in_specs=[pl.BlockSpec((2, TILE, WIDTH), lambda j, *_: (0, 0, 0))] * PAIRS + [whole, whole],
+            grid=(1,),
+            in_specs=[pl.BlockSpec(memory_space=pl.ANY)] * (PAIRS + 2),
             out_specs=pl.BlockSpec((C2, C2), lambda j, *_: (0, 0)),
-            scratch_shapes=[pltpu.VMEM((WIDTH, C2), jnp.bfloat16)] * 2,
+            scratch_shapes=[
+                pltpu.VMEM((WIDTH, C2), jnp.bfloat16),
+                pltpu.VMEM((WIDTH, C2), jnp.bfloat16),
+                pltpu.VMEM((2 * PAIRS, TILE, WIDTH), jnp.bfloat16),
+                pltpu.SemaphoreType.DMA((2,)),
+                pltpu.SemaphoreType.DMA((PAIRS,)),
+            ],
         ),
         compiler_params=pltpu.CompilerParams(vmem_limit_bytes=52 * 1024 * 1024),
         cost_estimate=cost(6),
     )(table, *parts, high, low)
+
+
+def held_back(first, second, after_this):
+    anywhere = pl.BlockSpec(memory_space=pl.ANY)
+    return pl.pallas_call(
+        lambda *refs: None,
+        out_shape=[jax.ShapeDtypeStruct(value.shape, value.dtype) for value in (first, second)],
+        in_specs=[anywhere] * 3,
+        out_specs=[anywhere] * 2,
+        input_output_aliases={0: 0, 1: 1},
+        cost_estimate=cost(1),
+    )(first, second, after_this)
 
 
 def joined_body(up, from_far_a, down, from_far_b, _, up_out, down_out):
@@ -317,15 +344,15 @@
 
     line = around((p_coarse * Q_SCALE).astype(jnp.float16), 0)
     square = around(line, 1)
-    prolong = square.reshape(CBS, TILE, C2).astype(jnp.float32) * (1.0 / Q_SCALE)
+    table = row_plan(a_cols, a_count, coarse_map, info)
+    *parts, scale = galerkin(table, maps, a_tiles, left, own, right)
+    far_a, far_b, up_b, down_a, up_a, down_b, own_a, own_b = parts
+    prolong = square.reshape(CBS, TILE, C2).astype(jnp.float32) * scale[0, 0]
     prolong_high = lax.reduce_precision(prolong, 8, 7)
     prolong_low = (prolong - prolong_high).astype(jnp.bfloat16)
     prolong_high = prolong_high.astype(jnp.bfloat16)
-
-    table = row_plan(a_cols, a_count, coarse_map, info)
-    all_held = jnp.sum(square[1:, 0, :8, :TILE].astype(jnp.float32), axis=0)
-    parts = galerkin(table, maps, a_tiles, left, own, right, all_held)
-    far_a, far_b, up_b, down_a, up_a, down_b, own_a, own_b = parts
+    far_a, far_b = held_back(far_a, far_b, prolong_high)
+    parts = (far_a, far_b, up_b, down_a, up_a, down_b, own_a, own_b)
     from_far_a, from_far_b = send(far_a, 0, 1), send(far_b, 0, -1)
     from_up_b, from_down_a = send(up_b, 0, 1), send(down_a, 0, -1)
     own_term = coarsest_term(table, parts, prolong_high, prolong_low)

time: 132 us -> 130 us (0.985)
  blocking collectives: 37.6 us -> 45.4 us
  starting transfers between devices: 34.1 us -> 27.9 us
  waiting for transfers between devices: 8.63 us -> 4.75 us
  Pallas kernels: 40.6 us -> 39.2 us
    all_to_all x1, blocking collectives: 20.7 us -> 28.4 us  [share_out(): return jnp.sum(lax.all_to_all(pieces, ('sect', 'rows'), 0, 0), axis=0)]
    ppermute x15, starting transfers between devices: 28.8 us -> 24 us  [send(): return lax.ppermute(value, ('sect', 'rows'), STEPS[second][by])]
    ppermute x15, waiting for transfers between devices: 8.62 us -> 4.75 us  [send(): return lax.ppermute(value, ('sect', 'rows'), STEPS[second][by])]
    pallas_call x1, Pallas kernels: 11.8 us -> 10.4 us  [coarsest_term(): pl.pallas_call(coarsest_body, out_shape=jax.ShapeDtypeStruct((C2, C2), jn...]
    ppermute x1, starting transfers between devices: 4.02 us -> 2.62 us  [per_device(): lax.ppermute(own, 'rows', up)]
    unnamed x13 -> x15, local copies, waits for them, and re-layouts: 1.43 us -> 2.65 us
  transfers between devices with their start and end apart: 17 -> 17, of which waited for: 2 -> 1; matrix products, arithmetic and copies ran while one was open for 4% -> 2% of each run, Pallas kernels for 13% -> 29%
where the time goes in v2:
time: 130 us; the launch traced here: 129 us
  blocking collectives  45.4 us (35%)
  Pallas kernels  39.2 us (30%)
  starting transfers between devices  27.9 us (21%)
  other arithmetic  7.27 us (6%)
  waiting for transfers between devices  4.75 us (4%)
  local copies, waits for them, and re-layouts  3.37 us (3%)
    all_to_all x1, blocking collectives, share_out(): return jnp.sum(lax.all_to_all(pieces, ('sect', 'rows'), 0, 0), axis=0)  28.4 us
    ppermute x15, starting transfers between devices, send(): return lax.ppermute(value, ('sect', 'rows'), STEPS[second][by])  24 us
    pallas_call x1, Pallas kernels, galerkin(): pl.pallas_call(galerkin_body, out_shape=[jax.ShapeDtypeStruct((2, TILE, W...  21.2 us
    all_to_all x1, blocking collectives, bring_back(): lax.all_to_all(jnp.broadcast_to(piece[None], (128,) + piece.shape), ('sec...  16.9 us
    pallas_call x1, Pallas kernels, coarsest_term(): pl.pallas_call(coarsest_body, out_shape=jax.ShapeDtypeStruct((C2, C2), jn...  10.4 us
    ppermute x15, waiting for transfers between devices, send(): return lax.ppermute(value, ('sect', 'rows'), STEPS[second][by])  4.75 us
    pallas_call x1, Pallas kernels, row_plan(): pl.pallas_call(plan_body, out_shape=jax.ShapeDtypeStruct((RB + 1, 32), jn...  2.91 us
    unnamed x15, local copies, waits for them, and re-layouts  2.65 us
  transfers between devices with their start and end apart: 17, of which 1 were waited for; matrix products, arithmetic and copies ran while one was open for 2% of the time, Pallas kernels for 29%

profile of v2, /device:TPU:1, one launch (start us, length us, event | category | flops | bytes accessed | tf_op | source)
XLA Modules:
  0.0 128.7 jit_solution(4186756089024060490)
XLA Ops:
  0.6 0.7 subtract_bitcast_fusion
  1.3 1.1 fusion.2.own_ref
  2.4 1.3 %collective-permute-start.1 = (bf16[17,128,128]{2,1,0:T(8,128)(2,1)S(1)}, bf16[17,128,128]{2,1,0:T(8,128)(2,1)S(1)}, u32[]{:S(2)}, u32[]{:S(2)}) collective-permute-start(bf16[17,128,128]{2,1,0:T(8,128)(2,1)S(1)} %fusion.2.own_ref), channel_id=1, source_target_pairs={{1,0},{2,1},{3,2},{4,3},{5,4},{6,5},{7,6},{8,7},{9,8},{10,9},{11,1... | collective-permute-start | bytes 1671176 | tf_op jit(solution)/shard_map/ppermute | solution.py:342
  3.7 0.9 multiply_convert_fusion
  4.6 4.6 %collective-permute-start.3 = (f16[128,256]{1,0:T(8,128)(2,1)S(1)}, f16[128,256]{1,0:T(8,128)(2,1)S(1)}, u32[]{:S(2)}, u32[]{:S(2)}) collective-permute-start(f16[128,256]{1,0:T(8,128)(2,1)S(1)} %multiply_convert_fusion), channel_id=1, source_target_pairs={{0,8},{1,9},{2,10},{3,11},{4,12},{5,13},{6,14},{7,15},{8,0},{9,1},... | collective-permute-start | bytes 196616 | tf_op jit(solution)/shard_map/ppermute | solution.py:278
  9.2 0.6 collective-permute-start.2
  9.8 0.8 collective-permute-start.4
  10.7 2.6 %collective-permute-start = (bf16[17,128,128]{2,1,0:T(8,128)(2,1)S(1)}, bf16[17,128,128]{2,1,0:T(8,128)(2,1)S(1)}, u32[]{:S(2)}, u32[]{:S(2)}) collective-permute-start(bf16[17,128,128]{2,1,0:T(8,128)(2,1)S(1)} %fusion.2.own_ref), channel_id=1, source_target_pairs={{0,1},{1,2},{2,3},{3,4},{4,5},{5,6},{6,7},{7,8},{8,9},{9,10},{10,1... | collective-permute-start | bytes 1671176 | tf_op jit(solution)/shard_map/ppermute | solution.py:342
  13.3 0.9 fusion.6
  14.3 0.7 stack.61.info
  15.0 2.9 %shard_map.77.table = s32[17,32]{1,0:T(8,128)} custom-call(s32[16,27]{1,0:T(8,128)} %cols.1, s32[16]{0:T(128)} %counts.1, s32[16]{0:T(128)} %own_map.1, s32[8]{0:T(128)} %stack.61.info), custom_call_target="tpu_custom_call" | custom-call | bytes 11100000 | tf_op jit(solution)/shard_map/pallas_call | solution.py:63
  17.9 0.0 collective-permute-done.3
  17.9 4.7 %collective-permute-done.2 = f16[128,256]{1,0:T(8,128)(2,1)S(1)} collective-permute-done((f16[128,256]{1,0:T(8,128)(2,1)S(1)}, f16[128,256]{1,0:T(8,128)(2,1)S(1)}, u32[]{:S(2)}, u32[]{:S(2)}) %collective-permute-start.2) | collective-permute-done | bytes 65568 | tf_op jit(solution)/shard_map/ppermute | solution.py:278
  22.6 0.0 collective-permute-done.4
  22.6 0.1 fusion.5
  22.7 2.8 %collective-permute-start.6 = (f16[4,128,256]{2,1,0:T(8,128)(2,1)S(1)}, f16[4,128,256]{2,1,0:T(8,128)(2,1)S(1)}, u32[]{:S(2)}, u32[]{:S(2)}) collective-permute-start(f16[4,128,256]{2,1,0:T(8,128)(2,1)S(1)} %get-tuple-element.39), channel_id=1, source_target_pairs={{0,2},{1,3},{2,0},{3,1},{4,6},{5,7},{6,4},{7,5},{8,10},{9,11},{10,... | collective-permute-start | bytes 786440 | tf_op jit(solution)/shard_map/ppermute | solution.py:278
  25.5 0.9 collective-permute-start.5
  26.4 0.6 collective-permute-start.7
  27.0 0.0 collective-permute-done.1.right_ref
  27.0 0.0 collective-permute-done.left_ref
  27.0 0.0 copy-start.5
  27.0 0.7 copy-done.5
  27.7 21.2 %shard_map.78 = (bf16[2,128,2048]{2,1,0:T(8,128)(2,1)}, bf16[2,128,2048]{2,1,0:T(8,128)(2,1)}, bf16[2,128,2048]{2,1,0:T(8,128)(2,1)}, bf16[2,128,2048]{2,1,0:T(8...) custom-call(s32[17,32]{1,0:T(8,128)S(1)} %copy-done.5, ...), custom_call_target="tpu_custom_call" | custom-call | bytes 74000000 | tf_op jit(solution)/shard_map/pallas_call | solution.py:143
  49.0 0.0 collective-permute-done.6
  49.0 0.0 collective-permute-done.5
  49.0 0.0 collective-permute-done.7
  49.0 0.3 convert_multiply_fusion
  49.4 1.8 %fusion = (bf16[16,128,256]{2,1,0:T(8,128)(2,1)}, bf16[16,128,256]{2,1,0:T(8,128)(2,1)}) fusion(f32[4,4,128,256]{3,2,1,0:T(8,128)S(1)} %convert_multiply_fusion), kind=kLoop, calls=%fused_computation.2 | loop fusion | flops 2097152 | bytes 4194304 | tf_op jit(solution)/shard_map/convert_element_type | solution.py:352
  51.2 0.0 copy-start.6
  51.2 0.9 collective-permute-start.8
  52.1 3.0 %collective-permute-start.9 = (bf16[2,128,2048]{2,1,0:T(8,128)(2,1)}, bf16[2,128,2048]{2,1,0:T(8,128)(2,1)S(1)}, u32[]{:S(2)}, u32[]{:S(2)}) collective-permute-start(bf16[2,128,2048]{2,1,0:T(8,128)(2,1)} %get-tuple-element.27.refs_1_), channel_id=1, source_target_pairs={{0,12},{1,13},{2,14},{3,15},{4,0},{5,1},{6,2},{7,3},{8,4},{9,5},{1... | collective-permute-start | bytes 3145736 | tf_op jit(solution)/shard_map/ppermute | solution.py:278
  55.1 0.0 collective-permute-start.11
  55.1 2.7 %collective-permute-start.12 = (bf16[2,128,2048]{2,1,0:T(8,128)(2,1)}, bf16[2,128,2048]{2,1,0:T(8,128)(2,1)}, u32[]{:S(2)}, u32[]{:S(2)}) collective-permute-start(bf16[2,128,2048]{2,1,0:T(8,128)(2,1)} %get-tuple-element.29.refs_3_), channel_id=1, source_target_pairs={{0,12},{1,13},{2,14},{3,15},{4,0},{5,1},{6,2},{7,3},{8,4},{9,5},{1... | collective-permute-start | bytes 3145736 | tf_op jit(solution)/shard_map/ppermute | solution.py:278
  57.8 0.0 copy-done.6
  57.8 0.0 copy-start.2
  57.8 1.2 copy-done.2
  59.0 10.4 %shard_map.80._ = f32[256,256]{1,0:T(8,128)S(1)} custom-call(s32[17,32]{1,0:T(8,128)S(1)} %copy-done.6, bf16[2,128,2048]{2,1,0:T(8,128)(2,1)S(1)} %copy-done.2, bf16[2,128,2048]{2,1,0:T(8,128)(2,1)} %get-tuple-element.27.refs_1_, bf16[2,128,2048]{2,1,0:T(8,128)(2,1)} %get-tuple-element.28.refs_2_, bf16[2,128,2048]{2,1,0:T(8,128)(2,1)} %get-tuple-element.29.refs_3_, ...), custom_call_target="tpu_custom_call" | custom-call | bytes 22200000 | tf_op jit(solution)/shard_map/pallas_call | solution.py:208
  69.4 0.0 copy-start.3
  69.4 0.0 copy-start.4
  69.4 0.0 collective-permute-done.8.from_far_a
  69.4 0.0 collective-permute-done.9.from_far_b
  69.4 0.0 copy-done
  69.5 0.0 copy-done.1
  69.5 2.3 %shard_map.81 = (bf16[2,128,2048]{2,1,0:T(8,128)(2,1)}, bf16[2,128,2048]{2,1,0:T(8,128)(2,1)}) custom-call(bf16[2,128,2048]{2,1,0:T(8,128)(2,1)S(1)} %copy-done, bf16[2,128,2048]{2,1,0:T(8,128)(2,1)S(1)} %collective-permute-done.8.from_far_a, bf16[2,128,2048]{2,1,0:T(8,128)(2,1)S(1)} %copy-done.1, ...), custom_call_target="tpu_custom_call" | custom-call | bytes 7400000 | tf_op jit(solution)/shard_map/pallas_call | solution.py:249
  71.7 0.0 collective-permute-start.10
  71.7 2.7 %collective-permute-start.13 = (bf16[2,128,2048]{2,1,0:T(8,128)(2,1)}, bf16[2,128,2048]{2,1,0:T(8,128)(2,1)}, u32[]{:S(2)}, u32[]{:S(2)}) collective-permute-start(bf16[2,128,2048]{2,1,0:T(8,128)(2,1)} %get-tuple-element.31), channel_id=1, source_target_pairs={{0,12},{1,13},{2,14},{3,15},{4,0},{5,1},{6,2},{7,3},{8,4},{9,5},{1... | collective-permute-start | bytes 3145736 | tf_op jit(solution)/shard_map/ppermute | solution.py:278
  74.4 28.4 %all_to_all.10 = f32[128,4,128]{2,1,0:T(4,128)S(1)} all-to-all(f32[128,4,128]{2,1,0:T(4,128)S(1)} %bitcast.44), channel_id=1, replica_groups=mesh['sect'=8,'rows'=16] {'sect','rows'}, dimensions={0} | all-to-all | bytes 524288 | tf_op jit(solution)/shard_map/all_to_all | solution.py:287
  102.8 0.1 reduce_sum.9._
  103.0 0.0 collective-permute-done.11.up_b
  103.0 0.0 collective-permute-done.12.down_a
  103.0 0.0 collective-permute-done.10.up_a
  103.0 0.0 collective-permute-done.13.down_b
  103.0 0.0 copy-done.3
  103.0 0.0 copy-done.4
  103.0 2.4 %shard_map.82 = (bf16[128,2048]{1,0:T(8,128)(2,1)S(1)}, bf16[128,2048]{1,0:T(8,128)(2,1)S(1)}, bf16[128,2048]{1,0:T(8,128)(2,1)S(1)}, f32[128,2048]{1,0:T(8,128)S(1)}) custom-call(bf16[2,128,2048]{2,1,0:T(8,128)(2,1)S(1)} %copy-done.3, bf16[2,128,2048]{2,1,0:T(8,128)(2,1)S(1)} %copy-done.4, bf16[2,128,2048]{2,1,0:T(8,128)(2,1)} %collective-permute-done.10.up_a, ...), custom_call_target="tpu_custom_call" | custom-call | bytes 11100000 | tf_op jit(solution)/shard_map/pallas_call | solution.py:317
  105.4 1.7 %collective-permute-start.14 = (bf16[128,2048]{1,0:T(8,128)(2,1)S(1)}, bf16[128,2048]{1,0:T(8,128)(2,1)S(1)}, u32[]{:S(2)}, u32[]{:S(2)}) collective-permute-start(bf16[128,2048]{1,0:T(8,128)(2,1)S(1)} %get-tuple-element.33), channel_id=1, source_target_pairs={{0,2},{1,3},{2,0},{3,1},{4,6},{5,7},{6,4},{7,5},{8,10},{9,11},{10,... | collective-permute-start | bytes 1572872 | tf_op jit(solution)/shard_map/ppermute | solution.py:278
  107.1 1.0 collective-permute-start.15
  108.1 1.7 %collective-permute-start.16 = (bf16[128,2048]{1,0:T(8,128)(2,1)S(1)}, bf16[128,2048]{1,0:T(8,128)(2,1)S(1)}, u32[]{:S(2)}, u32[]{:S(2)}) collective-permute-start(bf16[128,2048]{1,0:T(8,128)(2,1)S(1)} %get-tuple-element.35), channel_id=1, source_target_pairs={{0,3},{1,0},{2,1},{3,2},{4,7},{5,4},{6,5},{7,6},{8,11},{9,8},{10,9... | collective-permute-start | bytes 1572872 | tf_op jit(solution)/shard_map/ppermute | solution.py:278
  109.8 16.9 %all_to_all.11 = f32[128,4,128]{2,1,0:T(4,128)S(1)} all-to-all(f32[128,4,128]{2,1,0:T(4,128)S(1)} %broadcast_in_dim.10), channel_id=1, replica_groups=mesh['sect'=8,'rows'=16] {'sect','rows'}, dimensions={0} | all-to-all | bytes 524288 | tf_op jit(solution)/shard_map/all_to_all | solution.py:291
  126.8 0.0 collective-permute-done.14
  126.8 0.0 collective-permute-done.15
  126.8 0.0 collective-permute-done.16
  126.8 1.2 add_add_fusion
  128.0 0.7 copy.13
  (8 shorter events, 0.1 us)
Async XLA Ops:
  2.4 24.6 %collective-permute-start.1 = (bf16[17,128,128]{2,1,0:T(8,128)(2,1)S(1)}, bf16[17,128,128]{2,1,0:T(8,128)(2,1)S(1)}, u32[]{:S(2)}, u32[]{:S(2)}) collective-permute-start(bf16[17,128,128]{2,1,0:T(8,128)(2,1)S(1)} %fusion.2.own_ref), channel_id=1, source_target_pairs={{1,0},{2,1},{3,2},{4,3},{5,4},{6,5},{7,6},{8,7},{9,8},{10,9},{11,1... | collective-permute-start | bytes 1671176 | tf_op jit(solution)/shard_map/ppermute | solution.py:342
  4.6 13.3 %collective-permute-start.3 = (f16[128,256]{1,0:T(8,128)(2,1)S(1)}, f16[128,256]{1,0:T(8,128)(2,1)S(1)}, u32[]{:S(2)}, u32[]{:S(2)}) collective-permute-start(f16[128,256]{1,0:T(8,128)(2,1)S(1)} %multiply_convert_fusion), channel_id=1, source_target_pairs={{0,8},{1,9},{2,10},{3,11},{4,12},{5,13},{6,14},{7,15},{8,0},{9,1},... | collective-permute-start | bytes 196616 | tf_op jit(solution)/shard_map/ppermute | solution.py:278
  9.2 13.4 %collective-permute-start.2 = (f16[128,256]{1,0:T(8,128)(2,1)S(1)}, f16[128,256]{1,0:T(8,128)(2,1)S(1)}, u32[]{:S(2)}, u32[]{:S(2)}) collective-permute-start(f16[128,256]{1,0:T(8,128)(2,1)S(1)} %multiply_convert_fusion), channel_id=1, source_target_pairs={{0,12},{1,13},{2,14},{3,15},{4,0},{5,1},{6,2},{7,3},{8,4},{9,5},{1... | collective-permute-start | bytes 196616 | tf_op jit(solution)/shard_map/ppermute | solution.py:278
  9.8 12.8 %collective-permute-start.4 = (f16[128,256]{1,0:T(8,128)(2,1)S(1)}, f16[128,256]{1,0:T(8,128)(2,1)S(1)}, u32[]{:S(2)}, u32[]{:S(2)}) collective-permute-start(f16[128,256]{1,0:T(8,128)(2,1)S(1)} %multiply_convert_fusion), channel_id=1, source_target_pairs={{0,4},{1,5},{2,6},{3,7},{4,8},{5,9},{6,10},{7,11},{8,12},{9,13},{1... | collective-permute-start | bytes 196616 | tf_op jit(solution)/shard_map/ppermute | solution.py:278
  10.7 16.3 %collective-permute-start = (bf16[17,128,128]{2,1,0:T(8,128)(2,1)S(1)}, bf16[17,128,128]{2,1,0:T(8,128)(2,1)S(1)}, u32[]{:S(2)}, u32[]{:S(2)}) collective-permute-start(bf16[17,128,128]{2,1,0:T(8,128)(2,1)S(1)} %fusion.2.own_ref), channel_id=1, source_target_pairs={{0,1},{1,2},{2,3},{3,4},{4,5},{5,6},{6,7},{7,8},{8,9},{9,10},{10,1... | collective-permute-start | bytes 1671176 | tf_op jit(solution)/shard_map/ppermute | solution.py:342
  22.7 26.3 %collective-permute-start.6 = (f16[4,128,256]{2,1,0:T(8,128)(2,1)S(1)}, f16[4,128,256]{2,1,0:T(8,128)(2,1)S(1)}, u32[]{:S(2)}, u32[]{:S(2)}) collective-permute-start(f16[4,128,256]{2,1,0:T(8,128)(2,1)S(1)} %get-tuple-element.39), channel_id=1, source_target_pairs={{0,2},{1,3},{2,0},{3,1},{4,6},{5,7},{6,4},{7,5},{8,10},{9,11},{10,... | collective-permute-start | bytes 786440 | tf_op jit(solution)/shard_map/ppermute | solution.py:278
  25.5 23.5 %collective-permute-start.5 = (f16[4,128,256]{2,1,0:T(8,128)(2,1)S(1)}, f16[4,128,256]{2,1,0:T(8,128)(2,1)S(1)}, u32[]{:S(2)}, u32[]{:S(2)}) collective-permute-start(f16[4,128,256]{2,1,0:T(8,128)(2,1)S(1)} %get-tuple-element.39), channel_id=1, source_target_pairs={{0,3},{1,0},{2,1},{3,2},{4,7},{5,4},{6,5},{7,6},{8,11},{9,8},{10,9... | collective-permute-start | bytes 786440 | tf_op jit(solution)/shard_map/ppermute | solution.py:278
  26.4 22.6 %collective-permute-start.7 = (f16[4,128,256]{2,1,0:T(8,128)(2,1)S(1)}, f16[4,128,256]{2,1,0:T(8,128)(2,1)S(1)}, u32[]{:S(2)}, u32[]{:S(2)}) collective-permute-start(f16[4,128,256]{2,1,0:T(8,128)(2,1)S(1)} %get-tuple-element.39), channel_id=1, source_target_pairs={{0,1},{1,2},{2,3},{3,0},{4,5},{5,6},{6,7},{7,4},{8,9},{9,10},{10,1... | collective-permute-start | bytes 786440 | tf_op jit(solution)/shard_map/ppermute | solution.py:278
  27.0 0.7 copy-start.5
  51.2 6.6 %copy-start.6 = (s32[17,32]{1,0:T(8,128)S(1)}, s32[17,32]{1,0:T(8,128)}, u32[]{:S(2)}) copy-start(s32[17,32]{1,0:T(8,128)} %shard_map.77.table) | copy-start | bytes 6532
  51.2 18.2 %collective-permute-start.8 = (bf16[2,128,2048]{2,1,0:T(8,128)(2,1)}, bf16[2,128,2048]{2,1,0:T(8,128)(2,1)S(1)}, u32[]{:S(2)}, u32[]{:S(2)}) collective-permute-start(bf16[2,128,2048]{2,1,0:T(8,128)(2,1)} %get-tuple-element.25.refs_0_), channel_id=1, source_target_pairs={{0,4},{1,5},{2,6},{3,7},{4,8},{5,9},{6,10},{7,11},{8,12},{9,13},{1... | collective-permute-start | bytes 3145736 | tf_op jit(solution)/shard_map/ppermute | solution.py:278
  52.1 17.3 %collective-permute-start.9 = (bf16[2,128,2048]{2,1,0:T(8,128)(2,1)}, bf16[2,128,2048]{2,1,0:T(8,128)(2,1)S(1)}, u32[]{:S(2)}, u32[]{:S(2)}) collective-permute-start(bf16[2,128,2048]{2,1,0:T(8,128)(2,1)} %get-tuple-element.27.refs_1_), channel_id=1, source_target_pairs={{0,12},{1,13},{2,14},{3,15},{4,0},{5,1},{6,2},{7,3},{8,4},{9,5},{1... | collective-permute-start | bytes 3145736 | tf_op jit(solution)/shard_map/ppermute | solution.py:278
  55.1 47.9 %collective-permute-start.11 = (bf16[2,128,2048]{2,1,0:T(8,128)(2,1)}, bf16[2,128,2048]{2,1,0:T(8,128)(2,1)S(1)}, u32[]{:S(2)}, u32[]{:S(2)}) collective-permute-start(bf16[2,128,2048]{2,1,0:T(8,128)(2,1)} %get-tuple-element.28.refs_2_), channel_id=1, source_target_pairs={{0,4},{1,5},{2,6},{3,7},{4,8},{5,9},{6,10},{7,11},{8,12},{9,13},{1... | collective-permute-start | bytes 3145736 | tf_op jit(solution)/shard_map/ppermute | solution.py:278
  55.1 47.9 %collective-permute-start.12 = (bf16[2,128,2048]{2,1,0:T(8,128)(2,1)}, bf16[2,128,2048]{2,1,0:T(8,128)(2,1)}, u32[]{:S(2)}, u32[]{:S(2)}) collective-permute-start(bf16[2,128,2048]{2,1,0:T(8,128)(2,1)} %get-tuple-element.29.refs_3_), channel_id=1, source_target_pairs={{0,12},{1,13},{2,14},{3,15},{4,0},{5,1},{6,2},{7,3},{8,4},{9,5},{1... | collective-permute-start | bytes 3145736 | tf_op jit(solution)/shard_map/ppermute | solution.py:278
  57.8 1.2 copy-start.2
  59.0 10.4 %copy-start = (bf16[2,128,2048]{2,1,0:T(8,128)(2,1)S(1)}, bf16[2,128,2048]{2,1,0:T(8,128)(2,1)}, u32[]{:S(2)}) copy-start(bf16[2,128,2048]{2,1,0:T(8,128)(2,1)} %get-tuple-element.21.refs_4_.up) | copy-start | bytes 3145732
  59.0 10.4 %copy-start.1 = (bf16[2,128,2048]{2,1,0:T(8,128)(2,1)S(1)}, bf16[2,128,2048]{2,1,0:T(8,128)(2,1)}, u32[]{:S(2)}) copy-start(bf16[2,128,2048]{2,1,0:T(8,128)(2,1)} %get-tuple-element.26.refs_5_.down) | copy-start | bytes 3145732
  69.4 33.6 %copy-start.3 = (bf16[2,128,2048]{2,1,0:T(8,128)(2,1)S(1)}, bf16[2,128,2048]{2,1,0:T(8,128)(2,1)}, u32[]{:S(2)}) copy-start(bf16[2,128,2048]{2,1,0:T(8,128)(2,1)} %get-tuple-element.19.refs_6_.own_a) | copy-start | bytes 3145732
  69.4 33.6 %copy-start.4 = (bf16[2,128,2048]{2,1,0:T(8,128)(2,1)S(1)}, bf16[2,128,2048]{2,1,0:T(8,128)(2,1)}, u32[]{:S(2)}) copy-start(bf16[2,128,2048]{2,1,0:T(8,128)(2,1)} %get-tuple-element.20.refs_7_.own_b) | copy-start | bytes 3145732
  71.7 31.3 %collective-permute-start.10 = (bf16[2,128,2048]{2,1,0:T(8,128)(2,1)}, bf16[2,128,2048]{2,1,0:T(8,128)(2,1)}, u32[]{:S(2)}, u32[]{:S(2)}) collective-permute-start(bf16[2,128,2048]{2,1,0:T(8,128)(2,1)} %get-tuple-element.30), channel_id=1, source_target_pairs={{0,4},{1,5},{2,6},{3,7},{4,8},{5,9},{6,10},{7,11},{8,12},{9,13},{1... | collective-permute-start | bytes 3145736 | tf_op jit(solution)/shard_map/ppermute | solution.py:278
  71.7 31.3 %collective-permute-start.13 = (bf16[2,128,2048]{2,1,0:T(8,128)(2,1)}, bf16[2,128,2048]{2,1,0:T(8,128)(2,1)}, u32[]{:S(2)}, u32[]{:S(2)}) collective-permute-start(bf16[2,128,2048]{2,1,0:T(8,128)(2,1)} %get-tuple-element.31), channel_id=1, source_target_pairs={{0,12},{1,13},{2,14},{3,15},{4,0},{5,1},{6,2},{7,3},{8,4},{9,5},{1... | collective-permute-start | bytes 3145736 | tf_op jit(solution)/shard_map/ppermute | solution.py:278
  105.4 21.3 %collective-permute-start.14 = (bf16[128,2048]{1,0:T(8,128)(2,1)S(1)}, bf16[128,2048]{1,0:T(8,128)(2,1)S(1)}, u32[]{:S(2)}, u32[]{:S(2)}) collective-permute-start(bf16[128,2048]{1,0:T(8,128)(2,1)S(1)} %get-tuple-element.33), channel_id=1, source_target_pairs={{0,2},{1,3},{2,0},{3,1},{4,6},{5,7},{6,4},{7,5},{8,10},{9,11},{10,... | collective-permute-start | bytes 1572872 | tf_op jit(solution)/shard_map/ppermute | solution.py:278
  107.1 19.7 %collective-permute-start.15 = (bf16[128,2048]{1,0:T(8,128)(2,1)S(1)}, bf16[128,2048]{1,0:T(8,128)(2,1)S(1)}, u32[]{:S(2)}, u32[]{:S(2)}) collective-permute-start(bf16[128,2048]{1,0:T(8,128)(2,1)S(1)} %get-tuple-element.34), channel_id=1, source_target_pairs={{0,1},{1,2},{2,3},{3,0},{4,5},{5,6},{6,7},{7,4},{8,9},{9,10},{10,1... | collective-permute-start | bytes 1572872 | tf_op jit(solution)/shard_map/ppermute | solution.py:278
  108.1 18.7 %collective-permute-start.16 = (bf16[128,2048]{1,0:T(8,128)(2,1)S(1)}, bf16[128,2048]{1,0:T(8,128)(2,1)S(1)}, u32[]{:S(2)}, u32[]{:S(2)}) collective-permute-start(bf16[128,2048]{1,0:T(8,128)(2,1)S(1)} %get-tuple-element.35), channel_id=1, source_target_pairs={{0,3},{1,0},{2,1},{3,2},{4,7},{5,4},{6,5},{7,6},{8,11},{9,8},{10,9... | collective-permute-start | bytes 1572872 | tf_op jit(solution)/shard_map/ppermute | solution.py:278

commit v3 on v2

--- a/solution.py
+++ b/solution.py
@@ -11,7 +11,7 @@
 TILE = 128
 RB = 16
 KA = 27
-GROUP = 9
+GROUP = 1
 SIDE = 4
 WIDTH = CBS * TILE
 C2 = 256
@@ -98,16 +98,16 @@
         slot = lax.rem(r, 2)
         count = table[i, COUNT]
         left = tiles[RB + i].T
-        for k in range(0, KA, 2):
+        for k in range(0, KA, GROUP):
             products, places = [], []
-            for s in range(k, min(k + 2, KA)):
+            for s in range(k, min(k + GROUP, KA)):
                 col = jnp.clip(table[i, s], 0, 3 * RB - 1)
                 block = jnp.clip(maps[lax.shift_right_logical(col, 4), lax.bitwise_and(col, RB - 1)], 0, CBS - 1)
                 places.append(pl.multiple_of(jnp.where(s < count, block, CBS) * TILE, TILE))
                 products.append(
                     jnp.dot(a_buf[slot, s], tiles[col], preferred_element_type=jnp.float32).astype(jnp.bfloat16)
                 )
-            terms = jnp.dot(left, jnp.concatenate(products, axis=1), preferred_element_type=jnp.float32)
+            terms = jnp.dot(left, jnp.concatenate(products, axis=1) if len(products) > 1 else products[0], preferred_element_type=jnp.float32)
             for n, place in enumerate(places):
                 acc[:, pl.ds(place, TILE)] += terms[:, n * TILE:(n + 1) * TILE]
         return 0
@@ -166,7 +166,7 @@
 
 def coarsest_body(table, *refs):
     parts = refs[:PAIRS]
-    high_ref, low_ref, out_ref, right, rest, held, q_sem, part_sem = refs[PAIRS:]
+    high_ref, low_ref, out_ref, right, rest, left, left_rest, applied, applied_rest, held, q_sem, part_sem = refs[PAIRS:]
 
     def block_at(u, v):
         u, v = lax.bitwise_and(table[2, INFO] + u, 3), lax.bitwise_and(table[3, INFO] + v, 3)
@@ -181,27 +181,30 @@
     loads = [
         pltpu.make_async_copy(part, held.at[pl.ds(2 * n, 2)], part_sem.at[n]) for n, part in enumerate(parts)
     ]
-    for copy in factors[:CBS] + loads[:2] + factors[CBS:] + loads[2:]:
+    for copy in factors[:CBS] + loads[:2] + factors[CBS:]:
         copy.start()
     for m, (src, dst) in enumerate(((high_ref, right), (low_ref, rest))):
         pltpu.make_async_copy(src, dst.reshape(CBS, TILE, C2), q_sem.at[m]).wait()
-    total = None
-    for n in range(0, PAIRS, 2):
+    for n, code in enumerate(SEQUENCE):
+        place, columns = block_at(code // SIDE, code % SIDE), pl.ds(n * TILE, TILE)
+        left[:, columns] = right[place, :].T
+        left_rest[:, columns] = rest[place, :].T
+    for n in range(PAIRS):
         loads[n].wait()
-        loads[n + 1].wait()
-        rows = held[2 * n:2 * n + 4].reshape(4 * TILE, WIDTH)
-        applied = jnp.dot(rows, right[...], preferred_element_type=jnp.float32)
-        high = applied.astype(jnp.bfloat16)
-        low = (applied - high.astype(jnp.float32)).astype(jnp.bfloat16)
-        places = [block_at(code // SIDE, code % SIDE) for code in SEQUENCE[2 * n:2 * n + 4]]
-        left_high = jnp.concatenate([right[place, :] for place in places], axis=0).T
-        left_low = jnp.concatenate([rest[place, :] for place in places], axis=0).T
-        terms = jnp.dot(left_high, jnp.concatenate([high, low], axis=1), preferred_element_type=jnp.float32)
-        term = terms[:, :C2] + (terms[:, C2:] + jnp.dot(left_low, high, preferred_element_type=jnp.float32))
-        if n == 0:
-            out_ref[...] = term
-        else:
-            out_ref[...] += term
+        if n + 2 < PAIRS:
+            loads[n + 2].start()
+        for m in (2 * n, 2 * n + 1):
+            value = jnp.dot(held[m], right[...], preferred_element_type=jnp.float32)
+            high = value.astype(jnp.bfloat16)
+            rows = pl.ds(m * TILE, TILE)
+            applied[rows, :] = high
+            applied_rest[rows, :] = (value - high.astype(jnp.float32)).astype(jnp.bfloat16)
+    for first in range(0, C2, TILE):
+        rows = pl.ds(first, TILE)
+        term = jnp.dot(left[rows, :], applied[...], preferred_element_type=jnp.float32)
+        term += jnp.dot(left[rows, :], applied_rest[...], preferred_element_type=jnp.float32)
+        term += jnp.dot(left_rest[rows, :], applied[...], preferred_element_type=jnp.float32)
+        out_ref[rows, :] = term
 
 
 def coarsest_term(table, parts, high, low):
@@ -214,6 +217,10 @@
             in_specs=[pl.BlockSpec(memory_space=pl.ANY)] * (PAIRS + 2),
             out_specs=pl.BlockSpec((C2, C2), lambda j, *_: (0, 0)),
             scratch_shapes=[
+                pltpu.VMEM((WIDTH, C2), jnp.bfloat16),
+                pltpu.VMEM((WIDTH, C2), jnp.bfloat16),
+                pltpu.VMEM((C2, WIDTH), jnp.bfloat16),
+                pltpu.VMEM((C2, WIDTH), jnp.bfloat16),
                 pltpu.VMEM((WIDTH, C2), jnp.bfloat16),
                 pltpu.VMEM((WIDTH, C2), jnp.bfloat16),
                 pltpu.VMEM((2 * PAIRS, TILE, WIDTH), jnp.bfloat16),

time: 130 us -> 129 us (level)
  Pallas kernels: 39.2 us -> 37.4 us
    pallas_call x1, Pallas kernels: 10.4 us -> 8.73 us  [coarsest_term(): pl.pallas_call(coarsest_body, out_shape=jax.ShapeDtypeStruct((C2, C2), jn...]
    all_to_all x1, blocking collectives: 28.4 us -> 29.9 us  [share_out(): return jnp.sum(lax.all_to_all(pieces, ('sect', 'rows'), 0, 0), axis=0)]
  transfers between devices with their start and end apart: 17 -> 17, of which waited for: 1 -> 1; matrix products, arithmetic and copies ran while one was open for 2% -> 2% of each run, Pallas kernels for 29% -> 28%
where the time goes in v3:
time: 129 us; the launch traced here: 128 us
  blocking collectives  45.7 us (35%)
  Pallas kernels  37.4 us (29%)
  starting transfers between devices  28.1 us (22%)
  other arithmetic  7.27 us (6%)
  waiting for transfers between devices  4.75 us (4%)
  local copies, waits for them, and re-layouts  3.37 us (3%)
    all_to_all x1, blocking collectives, share_out(): return jnp.sum(lax.all_to_all(pieces, ('sect', 'rows'), 0, 0), axis=0)  29.9 us
    ppermute x15, starting transfers between devices, send(): return lax.ppermute(value, ('sect', 'rows'), STEPS[second][by])  24.2 us
    pallas_call x1, Pallas kernels, galerkin(): pl.pallas_call(galerkin_body, out_shape=[jax.ShapeDtypeStruct((2, TILE, W...  21.1 us
    all_to_all x1, blocking collectives, bring_back(): lax.all_to_all(jnp.broadcast_to(piece[None], (128,) + piece.shape), ('sec...  15.8 us
    pallas_call x1, Pallas kernels, coarsest_term(): pl.pallas_call(coarsest_body, out_shape=jax.ShapeDtypeStruct((C2, C2), jn...  8.73 us
    ppermute x15, waiting for transfers between devices, send(): return lax.ppermute(value, ('sect', 'rows'), STEPS[second][by])  4.75 us
    pallas_call x1, Pallas kernels, row_plan(): pl.pallas_call(plan_body, out_shape=jax.ShapeDtypeStruct((RB + 1, 32), jn...  2.91 us
    unnamed x15, local copies, waits for them, and re-layouts  2.65 us
  transfers between devices with their start and end apart: 17, of which 1 were waited for; matrix products, arithmetic and copies ran while one was open for 2% of the time, Pallas kernels for 28%

profile of v3, /device:TPU:1, one launch (start us, length us, event | category | flops | bytes accessed | tf_op | source)
XLA Modules:
  0.0 127.5 jit_solution(7356021006901879994)
XLA Ops:
  0.6 0.7 subtract_bitcast_fusion
  1.3 1.1 fusion.2.own_ref
  2.4 1.3 %collective-permute-start.1 = (bf16[17,128,128]{2,1,0:T(8,128)(2,1)S(1)}, bf16[17,128,128]{2,1,0:T(8,128)(2,1)S(1)}, u32[]{:S(2)}, u32[]{:S(2)}) collective-permute-start(bf16[17,128,128]{2,1,0:T(8,128)(2,1)S(1)} %fusion.2.own_ref), channel_id=1, source_target_pairs={{1,0},{2,1},{3,2},{4,3},{5,4},{6,5},{7,6},{8,7},{9,8},{10,9},{11,1... | collective-permute-start | bytes 1671176 | tf_op jit(solution)/shard_map/ppermute | solution.py:349
  3.7 0.9 multiply_convert_fusion
  4.6 4.6 %collective-permute-start.3 = (f16[128,256]{1,0:T(8,128)(2,1)S(1)}, f16[128,256]{1,0:T(8,128)(2,1)S(1)}, u32[]{:S(2)}, u32[]{:S(2)}) collective-permute-start(f16[128,256]{1,0:T(8,128)(2,1)S(1)} %multiply_convert_fusion), channel_id=1, source_target_pairs={{0,8},{1,9},{2,10},{3,11},{4,12},{5,13},{6,14},{7,15},{8,0},{9,1},... | collective-permute-start | bytes 196616 | tf_op jit(solution)/shard_map/ppermute | solution.py:285
  9.2 0.6 collective-permute-start.2
  9.8 0.8 collective-permute-start.4
  10.7 2.6 %collective-permute-start = (bf16[17,128,128]{2,1,0:T(8,128)(2,1)S(1)}, bf16[17,128,128]{2,1,0:T(8,128)(2,1)S(1)}, u32[]{:S(2)}, u32[]{:S(2)}) collective-permute-start(bf16[17,128,128]{2,1,0:T(8,128)(2,1)S(1)} %fusion.2.own_ref), channel_id=1, source_target_pairs={{0,1},{1,2},{2,3},{3,4},{4,5},{5,6},{6,7},{7,8},{8,9},{9,10},{10,1... | collective-permute-start | bytes 1671176 | tf_op jit(solution)/shard_map/ppermute | solution.py:349
  13.3 0.9 fusion.6
  14.3 0.7 stack.61.info
  15.0 2.9 %shard_map.77.table = s32[17,32]{1,0:T(8,128)} custom-call(s32[16,27]{1,0:T(8,128)} %cols.1, s32[16]{0:T(128)} %counts.1, s32[16]{0:T(128)} %own_map.1, s32[8]{0:T(128)} %stack.61.info), custom_call_target="tpu_custom_call" | custom-call | bytes 11100000 | tf_op jit(solution)/shard_map/pallas_call | solution.py:63
  17.9 0.0 collective-permute-done.3
  17.9 4.7 %collective-permute-done.2 = f16[128,256]{1,0:T(8,128)(2,1)S(1)} collective-permute-done((f16[128,256]{1,0:T(8,128)(2,1)S(1)}, f16[128,256]{1,0:T(8,128)(2,1)S(1)}, u32[]{:S(2)}, u32[]{:S(2)}) %collective-permute-start.2) | collective-permute-done | bytes 65568 | tf_op jit(solution)/shard_map/ppermute | solution.py:285
  22.6 0.0 collective-permute-done.4
  22.6 0.1 fusion.5
  22.7 2.8 %collective-permute-start.6 = (f16[4,128,256]{2,1,0:T(8,128)(2,1)S(1)}, f16[4,128,256]{2,1,0:T(8,128)(2,1)S(1)}, u32[]{:S(2)}, u32[]{:S(2)}) collective-permute-start(f16[4,128,256]{2,1,0:T(8,128)(2,1)S(1)} %get-tuple-element.39), channel_id=1, source_target_pairs={{0,2},{1,3},{2,0},{3,1},{4,6},{5,7},{6,4},{7,5},{8,10},{9,11},{10,... | collective-permute-start | bytes 786440 | tf_op jit(solution)/shard_map/ppermute | solution.py:285
  25.5 0.9 collective-permute-start.5
  26.4 0.6 collective-permute-start.7
  27.0 0.0 collective-permute-done.1.right_ref
  27.0 0.0 collective-permute-done.left_ref
  27.0 0.0 copy-start.5
  27.0 0.7 copy-done.5
  27.7 21.1 %shard_map.78 = (bf16[2,128,2048]{2,1,0:T(8,128)(2,1)}, bf16[2,128,2048]{2,1,0:T(8,128)(2,1)}, bf16[2,128,2048]{2,1,0:T(8,128)(2,1)}, bf16[2,128,2048]{2,1,0:T(8...) custom-call(s32[17,32]{1,0:T(8,128)S(1)} %copy-done.5, ...), custom_call_target="tpu_custom_call" | custom-call | bytes 74000000 | tf_op jit(solution)/shard_map/pallas_call | solution.py:143
  48.9 0.0 collective-permute-done.6
  48.9 0.0 collective-permute-done.5
  48.9 0.0 collective-permute-done.7
  48.9 0.3 convert_multiply_fusion
  49.3 1.8 %fusion = (bf16[16,128,256]{2,1,0:T(8,128)(2,1)}, bf16[16,128,256]{2,1,0:T(8,128)(2,1)}) fusion(f32[4,4,128,256]{3,2,1,0:T(8,128)S(1)} %convert_multiply_fusion), kind=kLoop, calls=%fused_computation.2 | loop fusion | flops 2097152 | bytes 4194304 | tf_op jit(solution)/shard_map/convert_element_type | solution.py:359
  51.1 0.0 copy-start.6
  51.1 0.0 collective-permute-start.8
  51.1 3.8 %collective-permute-start.9 = (bf16[2,128,2048]{2,1,0:T(8,128)(2,1)}, bf16[2,128,2048]{2,1,0:T(8,128)(2,1)S(1)}, u32[]{:S(2)}, u32[]{:S(2)}) collective-permute-start(bf16[2,128,2048]{2,1,0:T(8,128)(2,1)} %get-tuple-element.27.refs_1_), channel_id=1, source_target_pairs={{0,12},{1,13},{2,14},{3,15},{4,0},{5,1},{6,2},{7,3},{8,4},{9,5},{1... | collective-permute-start | bytes 3145736 | tf_op jit(solution)/shard_map/ppermute | solution.py:285
  55.0 0.0 collective-permute-start.11
  55.0 2.7 %collective-permute-start.12 = (bf16[2,128,2048]{2,1,0:T(8,128)(2,1)}, bf16[2,128,2048]{2,1,0:T(8,128)(2,1)}, u32[]{:S(2)}, u32[]{:S(2)}) collective-permute-start(bf16[2,128,2048]{2,1,0:T(8,128)(2,1)} %get-tuple-element.29.refs_3_), channel_id=1, source_target_pairs={{0,12},{1,13},{2,14},{3,15},{4,0},{5,1},{6,2},{7,3},{8,4},{9,5},{1... | collective-permute-start | bytes 3145736 | tf_op jit(solution)/shard_map/ppermute | solution.py:285
  57.6 0.0 copy-done.6
  57.6 0.0 copy-start.2
  57.6 1.2 copy-done.2
  58.9 8.7 %shard_map.80._ = f32[256,256]{1,0:T(8,128)S(1)} custom-call(s32[17,32]{1,0:T(8,128)S(1)} %copy-done.6, bf16[2,128,2048]{2,1,0:T(8,128)(2,1)S(1)} %copy-done.2, bf16[2,128,2048]{2,1,0:T(8,128)(2,1)} %get-tuple-element.27.refs_1_, bf16[2,128,2048]{2,1,0:T(8,128)(2,1)} %get-tuple-element.28.refs_2_, bf16[2,128,2048]{2,1,0:T(8,128)(2,1)} %get-tuple-element.29.refs_3_, ...), custom_call_target="tpu_custom_call" | custom-call | bytes 22200000 | tf_op jit(solution)/shard_map/pallas_call | solution.py:211
  67.6 0.0 copy-start.3
  67.6 0.0 copy-start.4
  67.6 0.0 collective-permute-done.8.from_far_a
  67.6 0.0 collective-permute-done.9.from_far_b
  67.7 0.0 copy-done
  67.7 0.0 copy-done.1
  67.7 2.3 %shard_map.81 = (bf16[2,128,2048]{2,1,0:T(8,128)(2,1)}, bf16[2,128,2048]{2,1,0:T(8,128)(2,1)}) custom-call(bf16[2,128,2048]{2,1,0:T(8,128)(2,1)S(1)} %copy-done, bf16[2,128,2048]{2,1,0:T(8,128)(2,1)S(1)} %collective-permute-done.8.from_far_a, bf16[2,128,2048]{2,1,0:T(8,128)(2,1)S(1)} %copy-done.1, ...), custom_call_target="tpu_custom_call" | custom-call | bytes 7400000 | tf_op jit(solution)/shard_map/pallas_call | solution.py:256
  70.0 0.8 collective-permute-start.10
  70.7 1.9 %collective-permute-start.13 = (bf16[2,128,2048]{2,1,0:T(8,128)(2,1)}, bf16[2,128,2048]{2,1,0:T(8,128)(2,1)}, u32[]{:S(2)}, u32[]{:S(2)}) collective-permute-start(bf16[2,128,2048]{2,1,0:T(8,128)(2,1)} %get-tuple-element.31), channel_id=1, source_target_pairs={{0,12},{1,13},{2,14},{3,15},{4,0},{5,1},{6,2},{7,3},{8,4},{9,5},{1... | collective-permute-start | bytes 3145736 | tf_op jit(solution)/shard_map/ppermute | solution.py:285
  72.6 29.9 %all_to_all.10 = f32[128,4,128]{2,1,0:T(4,128)S(1)} all-to-all(f32[128,4,128]{2,1,0:T(4,128)S(1)} %bitcast.44), channel_id=1, replica_groups=mesh['sect'=8,'rows'=16] {'sect','rows'}, dimensions={0} | all-to-all | bytes 524288 | tf_op jit(solution)/shard_map/all_to_all | solution.py:294
  102.5 0.1 reduce_sum.9._
  102.7 0.0 collective-permute-done.11.up_b
  102.7 0.0 collective-permute-done.12.down_a
  102.7 0.0 collective-permute-done.10.up_a
  102.7 0.0 collective-permute-done.13.down_b
  102.7 0.0 copy-done.3
  102.7 0.0 copy-done.4
  102.7 2.4 %shard_map.82 = (bf16[128,2048]{1,0:T(8,128)(2,1)S(1)}, bf16[128,2048]{1,0:T(8,128)(2,1)S(1)}, bf16[128,2048]{1,0:T(8,128)(2,1)S(1)}, f32[128,2048]{1,0:T(8,128)S(1)}) custom-call(bf16[2,128,2048]{2,1,0:T(8,128)(2,1)S(1)} %copy-done.3, bf16[2,128,2048]{2,1,0:T(8,128)(2,1)S(1)} %copy-done.4, bf16[2,128,2048]{2,1,0:T(8,128)(2,1)} %collective-permute-done.10.up_a, ...), custom_call_target="tpu_custom_call" | custom-call | bytes 11100000 | tf_op jit(solution)/shard_map/pallas_call | solution.py:324
  105.1 2.0 %collective-permute-start.14 = (bf16[128,2048]{1,0:T(8,128)(2,1)S(1)}, bf16[128,2048]{1,0:T(8,128)(2,1)S(1)}, u32[]{:S(2)}, u32[]{:S(2)}) collective-permute-start(bf16[128,2048]{1,0:T(8,128)(2,1)S(1)} %get-tuple-element.33), channel_id=1, source_target_pairs={{0,2},{1,3},{2,0},{3,1},{4,6},{5,7},{6,4},{7,5},{8,10},{9,11},{10,... | collective-permute-start | bytes 1572872 | tf_op jit(solution)/shard_map/ppermute | solution.py:285
  107.1 0.6 collective-permute-start.15
  107.7 2.1 %collective-permute-start.16 = (bf16[128,2048]{1,0:T(8,128)(2,1)S(1)}, bf16[128,2048]{1,0:T(8,128)(2,1)S(1)}, u32[]{:S(2)}, u32[]{:S(2)}) collective-permute-start(bf16[128,2048]{1,0:T(8,128)(2,1)S(1)} %get-tuple-element.35), channel_id=1, source_target_pairs={{0,3},{1,0},{2,1},{3,2},{4,7},{5,4},{6,5},{7,6},{8,11},{9,8},{10,9... | collective-permute-start | bytes 1572872 | tf_op jit(solution)/shard_map/ppermute | solution.py:285
  109.8 15.8 %all_to_all.11 = f32[128,4,128]{2,1,0:T(4,128)S(1)} all-to-all(f32[128,4,128]{2,1,0:T(4,128)S(1)} %broadcast_in_dim.10), channel_id=1, replica_groups=mesh['sect'=8,'rows'=16] {'sect','rows'}, dimensions={0} | all-to-all | bytes 524288 | tf_op jit(solution)/shard_map/all_to_all | solution.py:298
  125.6 0.0 collective-permute-done.14
  125.6 0.0 collective-permute-done.15
  125.6 0.0 collective-permute-done.16
  125.6 1.2 add_add_fusion
  126.8 0.7 copy.13
  (8 shorter events, 0.1 us)
Async XLA Ops:
  2.4 24.6 %collective-permute-start.1 = (bf16[17,128,128]{2,1,0:T(8,128)(2,1)S(1)}, bf16[17,128,128]{2,1,0:T(8,128)(2,1)S(1)}, u32[]{:S(2)}, u32[]{:S(2)}) collective-permute-start(bf16[17,128,128]{2,1,0:T(8,128)(2,1)S(1)} %fusion.2.own_ref), channel_id=1, source_target_pairs={{1,0},{2,1},{3,2},{4,3},{5,4},{6,5},{7,6},{8,7},{9,8},{10,9},{11,1... | collective-permute-start | bytes 1671176 | tf_op jit(solution)/shard_map/ppermute | solution.py:349
  4.6 13.3 %collective-permute-start.3 = (f16[128,256]{1,0:T(8,128)(2,1)S(1)}, f16[128,256]{1,0:T(8,128)(2,1)S(1)}, u32[]{:S(2)}, u32[]{:S(2)}) collective-permute-start(f16[128,256]{1,0:T(8,128)(2,1)S(1)} %multiply_convert_fusion), channel_id=1, source_target_pairs={{0,8},{1,9},{2,10},{3,11},{4,12},{5,13},{6,14},{7,15},{8,0},{9,1},... | collective-permute-start | bytes 196616 | tf_op jit(solution)/shard_map/ppermute | solution.py:285
  9.2 13.4 %collective-permute-start.2 = (f16[128,256]{1,0:T(8,128)(2,1)S(1)}, f16[128,256]{1,0:T(8,128)(2,1)S(1)}, u32[]{:S(2)}, u32[]{:S(2)}) collective-permute-start(f16[128,256]{1,0:T(8,128)(2,1)S(1)} %multiply_convert_fusion), channel_id=1, source_target_pairs={{0,12},{1,13},{2,14},{3,15},{4,0},{5,1},{6,2},{7,3},{8,4},{9,5},{1... | collective-permute-start | bytes 196616 | tf_op jit(solution)/shard_map/ppermute | solution.py:285
  9.8 12.8 %collective-permute-start.4 = (f16[128,256]{1,0:T(8,128)(2,1)S(1)}, f16[128,256]{1,0:T(8,128)(2,1)S(1)}, u32[]{:S(2)}, u32[]{:S(2)}) collective-permute-start(f16[128,256]{1,0:T(8,128)(2,1)S(1)} %multiply_convert_fusion), channel_id=1, source_target_pairs={{0,4},{1,5},{2,6},{3,7},{4,8},{5,9},{6,10},{7,11},{8,12},{9,13},{1... | collective-permute-start | bytes 196616 | tf_op jit(solution)/shard_map/ppermute | solution.py:285
  10.7 16.3 %collective-permute-start = (bf16[17,128,128]{2,1,0:T(8,128)(2,1)S(1)}, bf16[17,128,128]{2,1,0:T(8,128)(2,1)S(1)}, u32[]{:S(2)}, u32[]{:S(2)}) collective-permute-start(bf16[17,128,128]{2,1,0:T(8,128)(2,1)S(1)} %fusion.2.own_ref), channel_id=1, source_target_pairs={{0,1},{1,2},{2,3},{3,4},{4,5},{5,6},{6,7},{7,8},{8,9},{9,10},{10,1... | collective-permute-start | bytes 1671176 | tf_op jit(solution)/shard_map/ppermute | solution.py:349
  22.7 26.2 %collective-permute-start.6 = (f16[4,128,256]{2,1,0:T(8,128)(2,1)S(1)}, f16[4,128,256]{2,1,0:T(8,128)(2,1)S(1)}, u32[]{:S(2)}, u32[]{:S(2)}) collective-permute-start(f16[4,128,256]{2,1,0:T(8,128)(2,1)S(1)} %get-tuple-element.39), channel_id=1, source_target_pairs={{0,2},{1,3},{2,0},{3,1},{4,6},{5,7},{6,4},{7,5},{8,10},{9,11},{10,... | collective-permute-start | bytes 786440 | tf_op jit(solution)/shard_map/ppermute | solution.py:285
  25.5 23.4 %collective-permute-start.5 = (f16[4,128,256]{2,1,0:T(8,128)(2,1)S(1)}, f16[4,128,256]{2,1,0:T(8,128)(2,1)S(1)}, u32[]{:S(2)}, u32[]{:S(2)}) collective-permute-start(f16[4,128,256]{2,1,0:T(8,128)(2,1)S(1)} %get-tuple-element.39), channel_id=1, source_target_pairs={{0,3},{1,0},{2,1},{3,2},{4,7},{5,4},{6,5},{7,6},{8,11},{9,8},{10,9... | collective-permute-start | bytes 786440 | tf_op jit(solution)/shard_map/ppermute | solution.py:285
  26.4 22.5 %collective-permute-start.7 = (f16[4,128,256]{2,1,0:T(8,128)(2,1)S(1)}, f16[4,128,256]{2,1,0:T(8,128)(2,1)S(1)}, u32[]{:S(2)}, u32[]{:S(2)}) collective-permute-start(f16[4,128,256]{2,1,0:T(8,128)(2,1)S(1)} %get-tuple-element.39), channel_id=1, source_target_pairs={{0,1},{1,2},{2,3},{3,0},{4,5},{5,6},{6,7},{7,4},{8,9},{9,10},{10,1... | collective-permute-start | bytes 786440 | tf_op jit(solution)/shard_map/ppermute | solution.py:285
  27.0 0.7 copy-start.5
  51.1 6.5 %copy-start.6 = (s32[17,32]{1,0:T(8,128)S(1)}, s32[17,32]{1,0:T(8,128)}, u32[]{:S(2)}) copy-start(s32[17,32]{1,0:T(8,128)} %shard_map.77.table) | copy-start | bytes 6532
  51.1 16.5 %collective-permute-start.8 = (bf16[2,128,2048]{2,1,0:T(8,128)(2,1)}, bf16[2,128,2048]{2,1,0:T(8,128)(2,1)S(1)}, u32[]{:S(2)}, u32[]{:S(2)}) collective-permute-start(bf16[2,128,2048]{2,1,0:T(8,128)(2,1)} %get-tuple-element.25.refs_0_), channel_id=1, source_target_pairs={{0,4},{1,5},{2,6},{3,7},{4,8},{5,9},{6,10},{7,11},{8,12},{9,13},{1... | collective-permute-start | bytes 3145736 | tf_op jit(solution)/shard_map/ppermute | solution.py:285
  51.1 16.5 %collective-permute-start.9 = (bf16[2,128,2048]{2,1,0:T(8,128)(2,1)}, bf16[2,128,2048]{2,1,0:T(8,128)(2,1)S(1)}, u32[]{:S(2)}, u32[]{:S(2)}) collective-permute-start(bf16[2,128,2048]{2,1,0:T(8,128)(2,1)} %get-tuple-element.27.refs_1_), channel_id=1, source_target_pairs={{0,12},{1,13},{2,14},{3,15},{4,0},{5,1},{6,2},{7,3},{8,4},{9,5},{1... | collective-permute-start | bytes 3145736 | tf_op jit(solution)/shard_map/ppermute | solution.py:285
  55.0 47.7 %collective-permute-start.11 = (bf16[2,128,2048]{2,1,0:T(8,128)(2,1)}, bf16[2,128,2048]{2,1,0:T(8,128)(2,1)S(1)}, u32[]{:S(2)}, u32[]{:S(2)}) collective-permute-start(bf16[2,128,2048]{2,1,0:T(8,128)(2,1)} %get-tuple-element.28.refs_2_), channel_id=1, source_target_pairs={{0,4},{1,5},{2,6},{3,7},{4,8},{5,9},{6,10},{7,11},{8,12},{9,13},{1... | collective-permute-start | bytes 3145736 | tf_op jit(solution)/shard_map/ppermute | solution.py:285
  55.0 47.7 %collective-permute-start.12 = (bf16[2,128,2048]{2,1,0:T(8,128)(2,1)}, bf16[2,128,2048]{2,1,0:T(8,128)(2,1)}, u32[]{:S(2)}, u32[]{:S(2)}) collective-permute-start(bf16[2,128,2048]{2,1,0:T(8,128)(2,1)} %get-tuple-element.29.refs_3_), channel_id=1, source_target_pairs={{0,12},{1,13},{2,14},{3,15},{4,0},{5,1},{6,2},{7,3},{8,4},{9,5},{1... | collective-permute-start | bytes 3145736 | tf_op jit(solution)/shard_map/ppermute | solution.py:285
  57.6 1.2 copy-start.2
  58.9 8.8 %copy-start = (bf16[2,128,2048]{2,1,0:T(8,128)(2,1)S(1)}, bf16[2,128,2048]{2,1,0:T(8,128)(2,1)}, u32[]{:S(2)}) copy-start(bf16[2,128,2048]{2,1,0:T(8,128)(2,1)} %get-tuple-element.21.refs_4_.up) | copy-start | bytes 3145732
  58.9 8.8 %copy-start.1 = (bf16[2,128,2048]{2,1,0:T(8,128)(2,1)S(1)}, bf16[2,128,2048]{2,1,0:T(8,128)(2,1)}, u32[]{:S(2)}) copy-start(bf16[2,128,2048]{2,1,0:T(8,128)(2,1)} %get-tuple-element.26.refs_5_.down) | copy-start | bytes 3145732
  67.6 35.1 %copy-start.3 = (bf16[2,128,2048]{2,1,0:T(8,128)(2,1)S(1)}, bf16[2,128,2048]{2,1,0:T(8,128)(2,1)}, u32[]{:S(2)}) copy-start(bf16[2,128,2048]{2,1,0:T(8,128)(2,1)} %get-tuple-element.19.refs_6_.own_a) | copy-start | bytes 3145732
  67.6 35.1 %copy-start.4 = (bf16[2,128,2048]{2,1,0:T(8,128)(2,1)S(1)}, bf16[2,128,2048]{2,1,0:T(8,128)(2,1)}, u32[]{:S(2)}) copy-start(bf16[2,128,2048]{2,1,0:T(8,128)(2,1)} %get-tuple-element.20.refs_7_.own_b) | copy-start | bytes 3145732
  70.0 32.7 %collective-permute-start.10 = (bf16[2,128,2048]{2,1,0:T(8,128)(2,1)}, bf16[2,128,2048]{2,1,0:T(8,128)(2,1)}, u32[]{:S(2)}, u32[]{:S(2)}) collective-permute-start(bf16[2,128,2048]{2,1,0:T(8,128)(2,1)} %get-tuple-element.30), channel_id=1, source_target_pairs={{0,4},{1,5},{2,6},{3,7},{4,8},{5,9},{6,10},{7,11},{8,12},{9,13},{1... | collective-permute-start | bytes 3145736 | tf_op jit(solution)/shard_map/ppermute | solution.py:285
  70.7 32.0 %collective-permute-start.13 = (bf16[2,128,2048]{2,1,0:T(8,128)(2,1)}, bf16[2,128,2048]{2,1,0:T(8,128)(2,1)}, u32[]{:S(2)}, u32[]{:S(2)}) collective-permute-start(bf16[2,128,2048]{2,1,0:T(8,128)(2,1)} %get-tuple-element.31), channel_id=1, source_target_pairs={{0,12},{1,13},{2,14},{3,15},{4,0},{5,1},{6,2},{7,3},{8,4},{9,5},{1... | collective-permute-start | bytes 3145736 | tf_op jit(solution)/shard_map/ppermute | solution.py:285
  105.1 20.5 %collective-permute-start.14 = (bf16[128,2048]{1,0:T(8,128)(2,1)S(1)}, bf16[128,2048]{1,0:T(8,128)(2,1)S(1)}, u32[]{:S(2)}, u32[]{:S(2)}) collective-permute-start(bf16[128,2048]{1,0:T(8,128)(2,1)S(1)} %get-tuple-element.33), channel_id=1, source_target_pairs={{0,2},{1,3},{2,0},{3,1},{4,6},{5,7},{6,4},{7,5},{8,10},{9,11},{10,... | collective-permute-start | bytes 1572872 | tf_op jit(solution)/shard_map/ppermute | solution.py:285
  107.1 18.5 %collective-permute-start.15 = (bf16[128,2048]{1,0:T(8,128)(2,1)S(1)}, bf16[128,2048]{1,0:T(8,128)(2,1)S(1)}, u32[]{:S(2)}, u32[]{:S(2)}) collective-permute-start(bf16[128,2048]{1,0:T(8,128)(2,1)S(1)} %get-tuple-element.34), channel_id=1, source_target_pairs={{0,1},{1,2},{2,3},{3,0},{4,5},{5,6},{6,7},{7,4},{8,9},{9,10},{10,1... | collective-permute-start | bytes 1572872 | tf_op jit(solution)/shard_map/ppermute | solution.py:285
  107.7 17.9 %collective-permute-start.16 = (bf16[128,2048]{1,0:T(8,128)(2,1)S(1)}, bf16[128,2048]{1,0:T(8,128)(2,1)S(1)}, u32[]{:S(2)}, u32[]{:S(2)}) collective-permute-start(bf16[128,2048]{1,0:T(8,128)(2,1)S(1)} %get-tuple-element.35), channel_id=1, source_target_pairs={{0,3},{1,0},{2,1},{3,2},{4,7},{5,4},{6,5},{7,6},{8,11},{9,8},{10,9... | collective-permute-start | bytes 1572872 | tf_op jit(solution)/shard_map/ppermute | solution.py:285

commit v4 on v3

--- a/solution.py
+++ b/solution.py
@@ -11,7 +11,6 @@
 TILE = 128
 RB = 16
 KA = 27
-GROUP = 1
 SIDE = 4
 WIDTH = CBS * TILE
 C2 = 256
@@ -98,18 +97,22 @@
         slot = lax.rem(r, 2)
         count = table[i, COUNT]
         left = tiles[RB + i].T
-        for k in range(0, KA, GROUP):
-            products, places = [], []
-            for s in range(k, min(k + GROUP, KA)):
+        for k in range(0, KA, 2):
+            terms, places = [], []
+            for s in range(k, min(k + 2, KA)):
                 col = jnp.clip(table[i, s], 0, 3 * RB - 1)
                 block = jnp.clip(maps[lax.shift_right_logical(col, 4), lax.bitwise_and(col, RB - 1)], 0, CBS - 1)
                 places.append(pl.multiple_of(jnp.where(s < count, block, CBS) * TILE, TILE))
-                products.append(
-                    jnp.dot(a_buf[slot, s], tiles[col], preferred_element_type=jnp.float32).astype(jnp.bfloat16)
-                )
-            terms = jnp.dot(left, jnp.concatenate(products, axis=1) if len(products) > 1 else products[0], preferred_element_type=jnp.float32)
-            for n, place in enumerate(places):
-                acc[:, pl.ds(place, TILE)] += terms[:, n * TILE:(n + 1) * TILE]
+                product = jnp.dot(a_buf[slot, s], tiles[col], preferred_element_type=jnp.float32).astype(jnp.bfloat16)
+                terms.append(jnp.dot(left, product, preferred_element_type=jnp.float32))
+            columns = [pl.ds(place, TILE) for place in places]
+            held = [acc[:, column] for column in columns]
+            first = held[0] + terms[0]
+            if len(columns) == 2:
+                second = jnp.where(places[0] == places[1], first, held[1]) + terms[1]
+            acc[:, columns[0]] = first
+            if len(columns) == 2:
+                acc[:, columns[1]] = second
         return 0
 
     def leave(n, half):
@@ -361,8 +364,9 @@
     far_a, far_b = held_back(far_a, far_b, prolong_high)
     parts = (far_a, far_b, up_b, down_a, up_a, down_b, own_a, own_b)
     from_far_a, from_far_b = send(far_a, 0, 1), send(far_b, 0, -1)
+    own_term = coarsest_term(table, parts, prolong_high, prolong_low)
+    up_b, down_a = held_back(up_b, down_a, own_term)
     from_up_b, from_down_a = send(up_b, 0, 1), send(down_a, 0, -1)
-    own_term = coarsest_term(table, parts, prolong_high, prolong_low)
     up_a, down_b = joined(up_a, from_far_a, down_b, from_far_b, own_term)
     from_up_a, from_down_b = send(up_a, 0, 1), send(down_b, 0, -1)
 

time: 129 us -> 133 us (1.031)
  local copies, waits for them, and re-layouts: 3.37 us -> 8.41 us
  blocking collectives: 45.7 us -> 43.8 us
  Pallas kernels: 37.4 us -> 38.8 us
    unnamed x15 -> x23, local copies, waits for them, and re-layouts: 2.65 us -> 7.7 us
    all_to_all x1, blocking collectives: 29.9 us -> 26.7 us  [share_out(): return jnp.sum(lax.all_to_all(pieces, ('sect', 'rows'), 0, 0), axis=0)]
    pallas_call x1, Pallas kernels: 2.28 us -> 3.92 us  [joined(): pl.pallas_call(joined_body, out_shape=[jax.ShapeDtypeStruct(up.shape, jnp...]
where the time goes in v4:
time: 133 us; the launch traced here: 132 us
  blocking collectives  43.8 us (33%)
  Pallas kernels  38.8 us (29%)
  starting transfers between devices  27.8 us (21%)
  local copies, waits for them, and re-layouts  8.41 us (6%)
  other arithmetic  7.29 us (5%)
  waiting for transfers between devices  4.77 us (4%)
    all_to_all x1, blocking collectives, share_out(): return jnp.sum(lax.all_to_all(pieces, ('sect', 'rows'), 0, 0), axis=0)  26.7 us
    ppermute x15, starting transfers between devices, send(): return lax.ppermute(value, ('sect', 'rows'), STEPS[second][by])  23.9 us
    pallas_call x1, Pallas kernels, galerkin(): pl.pallas_call(galerkin_body, out_shape=[jax.ShapeDtypeStruct((2, TILE, W...  21.2 us
    all_to_all x1, blocking collectives, bring_back(): lax.all_to_all(jnp.broadcast_to(piece[None], (128,) + piece.shape), ('sec...  17 us
    pallas_call x1, Pallas kernels, coarsest_term(): pl.pallas_call(coarsest_body, out_shape=jax.ShapeDtypeStruct((C2, C2), jn...  8.71 us
    unnamed x23, local copies, waits for them, and re-layouts  7.7 us
    ppermute x15, waiting for transfers between devices, send(): return lax.ppermute(value, ('sect', 'rows'), STEPS[second][by])  4.77 us
    pallas_call x1, Pallas kernels, joined(): pl.pallas_call(joined_body, out_shape=[jax.ShapeDtypeStruct(up.shape, jnp...  3.92 us
  transfers between devices with their start and end apart: 17, of which 1 were waited for; matrix products, arithmetic and copies ran while one was open for 2% of the time, Pallas kernels for 28%

profile of v4, /device:TPU:1, one launch (start us, length us, event | category | flops | bytes accessed | tf_op | source)
XLA Modules:
  0.0 131.7 jit_solution(14166226518297076618)
XLA Ops:
  0.6 0.7 subtract_bitcast_fusion
  1.3 1.1 fusion.2.own_ref
  2.4 1.3 collective-permute-start.1
  3.7 0.9 multiply_convert_fusion
  4.6 4.6 %collective-permute-start.3 = (f16[128,256]{1,0:T(8,128)(2,1)S(1)}, f16[128,256]{1,0:T(8,128)(2,1)S(1)}, u32[]{:S(2)}, u32[]{:S(2)}) collective-permute-start(f16[128,256]{1,0:T(8,128)(2,1)S(1)} %multiply_convert_fusion), channel_id=1, source_target_pairs={{0,8},{1,9},{2,10},{3,11},{4,12},{5,13},{6,14},{7,15},{8,0},{9,1},... | collective-permute-start | bytes 196616 | tf_op jit(solution)/shard_map/ppermute | solution.py:288
  9.2 0.6 collective-permute-start.2
  9.8 0.8 collective-permute-start.4
  10.7 2.6 %collective-permute-start = (bf16[17,128,128]{2,1,0:T(8,128)(2,1)S(1)}, bf16[17,128,128]{2,1,0:T(8,128)(2,1)S(1)}, u32[]{:S(2)}, u32[]{:S(2)}) collective-permute-start(bf16[17,128,128]{2,1,0:T(8,128)(2,1)S(1)} %fusion.2.own_ref), channel_id=1, source_target_pairs={{0,1},{1,2},{2,3},{3,4},{4,5},{5,6},{6,7},{7,8},{8,9},{9,10},{10,1... | collective-permute-start | bytes 1671176 | tf_op jit(solution)/shard_map/ppermute | solution.py:352
  13.3 0.9 fusion.6
  14.3 0.7 stack.61.info
  14.9 2.9 %shard_map.77.table = s32[17,32]{1,0:T(8,128)} custom-call(s32[16,27]{1,0:T(8,128)} %cols.1, s32[16]{0:T(128)} %counts.1, s32[16]{0:T(128)} %own_map.1, s32[8]{0:T(128)} %stack.61.info), custom_call_target="tpu_custom_call" | custom-call | bytes 11100000 | tf_op jit(solution)/shard_map/pallas_call | solution.py:62
  17.9 0.0 collective-permute-done.3
  17.9 4.7 %collective-permute-done.2 = f16[128,256]{1,0:T(8,128)(2,1)S(1)} collective-permute-done((f16[128,256]{1,0:T(8,128)(2,1)S(1)}, f16[128,256]{1,0:T(8,128)(2,1)S(1)}, u32[]{:S(2)}, u32[]{:S(2)}) %collective-permute-start.2) | collective-permute-done | bytes 65568 | tf_op jit(solution)/shard_map/ppermute | solution.py:288
  22.6 0.0 collective-permute-done.4
  22.6 0.1 fusion.5
  22.7 2.8 %collective-permute-start.6 = (f16[4,128,256]{2,1,0:T(8,128)(2,1)S(1)}, f16[4,128,256]{2,1,0:T(8,128)(2,1)S(1)}, u32[]{:S(2)}, u32[]{:S(2)}) collective-permute-start(f16[4,128,256]{2,1,0:T(8,128)(2,1)S(1)} %get-tuple-element.43), channel_id=1, source_target_pairs={{0,2},{1,3},{2,0},{3,1},{4,6},{5,7},{6,4},{7,5},{8,10},{9,11},{10,... | collective-permute-start | bytes 786440 | tf_op jit(solution)/shard_map/ppermute | solution.py:288
  25.5 0.9 collective-permute-start.5
  26.4 0.6 collective-permute-start.7
  27.0 0.0 collective-permute-done.1.right_ref
  27.0 0.0 collective-permute-done.left_ref
  27.0 0.0 copy-start.9
  27.0 0.7 copy-done.9
  27.7 21.2 %shard_map.78 = (bf16[2,128,2048]{2,1,0:T(8,128)(2,1)}, bf16[2,128,2048]{2,1,0:T(8,128)(2,1)}, bf16[2,128,2048]{2,1,0:T(8,128)(2,1)}, bf16[2,128,2048]{2,1,0:T(8...) custom-call(s32[17,32]{1,0:T(8,128)S(1)} %copy-done.9, ...), custom_call_target="tpu_custom_call" | custom-call | bytes 74000000 | tf_op jit(solution)/shard_map/pallas_call | solution.py:146
  48.9 0.0 collective-permute-done.6
  48.9 0.0 collective-permute-done.5
  48.9 0.0 collective-permute-done.7
  48.9 0.3 convert_multiply_fusion
  49.3 1.8 %fusion = (bf16[16,128,256]{2,1,0:T(8,128)(2,1)}, bf16[16,128,256]{2,1,0:T(8,128)(2,1)}) fusion(f32[4,4,128,256]{3,2,1,0:T(8,128)S(1)} %convert_multiply_fusion), kind=kLoop, calls=%fused_computation.2 | loop fusion | flops 2097152 | bytes 4194304 | tf_op jit(solution)/shard_map/convert_element_type | solution.py:362
  51.1 0.0 collective-permute-start.8
  51.1 3.5 %collective-permute-start.9 = (bf16[2,128,2048]{2,1,0:T(8,128)(2,1)}, bf16[2,128,2048]{2,1,0:T(8,128)(2,1)}, u32[]{:S(2)}, u32[]{:S(2)}) collective-permute-start(bf16[2,128,2048]{2,1,0:T(8,128)(2,1)} %get-tuple-element.29.refs_1_), channel_id=1, source_target_pairs={{0,12},{1,13},{2,14},{3,15},{4,0},{5,1},{6,2},{7,3},{8,4},{9,5},{1... | collective-permute-start | bytes 3145736 | tf_op jit(solution)/shard_map/ppermute | solution.py:288
  54.7 0.0 copy-done.10
  54.7 1.2 copy-done.4
  55.9 8.7 %shard_map.80._.refs_2_ = f32[256,256]{1,0:T(8,128)S(1)} custom-call(s32[17,32]{1,0:T(8,128)S(1)} %copy-done.10, bf16[2,128,2048]{2,1,0:T(8,128)(2,1)S(1)} %copy-done.4, bf16[2,128,2048]{2,1,0:T(8,128)(2,1)} %get-tuple-element.29.refs_1_, bf16[2,128,2048]{2,1,0:T(8,128)(2,1)} %get-tuple-element.30.refs_2_.refs_0_, ...), custom_call_target="tpu_custom_call" | custom-call | bytes 22200000 | tf_op jit(solution)/shard_map/pallas_call | solution.py:214
  64.6 0.0 copy-start
  64.6 0.7 copy-done
  65.3 0.0 collective-permute-start.11
  65.3 2.7 %collective-permute-start.12 = (bf16[2,128,2048]{2,1,0:T(8,128)(2,1)}, bf16[2,128,2048]{2,1,0:T(8,128)(2,1)}, u32[]{:S(2)}, u32[]{:S(2)}) collective-permute-start(bf16[2,128,2048]{2,1,0:T(8,128)(2,1)} %get-tuple-element.34), channel_id=1, source_target_pairs={{0,12},{1,13},{2,14},{3,15},{4,0},{5,1},{6,2},{7,3},{8,4},{9,5},{1... | collective-permute-start | bytes 3145736 | tf_op jit(solution)/shard_map/ppermute | solution.py:288
  68.0 0.0 collective-permute-done.8.from_far_a
  68.0 1.0 copy-done.7
  69.0 0.0 collective-permute-done.9.from_far_b
  69.0 0.0 copy-done.2
  69.0 0.0 copy-start.1
  69.0 0.9 copy-done.1
  69.9 1.2 copy-done.8
  71.2 3.9 %shard_map.81 = (bf16[2,128,2048]{2,1,0:T(8,128)(2,1)}, bf16[2,128,2048]{2,1,0:T(8,128)(2,1)}) custom-call(bf16[2,128,2048]{2,1,0:T(8,128)(2,1)S(1)} %copy-done.2, bf16[2,128,2048]{2,1,0:T(8,128)(2,1)S(1)} %copy-done.8, bf16[2,128,2048]{2,1,0:T(8,128)(2,1)S(1)} %copy-done.3, bf16[2,128,2048]{2,1,0:T(8,128)(2,1)} %collective-permute-done.9.from_far_b, ...), custom_call_target="tpu_custom_call" | custom-call | bytes 7400000 | tf_op jit(solution)/shard_map/pallas_call | solution.py:259
  75.1 0.0 collective-permute-start.10
  75.1 2.7 %collective-permute-start.13 = (bf16[2,128,2048]{2,1,0:T(8,128)(2,1)}, bf16[2,128,2048]{2,1,0:T(8,128)(2,1)S(1)}, u32[]{:S(2)}, u32[]{:S(2)}) collective-permute-start(bf16[2,128,2048]{2,1,0:T(8,128)(2,1)} %get-tuple-element.35), channel_id=1, source_target_pairs={{0,12},{1,13},{2,14},{3,15},{4,0},{5,1},{6,2},{7,3},{8,4},{9,5},{1... | collective-permute-start | bytes 3145736 | tf_op jit(solution)/shard_map/ppermute | solution.py:288
  77.8 26.7 %all_to_all.10 = f32[128,4,128]{2,1,0:T(4,128)S(1)} all-to-all(f32[128,4,128]{2,1,0:T(4,128)S(1)} %bitcast.44), channel_id=1, replica_groups=mesh['sect'=8,'rows'=16] {'sect','rows'}, dimensions={0} | all-to-all | bytes 524288 | tf_op jit(solution)/shard_map/all_to_all | solution.py:297
  104.5 0.1 reduce_sum.9._
  104.6 0.0 collective-permute-done.11.up_b
  104.6 0.0 collective-permute-done.12.down_a
  104.6 0.0 collective-permute-done.10.up_a
  104.6 0.0 collective-permute-done.13.down_b
  104.7 1.2 copy-done.6
  105.9 2.1 %shard_map.83 = (bf16[128,2048]{1,0:T(8,128)(2,1)S(1)}, bf16[128,2048]{1,0:T(8,128)(2,1)S(1)}, bf16[128,2048]{1,0:T(8,128)(2,1)S(1)}, f32[128,2048]{1,0:T(8,128)S(1)}) custom-call(bf16[2,128,2048]{2,1,0:T(8,128)(2,1)S(1)} %copy-done.5, bf16[2,128,2048]{2,1,0:T(8,128)(2,1)S(1)} %copy-done.6, bf16[2,128,2048]{2,1,0:T(8,128)(2,1)S(1)} %collective-permute-done.10.up_a, ...), custom_call_target="tpu_custom_call" | custom-call | bytes 11100000 | tf_op jit(solution)/shard_map/pallas_call | solution.py:327
  108.0 2.0 %collective-permute-start.14 = (bf16[128,2048]{1,0:T(8,128)(2,1)S(1)}, bf16[128,2048]{1,0:T(8,128)(2,1)S(1)}, u32[]{:S(2)}, u32[]{:S(2)}) collective-permute-start(bf16[128,2048]{1,0:T(8,128)(2,1)S(1)} %get-tuple-element.37), channel_id=1, source_target_pairs={{0,2},{1,3},{2,0},{3,1},{4,6},{5,7},{6,4},{7,5},{8,10},{9,11},{10,... | collective-permute-start | bytes 1572872 | tf_op jit(solution)/shard_map/ppermute | solution.py:288
  110.0 1.3 %collective-permute-start.15 = (bf16[128,2048]{1,0:T(8,128)(2,1)S(1)}, bf16[128,2048]{1,0:T(8,128)(2,1)S(1)}, u32[]{:S(2)}, u32[]{:S(2)}) collective-permute-start(bf16[128,2048]{1,0:T(8,128)(2,1)S(1)} %get-tuple-element.38), channel_id=1, source_target_pairs={{0,1},{1,2},{2,3},{3,0},{4,5},{5,6},{6,7},{7,4},{8,9},{9,10},{10,1... | collective-permute-start | bytes 1572872 | tf_op jit(solution)/shard_map/ppermute | solution.py:288
  111.3 1.3 %collective-permute-start.16 = (bf16[128,2048]{1,0:T(8,128)(2,1)S(1)}, bf16[128,2048]{1,0:T(8,128)(2,1)S(1)}, u32[]{:S(2)}, u32[]{:S(2)}) collective-permute-start(bf16[128,2048]{1,0:T(8,128)(2,1)S(1)} %get-tuple-element.39), channel_id=1, source_target_pairs={{0,3},{1,0},{2,1},{3,2},{4,7},{5,4},{6,5},{7,6},{8,11},{9,8},{10,9... | collective-permute-start | bytes 1572872 | tf_op jit(solution)/shard_map/ppermute | solution.py:288
  112.7 17.0 %all_to_all.11 = f32[128,4,128]{2,1,0:T(4,128)S(1)} all-to-all(f32[128,4,128]{2,1,0:T(4,128)S(1)} %broadcast_in_dim.10), channel_id=1, replica_groups=mesh['sect'=8,'rows'=16] {'sect','rows'}, dimensions={0} | all-to-all | bytes 524288 | tf_op jit(solution)/shard_map/all_to_all | solution.py:301
  129.7 0.0 collective-permute-done.14
  129.7 0.0 collective-permute-done.15
  129.7 0.0 collective-permute-done.16
  129.7 1.3 add_add_fusion
  131.0 0.7 copy.17
  (17 shorter events, 0.1 us)
Async XLA Ops:
  2.4 24.6 %collective-permute-start.1 = (bf16[17,128,128]{2,1,0:T(8,128)(2,1)S(1)}, bf16[17,128,128]{2,1,0:T(8,128)(2,1)S(1)}, u32[]{:S(2)}, u32[]{:S(2)}) collective-permute-start(bf16[17,128,128]{2,1,0:T(8,128)(2,1)S(1)} %fusion.2.own_ref), channel_id=1, source_target_pairs={{1,0},{2,1},{3,2},{4,3},{5,4},{6,5},{7,6},{8,7},{9,8},{10,9},{11,1... | collective-permute-start | bytes 1671176 | tf_op jit(solution)/shard_map/ppermute | solution.py:352
  4.6 13.2 %collective-permute-start.3 = (f16[128,256]{1,0:T(8,128)(2,1)S(1)}, f16[128,256]{1,0:T(8,128)(2,1)S(1)}, u32[]{:S(2)}, u32[]{:S(2)}) collective-permute-start(f16[128,256]{1,0:T(8,128)(2,1)S(1)} %multiply_convert_fusion), channel_id=1, source_target_pairs={{0,8},{1,9},{2,10},{3,11},{4,12},{5,13},{6,14},{7,15},{8,0},{9,1},... | collective-permute-start | bytes 196616 | tf_op jit(solution)/shard_map/ppermute | solution.py:288
  9.2 13.4 %collective-permute-start.2 = (f16[128,256]{1,0:T(8,128)(2,1)S(1)}, f16[128,256]{1,0:T(8,128)(2,1)S(1)}, u32[]{:S(2)}, u32[]{:S(2)}) collective-permute-start(f16[128,256]{1,0:T(8,128)(2,1)S(1)} %multiply_convert_fusion), channel_id=1, source_target_pairs={{0,12},{1,13},{2,14},{3,15},{4,0},{5,1},{6,2},{7,3},{8,4},{9,5},{1... | collective-permute-start | bytes 196616 | tf_op jit(solution)/shard_map/ppermute | solution.py:288
  9.8 12.8 %collective-permute-start.4 = (f16[128,256]{1,0:T(8,128)(2,1)S(1)}, f16[128,256]{1,0:T(8,128)(2,1)S(1)}, u32[]{:S(2)}, u32[]{:S(2)}) collective-permute-start(f16[128,256]{1,0:T(8,128)(2,1)S(1)} %multiply_convert_fusion), channel_id=1, source_target_pairs={{0,4},{1,5},{2,6},{3,7},{4,8},{5,9},{6,10},{7,11},{8,12},{9,13},{1... | collective-permute-start | bytes 196616 | tf_op jit(solution)/shard_map/ppermute | solution.py:288
  10.7 16.3 %collective-permute-start = (bf16[17,128,128]{2,1,0:T(8,128)(2,1)S(1)}, bf16[17,128,128]{2,1,0:T(8,128)(2,1)S(1)}, u32[]{:S(2)}, u32[]{:S(2)}) collective-permute-start(bf16[17,128,128]{2,1,0:T(8,128)(2,1)S(1)} %fusion.2.own_ref), channel_id=1, source_target_pairs={{0,1},{1,2},{2,3},{3,4},{4,5},{5,6},{6,7},{7,8},{8,9},{9,10},{10,1... | collective-permute-start | bytes 1671176 | tf_op jit(solution)/shard_map/ppermute | solution.py:352
  22.7 26.2 %collective-permute-start.6 = (f16[4,128,256]{2,1,0:T(8,128)(2,1)S(1)}, f16[4,128,256]{2,1,0:T(8,128)(2,1)S(1)}, u32[]{:S(2)}, u32[]{:S(2)}) collective-permute-start(f16[4,128,256]{2,1,0:T(8,128)(2,1)S(1)} %get-tuple-element.43), channel_id=1, source_target_pairs={{0,2},{1,3},{2,0},{3,1},{4,6},{5,7},{6,4},{7,5},{8,10},{9,11},{10,... | collective-permute-start | bytes 786440 | tf_op jit(solution)/shard_map/ppermute | solution.py:288
  25.5 23.4 %collective-permute-start.5 = (f16[4,128,256]{2,1,0:T(8,128)(2,1)S(1)}, f16[4,128,256]{2,1,0:T(8,128)(2,1)S(1)}, u32[]{:S(2)}, u32[]{:S(2)}) collective-permute-start(f16[4,128,256]{2,1,0:T(8,128)(2,1)S(1)} %get-tuple-element.43), channel_id=1, source_target_pairs={{0,3},{1,0},{2,1},{3,2},{4,7},{5,4},{6,5},{7,6},{8,11},{9,8},{10,9... | collective-permute-start | bytes 786440 | tf_op jit(solution)/shard_map/ppermute | solution.py:288
  26.4 22.5 %collective-permute-start.7 = (f16[4,128,256]{2,1,0:T(8,128)(2,1)S(1)}, f16[4,128,256]{2,1,0:T(8,128)(2,1)S(1)}, u32[]{:S(2)}, u32[]{:S(2)}) collective-permute-start(f16[4,128,256]{2,1,0:T(8,128)(2,1)S(1)} %get-tuple-element.43), channel_id=1, source_target_pairs={{0,1},{1,2},{2,3},{3,0},{4,5},{5,6},{6,7},{7,4},{8,9},{9,10},{10,1... | collective-permute-start | bytes 786440 | tf_op jit(solution)/shard_map/ppermute | solution.py:288
  27.0 0.7 copy-start.9
  51.1 3.5 %copy-start.10 = (s32[17,32]{1,0:T(8,128)S(1)}, s32[17,32]{1,0:T(8,128)}, u32[]{:S(2)}) copy-start(s32[17,32]{1,0:T(8,128)} %shard_map.77.table) | copy-start | bytes 6532
  51.1 16.9 %collective-permute-start.8 = (bf16[2,128,2048]{2,1,0:T(8,128)(2,1)}, bf16[2,128,2048]{2,1,0:T(8,128)(2,1)S(1)}, u32[]{:S(2)}, u32[]{:S(2)}) collective-permute-start(bf16[2,128,2048]{2,1,0:T(8,128)(2,1)} %get-tuple-element.27.refs_0_), channel_id=1, source_target_pairs={{0,4},{1,5},{2,6},{3,7},{4,8},{5,9},{6,10},{7,11},{8,12},{9,13},{1... | collective-permute-start | bytes 3145736 | tf_op jit(solution)/shard_map/ppermute | solution.py:288
  51.1 17.8 %collective-permute-start.9 = (bf16[2,128,2048]{2,1,0:T(8,128)(2,1)}, bf16[2,128,2048]{2,1,0:T(8,128)(2,1)}, u32[]{:S(2)}, u32[]{:S(2)}) collective-permute-start(bf16[2,128,2048]{2,1,0:T(8,128)(2,1)} %get-tuple-element.29.refs_1_), channel_id=1, source_target_pairs={{0,12},{1,13},{2,14},{3,15},{4,0},{5,1},{6,2},{7,3},{8,4},{9,5},{1... | collective-permute-start | bytes 3145736 | tf_op jit(solution)/shard_map/ppermute | solution.py:288
  54.7 1.2 copy-start.4
  64.6 0.7 copy-start
  65.3 3.7 %copy-start.2 = (bf16[2,128,2048]{2,1,0:T(8,128)(2,1)S(1)}, bf16[2,128,2048]{2,1,0:T(8,128)(2,1)}, u32[]{:S(2)}) copy-start(bf16[2,128,2048]{2,1,0:T(8,128)(2,1)} %get-tuple-element.23.refs_4_.up) | copy-start | bytes 3145732
  65.3 3.7 %copy-start.3 = (bf16[2,128,2048]{2,1,0:T(8,128)(2,1)S(1)}, bf16[2,128,2048]{2,1,0:T(8,128)(2,1)}, u32[]{:S(2)}) copy-start(bf16[2,128,2048]{2,1,0:T(8,128)(2,1)} %get-tuple-element.28.refs_5_.down) | copy-start | bytes 3145732
  65.3 39.3 %collective-permute-start.11 = (bf16[2,128,2048]{2,1,0:T(8,128)(2,1)}, bf16[2,128,2048]{2,1,0:T(8,128)(2,1)}, u32[]{:S(2)}, u32[]{:S(2)}) collective-permute-start(bf16[2,128,2048]{2,1,0:T(8,128)(2,1)} %get-tuple-element.33), channel_id=1, source_target_pairs={{0,4},{1,5},{2,6},{3,7},{4,8},{5,9},{6,10},{7,11},{8,12},{9,13},{1... | collective-permute-start | bytes 3145736 | tf_op jit(solution)/shard_map/ppermute | solution.py:288
  65.3 39.3 %collective-permute-start.12 = (bf16[2,128,2048]{2,1,0:T(8,128)(2,1)}, bf16[2,128,2048]{2,1,0:T(8,128)(2,1)}, u32[]{:S(2)}, u32[]{:S(2)}) collective-permute-start(bf16[2,128,2048]{2,1,0:T(8,128)(2,1)} %get-tuple-element.34), channel_id=1, source_target_pairs={{0,12},{1,13},{2,14},{3,15},{4,0},{5,1},{6,2},{7,3},{8,4},{9,5},{1... | collective-permute-start | bytes 3145736 | tf_op jit(solution)/shard_map/ppermute | solution.py:288
  68.0 1.0 copy-start.7
  69.0 1.0 copy-start.1
  69.9 1.2 copy-start.8
  71.2 33.5 %copy-start.5 = (bf16[2,128,2048]{2,1,0:T(8,128)(2,1)S(1)}, bf16[2,128,2048]{2,1,0:T(8,128)(2,1)}, u32[]{:S(2)}) copy-start(bf16[2,128,2048]{2,1,0:T(8,128)(2,1)} %get-tuple-element.21.refs_6_.own_a) | copy-start | bytes 3145732
  75.1 29.6 %collective-permute-start.10 = (bf16[2,128,2048]{2,1,0:T(8,128)(2,1)}, bf16[2,128,2048]{2,1,0:T(8,128)(2,1)S(1)}, u32[]{:S(2)}, u32[]{:S(2)}) collective-permute-start(bf16[2,128,2048]{2,1,0:T(8,128)(2,1)} %get-tuple-element.32), channel_id=1, source_target_pairs={{0,4},{1,5},{2,6},{3,7},{4,8},{5,9},{6,10},{7,11},{8,12},{9,13},{1... | collective-permute-start | bytes 3145736 | tf_op jit(solution)/shard_map/ppermute | solution.py:288
  75.1 29.6 %collective-permute-start.13 = (bf16[2,128,2048]{2,1,0:T(8,128)(2,1)}, bf16[2,128,2048]{2,1,0:T(8,128)(2,1)S(1)}, u32[]{:S(2)}, u32[]{:S(2)}) collective-permute-start(bf16[2,128,2048]{2,1,0:T(8,128)(2,1)} %get-tuple-element.35), channel_id=1, source_target_pairs={{0,12},{1,13},{2,14},{3,15},{4,0},{5,1},{6,2},{7,3},{8,4},{9,5},{1... | collective-permute-start | bytes 3145736 | tf_op jit(solution)/shard_map/ppermute | solution.py:288
  104.7 1.2 copy-start.6
  108.0 21.8 %collective-permute-start.14 = (bf16[128,2048]{1,0:T(8,128)(2,1)S(1)}, bf16[128,2048]{1,0:T(8,128)(2,1)S(1)}, u32[]{:S(2)}, u32[]{:S(2)}) collective-permute-start(bf16[128,2048]{1,0:T(8,128)(2,1)S(1)} %get-tuple-element.37), channel_id=1, source_target_pairs={{0,2},{1,3},{2,0},{3,1},{4,6},{5,7},{6,4},{7,5},{8,10},{9,11},{10,... | collective-permute-start | bytes 1572872 | tf_op jit(solution)/shard_map/ppermute | solution.py:288
  110.0 19.8 %collective-permute-start.15 = (bf16[128,2048]{1,0:T(8,128)(2,1)S(1)}, bf16[128,2048]{1,0:T(8,128)(2,1)S(1)}, u32[]{:S(2)}, u32[]{:S(2)}) collective-permute-start(bf16[128,2048]{1,0:T(8,128)(2,1)S(1)} %get-tuple-element.38), channel_id=1, source_target_pairs={{0,1},{1,2},{2,3},{3,0},{4,5},{5,6},{6,7},{7,4},{8,9},{9,10},{10,1... | collective-permute-start | bytes 1572872 | tf_op jit(solution)/shard_map/ppermute | solution.py:288
  111.3 18.4 %collective-permute-start.16 = (bf16[128,2048]{1,0:T(8,128)(2,1)S(1)}, bf16[128,2048]{1,0:T(8,128)(2,1)S(1)}, u32[]{:S(2)}, u32[]{:S(2)}) collective-permute-start(bf16[128,2048]{1,0:T(8,128)(2,1)S(1)} %get-tuple-element.39), channel_id=1, source_target_pairs={{0,3},{1,0},{2,1},{3,2},{4,7},{5,4},{6,5},{7,6},{8,11},{9,8},{10,9... | collective-permute-start | bytes 1572872 | tf_op jit(solution)/shard_map/ppermute | solution.py:288

commit v5 on v3

--- a/solution.py
+++ b/solution.py
@@ -11,7 +11,9 @@
 TILE = 128
 RB = 16
 KA = 27
-GROUP = 1
+GROUP = 2
+AHEAD = 3
+CUTS = 3
 SIDE = 4
 WIDTH = CBS * TILE
 C2 = 256
@@ -74,10 +76,18 @@
     scale_ref[...] = jnp.full(scale_ref.shape, 1.0 / Q_SCALE, jnp.float32)
 
     def fetch(r):
-        slot = lax.rem(r, 2)
-        return pltpu.make_async_copy(a_ref.at[table[r, ORDER]], a_buf.at[slot], a_sem.at[slot])
-
-    fetch(0).start()
+        slot = lax.rem(r, AHEAD + 1)
+        part = KA // CUTS
+        return [
+            pltpu.make_async_copy(
+                a_ref.at[table[r, ORDER], pl.ds(n * part, part)], a_buf.at[slot, pl.ds(n * part, part)], a_sem.at[slot, n]
+            )
+            for n in range(CUTS)
+        ]
+
+    for r in range(AHEAD):
+        for copy in fetch(r):
+            copy.start()
     loads = [
         pltpu.make_async_copy(src.at[pl.ds(0, RB)], tiles.at[pl.ds(n * RB, RB)], p_sem.at[n])
         for n, src in enumerate((left_ref, own_ref, right_ref))
@@ -89,13 +99,15 @@
         load.wait()
 
     def row(r, _):
-        @pl.when(r + 1 < RB)
+        @pl.when(r + AHEAD < RB)
         def _():
-            fetch(r + 1).start()
-
-        fetch(r).wait()
+            for copy in fetch(r + AHEAD):
+                copy.start()
+
+        for copy in fetch(r):
+            copy.wait()
         i = table[r, ORDER]
-        slot = lax.rem(r, 2)
+        slot = lax.rem(r, AHEAD + 1)
         count = table[i, COUNT]
         left = tiles[RB + i].T
         for k in range(0, KA, GROUP):
@@ -150,11 +162,11 @@
             in_specs=[pl.BlockSpec(memory_space=pltpu.HBM)] + [anywhere] * 3,
             out_specs=[anywhere] * PAIRS + [pl.BlockSpec((1, TILE), lambda j, *_: (0, 0))],
             scratch_shapes=[
-                pltpu.VMEM((2, KA, TILE, TILE), jnp.bfloat16),
+                pltpu.VMEM((AHEAD + 1, KA, TILE, TILE), jnp.bfloat16),
                 pltpu.VMEM((3 * RB, TILE, TILE), jnp.bfloat16),
                 pltpu.VMEM((TILE, WIDTH + TILE), jnp.float32),
                 pltpu.VMEM((2, TILE, WIDTH), jnp.bfloat16),
-                pltpu.SemaphoreType.DMA((2,)),
+                pltpu.SemaphoreType.DMA((AHEAD + 1, CUTS)),
                 pltpu.SemaphoreType.DMA((3,)),
                 pltpu.SemaphoreType.DMA((2,)),
             ],
@@ -181,7 +193,7 @@
     loads = [
         pltpu.make_async_copy(part, held.at[pl.ds(2 * n, 2)], part_sem.at[n]) for n, part in enumerate(parts)
     ]
-    for copy in factors[:CBS] + loads[:2] + factors[CBS:]:
+    for copy in factors[:CBS] + loads[:4] + factors[CBS:]:
         copy.start()
     for m, (src, dst) in enumerate(((high_ref, right), (low_ref, rest))):
         pltpu.make_async_copy(src, dst.reshape(CBS, TILE, C2), q_sem.at[m]).wait()
@@ -191,8 +203,8 @@
         left_rest[:, columns] = rest[place, :].T
     for n in range(PAIRS):
         loads[n].wait()
-        if n + 2 < PAIRS:
-            loads[n + 2].start()
+        if n + 4 < PAIRS:
+            loads[n + 4].start()
         for m in (2 * n, 2 * n + 1):
             value = jnp.dot(held[m], right[...], preferred_element_type=jnp.float32)
             high = value.astype(jnp.bfloat16)

time: 129 us -> 126 us (0.977)
  Pallas kernels: 37.4 us -> 33.9 us
  blocking collectives: 45.7 us -> 47.3 us
    pallas_call x1, Pallas kernels: 21.1 us -> 18.2 us  [galerkin(): pl.pallas_call(galerkin_body, out_shape=[jax.ShapeDtypeStruct((2, TILE, W...]
    all_to_all x1, blocking collectives: 29.9 us -> 31.6 us  [share_out(): return jnp.sum(lax.all_to_all(pieces, ('sect', 'rows'), 0, 0), axis=0)]
  transfers between devices with their start and end apart: 17 -> 17, of which waited for: 1 -> 2; matrix products, arithmetic and copies ran while one was open for 2% -> 2% of each run, Pallas kernels for 28% -> 25%
where the time goes in v5:
time: 126 us; the launch traced here: 125 us
  blocking collectives  47.3 us (38%)
  Pallas kernels  33.9 us (27%)
  starting transfers between devices  27.5 us (22%)
  other arithmetic  7.27 us (6%)
  waiting for transfers between devices  5.29 us (4%)
  local copies, waits for them, and re-layouts  3.37 us (3%)
    all_to_all x1, blocking collectives, share_out(): return jnp.sum(lax.all_to_all(pieces, ('sect', 'rows'), 0, 0), axis=0)  31.6 us
    ppermute x15, starting transfers between devices, send(): return lax.ppermute(value, ('sect', 'rows'), STEPS[second][by])  23.5 us
    pallas_call x1, Pallas kernels, galerkin(): pl.pallas_call(galerkin_body, out_shape=[jax.ShapeDtypeStruct((2, TILE, W...  18.2 us
    all_to_all x1, blocking collectives, bring_back(): lax.all_to_all(jnp.broadcast_to(piece[None], (128,) + piece.shape), ('sec...  15.7 us
    pallas_call x1, Pallas kernels, coarsest_term(): pl.pallas_call(coarsest_body, out_shape=jax.ShapeDtypeStruct((C2, C2), jn...  8.15 us
    ppermute x15, waiting for transfers between devices, send(): return lax.ppermute(value, ('sect', 'rows'), STEPS[second][by])  5.28 us
    pallas_call x1, Pallas kernels, row_plan(): pl.pallas_call(plan_body, out_shape=jax.ShapeDtypeStruct((RB + 1, 32), jn...  2.91 us
    unnamed x15, local copies, waits for them, and re-layouts  2.65 us
  transfers between devices with their start and end apart: 17, of which 2 were waited for; matrix products, arithmetic and copies ran while one was open for 2% of the time, Pallas kernels for 25%

profile of v5, /device:TPU:1, one launch (start us, length us, event | category | flops | bytes accessed | tf_op | source)
XLA Modules:
  0.0 125.5 jit_solution(12520154415022023428)
XLA Ops:
  0.6 0.7 subtract_bitcast_fusion
  1.3 1.1 fusion.2.own_ref
  2.4 1.3 %collective-permute-start.1 = (bf16[17,128,128]{2,1,0:T(8,128)(2,1)S(1)}, bf16[17,128,128]{2,1,0:T(8,128)(2,1)S(1)}, u32[]{:S(2)}, u32[]{:S(2)}) collective-permute-start(bf16[17,128,128]{2,1,0:T(8,128)(2,1)S(1)} %fusion.2.own_ref), channel_id=1, source_target_pairs={{1,0},{2,1},{3,2},{4,3},{5,4},{6,5},{7,6},{8,7},{9,8},{10,9},{11,1... | collective-permute-start | bytes 1671176 | tf_op jit(solution)/shard_map/ppermute | solution.py:361
  3.7 0.9 multiply_convert_fusion
  4.6 4.6 %collective-permute-start.3 = (f16[128,256]{1,0:T(8,128)(2,1)S(1)}, f16[128,256]{1,0:T(8,128)(2,1)S(1)}, u32[]{:S(2)}, u32[]{:S(2)}) collective-permute-start(f16[128,256]{1,0:T(8,128)(2,1)S(1)} %multiply_convert_fusion), channel_id=1, source_target_pairs={{0,8},{1,9},{2,10},{3,11},{4,12},{5,13},{6,14},{7,15},{8,0},{9,1},... | collective-permute-start | bytes 196616 | tf_op jit(solution)/shard_map/ppermute | solution.py:297
  9.2 0.6 collective-permute-start.2
  9.8 0.8 collective-permute-start.4
  10.7 2.6 %collective-permute-start = (bf16[17,128,128]{2,1,0:T(8,128)(2,1)S(1)}, bf16[17,128,128]{2,1,0:T(8,128)(2,1)S(1)}, u32[]{:S(2)}, u32[]{:S(2)}) collective-permute-start(bf16[17,128,128]{2,1,0:T(8,128)(2,1)S(1)} %fusion.2.own_ref), channel_id=1, source_target_pairs={{0,1},{1,2},{2,3},{3,4},{4,5},{5,6},{6,7},{7,8},{8,9},{9,10},{10,1... | collective-permute-start | bytes 1671176 | tf_op jit(solution)/shard_map/ppermute | solution.py:361
  13.3 0.9 fusion.6
  14.3 0.7 stack.61.info
  15.0 2.9 %shard_map.77.table = s32[17,32]{1,0:T(8,128)} custom-call(s32[16,27]{1,0:T(8,128)} %cols.1, s32[16]{0:T(128)} %counts.1, s32[16]{0:T(128)} %own_map.1, s32[8]{0:T(128)} %stack.61.info), custom_call_target="tpu_custom_call" | custom-call | bytes 11100000 | tf_op jit(solution)/shard_map/pallas_call | solution.py:65
  17.9 0.0 collective-permute-done.3
  17.9 4.7 %collective-permute-done.2 = f16[128,256]{1,0:T(8,128)(2,1)S(1)} collective-permute-done((f16[128,256]{1,0:T(8,128)(2,1)S(1)}, f16[128,256]{1,0:T(8,128)(2,1)S(1)}, u32[]{:S(2)}, u32[]{:S(2)}) %collective-permute-start.2) | collective-permute-done | bytes 65568 | tf_op jit(solution)/shard_map/ppermute | solution.py:297
  22.6 0.0 collective-permute-done.4
  22.6 0.1 fusion.5
  22.7 2.8 %collective-permute-start.6 = (f16[4,128,256]{2,1,0:T(8,128)(2,1)S(1)}, f16[4,128,256]{2,1,0:T(8,128)(2,1)S(1)}, u32[]{:S(2)}, u32[]{:S(2)}) collective-permute-start(f16[4,128,256]{2,1,0:T(8,128)(2,1)S(1)} %get-tuple-element.39), channel_id=1, source_target_pairs={{0,2},{1,3},{2,0},{3,1},{4,6},{5,7},{6,4},{7,5},{8,10},{9,11},{10,... | collective-permute-start | bytes 786440 | tf_op jit(solution)/shard_map/ppermute | solution.py:297
  25.5 0.9 collective-permute-start.5
  26.4 0.6 collective-permute-start.7
  27.0 0.0 collective-permute-done.1.right_ref
  27.0 0.0 collective-permute-done.left_ref
  27.0 0.0 copy-start.5
  27.0 0.7 copy-done.5
  27.7 18.2 %shard_map.78 = (bf16[2,128,2048]{2,1,0:T(8,128)(2,1)}, bf16[2,128,2048]{2,1,0:T(8,128)(2,1)}, bf16[2,128,2048]{2,1,0:T(8,128)(2,1)}, bf16[2,128,2048]{2,1,0:T(8...) custom-call(s32[17,32]{1,0:T(8,128)S(1)} %copy-done.5, ...), custom_call_target="tpu_custom_call" | custom-call | bytes 74000000 | tf_op jit(solution)/shard_map/pallas_call | solution.py:155
  45.9 0.0 collective-permute-done.6
  46.0 0.0 collective-permute-done.5
  46.0 0.0 collective-permute-done.7
  46.0 0.3 convert_multiply_fusion
  46.3 1.8 %fusion = (bf16[16,128,256]{2,1,0:T(8,128)(2,1)}, bf16[16,128,256]{2,1,0:T(8,128)(2,1)}) fusion(f32[4,4,128,256]{3,2,1,0:T(8,128)S(1)} %convert_multiply_fusion), kind=kLoop, calls=%fused_computation.2 | loop fusion | flops 2097152 | bytes 4194304 | tf_op jit(solution)/shard_map/convert_element_type | solution.py:371
  48.2 0.0 copy-start.6
  48.2 0.0 collective-permute-start.8
  48.2 2.8 %collective-permute-start.9 = (bf16[2,128,2048]{2,1,0:T(8,128)(2,1)}, bf16[2,128,2048]{2,1,0:T(8,128)(2,1)S(1)}, u32[]{:S(2)}, u32[]{:S(2)}) collective-permute-start(bf16[2,128,2048]{2,1,0:T(8,128)(2,1)} %get-tuple-element.27.refs_1_), channel_id=1, source_target_pairs={{0,12},{1,13},{2,14},{3,15},{4,0},{5,1},{6,2},{7,3},{8,4},{9,5},{1... | collective-permute-start | bytes 3145736 | tf_op jit(solution)/shard_map/ppermute | solution.py:297
  51.0 0.0 collective-permute-start.11
  51.0 2.7 %collective-permute-start.12 = (bf16[2,128,2048]{2,1,0:T(8,128)(2,1)}, bf16[2,128,2048]{2,1,0:T(8,128)(2,1)}, u32[]{:S(2)}, u32[]{:S(2)}) collective-permute-start(bf16[2,128,2048]{2,1,0:T(8,128)(2,1)} %get-tuple-element.29.refs_3_), channel_id=1, source_target_pairs={{0,12},{1,13},{2,14},{3,15},{4,0},{5,1},{6,2},{7,3},{8,4},{9,5},{1... | collective-permute-start | bytes 3145736 | tf_op jit(solution)/shard_map/ppermute | solution.py:297
  53.7 0.0 copy-done.6
  53.7 0.0 copy-start.2
  53.7 1.2 copy-done.2
  54.9 8.2 %shard_map.80._ = f32[256,256]{1,0:T(8,128)S(1)} custom-call(s32[17,32]{1,0:T(8,128)S(1)} %copy-done.6, bf16[2,128,2048]{2,1,0:T(8,128)(2,1)S(1)} %copy-done.2, bf16[2,128,2048]{2,1,0:T(8,128)(2,1)} %get-tuple-element.27.refs_1_, bf16[2,128,2048]{2,1,0:T(8,128)(2,1)} %get-tuple-element.28.refs_2_, bf16[2,128,2048]{2,1,0:T(8,128)(2,1)} %get-tuple-element.29.refs_3_, ...), custom_call_target="tpu_custom_call" | custom-call | bytes 22200000 | tf_op jit(solution)/shard_map/pallas_call | solution.py:223
  63.1 0.0 copy-start.3
  63.1 0.0 copy-start.4
  63.1 0.5 collective-permute-done.8.from_far_a
  63.6 0.0 collective-permute-done.9.from_far_b
  63.6 0.0 copy-done
  63.6 0.0 copy-done.1
  63.6 2.3 %shard_map.81 = (bf16[2,128,2048]{2,1,0:T(8,128)(2,1)}, bf16[2,128,2048]{2,1,0:T(8,128)(2,1)}) custom-call(bf16[2,128,2048]{2,1,0:T(8,128)(2,1)S(1)} %copy-done, bf16[2,128,2048]{2,1,0:T(8,128)(2,1)S(1)} %collective-permute-done.8.from_far_a, bf16[2,128,2048]{2,1,0:T(8,128)(2,1)S(1)} %copy-done.1, ...), custom_call_target="tpu_custom_call" | custom-call | bytes 7400000 | tf_op jit(solution)/shard_map/pallas_call | solution.py:268
  65.9 0.8 collective-permute-start.10
  66.8 1.9 %collective-permute-start.13 = (bf16[2,128,2048]{2,1,0:T(8,128)(2,1)}, bf16[2,128,2048]{2,1,0:T(8,128)(2,1)}, u32[]{:S(2)}, u32[]{:S(2)}) collective-permute-start(bf16[2,128,2048]{2,1,0:T(8,128)(2,1)} %get-tuple-element.31), channel_id=1, source_target_pairs={{0,12},{1,13},{2,14},{3,15},{4,0},{5,1},{6,2},{7,3},{8,4},{9,5},{1... | collective-permute-start | bytes 3145736 | tf_op jit(solution)/shard_map/ppermute | solution.py:297
  68.6 31.6 %all_to_all.10 = f32[128,4,128]{2,1,0:T(4,128)S(1)} all-to-all(f32[128,4,128]{2,1,0:T(4,128)S(1)} %bitcast.44), channel_id=1, replica_groups=mesh['sect'=8,'rows'=16] {'sect','rows'}, dimensions={0} | all-to-all | bytes 524288 | tf_op jit(solution)/shard_map/all_to_all | solution.py:306
  100.2 0.1 reduce_sum.9._
  100.3 0.0 collective-permute-done.11.up_b
  100.3 0.0 collective-permute-done.12.down_a
  100.4 0.0 collective-permute-done.10.up_a
  100.4 0.0 collective-permute-done.13.down_b
  100.4 0.0 copy-done.3
  100.4 0.0 copy-done.4
  100.4 2.4 %shard_map.82 = (bf16[128,2048]{1,0:T(8,128)(2,1)S(1)}, bf16[128,2048]{1,0:T(8,128)(2,1)S(1)}, bf16[128,2048]{1,0:T(8,128)(2,1)S(1)}, f32[128,2048]{1,0:T(8,128)S(1)}) custom-call(bf16[2,128,2048]{2,1,0:T(8,128)(2,1)S(1)} %copy-done.3, bf16[2,128,2048]{2,1,0:T(8,128)(2,1)S(1)} %copy-done.4, bf16[2,128,2048]{2,1,0:T(8,128)(2,1)} %collective-permute-done.10.up_a, ...), custom_call_target="tpu_custom_call" | custom-call | bytes 11100000 | tf_op jit(solution)/shard_map/pallas_call | solution.py:336
  102.8 2.3 %collective-permute-start.14 = (bf16[128,2048]{1,0:T(8,128)(2,1)S(1)}, bf16[128,2048]{1,0:T(8,128)(2,1)S(1)}, u32[]{:S(2)}, u32[]{:S(2)}) collective-permute-start(bf16[128,2048]{1,0:T(8,128)(2,1)S(1)} %get-tuple-element.33), channel_id=1, source_target_pairs={{0,2},{1,3},{2,0},{3,1},{4,6},{5,7},{6,4},{7,5},{8,10},{9,11},{10,... | collective-permute-start | bytes 1572872 | tf_op jit(solution)/shard_map/ppermute | solution.py:297
  105.1 0.0 collective-permute-start.15
  105.1 2.7 %collective-permute-start.16 = (bf16[128,2048]{1,0:T(8,128)(2,1)S(1)}, bf16[128,2048]{1,0:T(8,128)(2,1)S(1)}, u32[]{:S(2)}, u32[]{:S(2)}) collective-permute-start(bf16[128,2048]{1,0:T(8,128)(2,1)S(1)} %get-tuple-element.35), channel_id=1, source_target_pairs={{0,3},{1,0},{2,1},{3,2},{4,7},{5,4},{6,5},{7,6},{8,11},{9,8},{10,9... | collective-permute-start | bytes 1572872 | tf_op jit(solution)/shard_map/ppermute | solution.py:297
  107.8 15.7 %all_to_all.11 = f32[128,4,128]{2,1,0:T(4,128)S(1)} all-to-all(f32[128,4,128]{2,1,0:T(4,128)S(1)} %broadcast_in_dim.10), channel_id=1, replica_groups=mesh['sect'=8,'rows'=16] {'sect','rows'}, dimensions={0} | all-to-all | bytes 524288 | tf_op jit(solution)/shard_map/all_to_all | solution.py:310
  123.5 0.0 collective-permute-done.14
  123.5 0.0 collective-permute-done.15
  123.5 0.0 collective-permute-done.16
  123.5 1.2 add_add_fusion
  124.8 0.7 copy.13
  (8 shorter events, 0.1 us)
Async XLA Ops:
  2.4 24.6 %collective-permute-start.1 = (bf16[17,128,128]{2,1,0:T(8,128)(2,1)S(1)}, bf16[17,128,128]{2,1,0:T(8,128)(2,1)S(1)}, u32[]{:S(2)}, u32[]{:S(2)}) collective-permute-start(bf16[17,128,128]{2,1,0:T(8,128)(2,1)S(1)} %fusion.2.own_ref), channel_id=1, source_target_pairs={{1,0},{2,1},{3,2},{4,3},{5,4},{6,5},{7,6},{8,7},{9,8},{10,9},{11,1... | collective-permute-start | bytes 1671176 | tf_op jit(solution)/shard_map/ppermute | solution.py:361
  4.6 13.3 %collective-permute-start.3 = (f16[128,256]{1,0:T(8,128)(2,1)S(1)}, f16[128,256]{1,0:T(8,128)(2,1)S(1)}, u32[]{:S(2)}, u32[]{:S(2)}) collective-permute-start(f16[128,256]{1,0:T(8,128)(2,1)S(1)} %multiply_convert_fusion), channel_id=1, source_target_pairs={{0,8},{1,9},{2,10},{3,11},{4,12},{5,13},{6,14},{7,15},{8,0},{9,1},... | collective-permute-start | bytes 196616 | tf_op jit(solution)/shard_map/ppermute | solution.py:297
  9.2 13.4 %collective-permute-start.2 = (f16[128,256]{1,0:T(8,128)(2,1)S(1)}, f16[128,256]{1,0:T(8,128)(2,1)S(1)}, u32[]{:S(2)}, u32[]{:S(2)}) collective-permute-start(f16[128,256]{1,0:T(8,128)(2,1)S(1)} %multiply_convert_fusion), channel_id=1, source_target_pairs={{0,12},{1,13},{2,14},{3,15},{4,0},{5,1},{6,2},{7,3},{8,4},{9,5},{1... | collective-permute-start | bytes 196616 | tf_op jit(solution)/shard_map/ppermute | solution.py:297
  9.8 12.8 %collective-permute-start.4 = (f16[128,256]{1,0:T(8,128)(2,1)S(1)}, f16[128,256]{1,0:T(8,128)(2,1)S(1)}, u32[]{:S(2)}, u32[]{:S(2)}) collective-permute-start(f16[128,256]{1,0:T(8,128)(2,1)S(1)} %multiply_convert_fusion), channel_id=1, source_target_pairs={{0,4},{1,5},{2,6},{3,7},{4,8},{5,9},{6,10},{7,11},{8,12},{9,13},{1... | collective-permute-start | bytes 196616 | tf_op jit(solution)/shard_map/ppermute | solution.py:297
  10.7 16.3 %collective-permute-start = (bf16[17,128,128]{2,1,0:T(8,128)(2,1)S(1)}, bf16[17,128,128]{2,1,0:T(8,128)(2,1)S(1)}, u32[]{:S(2)}, u32[]{:S(2)}) collective-permute-start(bf16[17,128,128]{2,1,0:T(8,128)(2,1)S(1)} %fusion.2.own_ref), channel_id=1, source_target_pairs={{0,1},{1,2},{2,3},{3,4},{4,5},{5,6},{6,7},{7,8},{8,9},{9,10},{10,1... | collective-permute-start | bytes 1671176 | tf_op jit(solution)/shard_map/ppermute | solution.py:361
  22.7 23.3 %collective-permute-start.6 = (f16[4,128,256]{2,1,0:T(8,128)(2,1)S(1)}, f16[4,128,256]{2,1,0:T(8,128)(2,1)S(1)}, u32[]{:S(2)}, u32[]{:S(2)}) collective-permute-start(f16[4,128,256]{2,1,0:T(8,128)(2,1)S(1)} %get-tuple-element.39), channel_id=1, source_target_pairs={{0,2},{1,3},{2,0},{3,1},{4,6},{5,7},{6,4},{7,5},{8,10},{9,11},{10,... | collective-permute-start | bytes 786440 | tf_op jit(solution)/shard_map/ppermute | solution.py:297
  25.5 20.4 %collective-permute-start.5 = (f16[4,128,256]{2,1,0:T(8,128)(2,1)S(1)}, f16[4,128,256]{2,1,0:T(8,128)(2,1)S(1)}, u32[]{:S(2)}, u32[]{:S(2)}) collective-permute-start(f16[4,128,256]{2,1,0:T(8,128)(2,1)S(1)} %get-tuple-element.39), channel_id=1, source_target_pairs={{0,3},{1,0},{2,1},{3,2},{4,7},{5,4},{6,5},{7,6},{8,11},{9,8},{10,9... | collective-permute-start | bytes 786440 | tf_op jit(solution)/shard_map/ppermute | solution.py:297
  26.4 19.6 %collective-permute-start.7 = (f16[4,128,256]{2,1,0:T(8,128)(2,1)S(1)}, f16[4,128,256]{2,1,0:T(8,128)(2,1)S(1)}, u32[]{:S(2)}, u32[]{:S(2)}) collective-permute-start(f16[4,128,256]{2,1,0:T(8,128)(2,1)S(1)} %get-tuple-element.39), channel_id=1, source_target_pairs={{0,1},{1,2},{2,3},{3,0},{4,5},{5,6},{6,7},{7,4},{8,9},{9,10},{10,1... | collective-permute-start | bytes 786440 | tf_op jit(solution)/shard_map/ppermute | solution.py:297
  27.0 0.7 copy-start.5
  48.2 5.5 %copy-start.6 = (s32[17,32]{1,0:T(8,128)S(1)}, s32[17,32]{1,0:T(8,128)}, u32[]{:S(2)}) copy-start(s32[17,32]{1,0:T(8,128)} %shard_map.77.table) | copy-start | bytes 6532
  48.2 15.4 %collective-permute-start.8 = (bf16[2,128,2048]{2,1,0:T(8,128)(2,1)}, bf16[2,128,2048]{2,1,0:T(8,128)(2,1)S(1)}, u32[]{:S(2)}, u32[]{:S(2)}) collective-permute-start(bf16[2,128,2048]{2,1,0:T(8,128)(2,1)} %get-tuple-element.25.refs_0_), channel_id=1, source_target_pairs={{0,4},{1,5},{2,6},{3,7},{4,8},{5,9},{6,10},{7,11},{8,12},{9,13},{1... | collective-permute-start | bytes 3145736 | tf_op jit(solution)/shard_map/ppermute | solution.py:297
  48.2 15.4 %collective-permute-start.9 = (bf16[2,128,2048]{2,1,0:T(8,128)(2,1)}, bf16[2,128,2048]{2,1,0:T(8,128)(2,1)S(1)}, u32[]{:S(2)}, u32[]{:S(2)}) collective-permute-start(bf16[2,128,2048]{2,1,0:T(8,128)(2,1)} %get-tuple-element.27.refs_1_), channel_id=1, source_target_pairs={{0,12},{1,13},{2,14},{3,15},{4,0},{5,1},{6,2},{7,3},{8,4},{9,5},{1... | collective-permute-start | bytes 3145736 | tf_op jit(solution)/shard_map/ppermute | solution.py:297
  51.0 49.4 %collective-permute-start.11 = (bf16[2,128,2048]{2,1,0:T(8,128)(2,1)}, bf16[2,128,2048]{2,1,0:T(8,128)(2,1)S(1)}, u32[]{:S(2)}, u32[]{:S(2)}) collective-permute-start(bf16[2,128,2048]{2,1,0:T(8,128)(2,1)} %get-tuple-element.28.refs_2_), channel_id=1, source_target_pairs={{0,4},{1,5},{2,6},{3,7},{4,8},{5,9},{6,10},{7,11},{8,12},{9,13},{1... | collective-permute-start | bytes 3145736 | tf_op jit(solution)/shard_map/ppermute | solution.py:297
  51.0 49.4 %collective-permute-start.12 = (bf16[2,128,2048]{2,1,0:T(8,128)(2,1)}, bf16[2,128,2048]{2,1,0:T(8,128)(2,1)}, u32[]{:S(2)}, u32[]{:S(2)}) collective-permute-start(bf16[2,128,2048]{2,1,0:T(8,128)(2,1)} %get-tuple-element.29.refs_3_), channel_id=1, source_target_pairs={{0,12},{1,13},{2,14},{3,15},{4,0},{5,1},{6,2},{7,3},{8,4},{9,5},{1... | collective-permute-start | bytes 3145736 | tf_op jit(solution)/shard_map/ppermute | solution.py:297
  53.7 1.2 copy-start.2
  54.9 8.7 %copy-start = (bf16[2,128,2048]{2,1,0:T(8,128)(2,1)S(1)}, bf16[2,128,2048]{2,1,0:T(8,128)(2,1)}, u32[]{:S(2)}) copy-start(bf16[2,128,2048]{2,1,0:T(8,128)(2,1)} %get-tuple-element.21.refs_4_.up) | copy-start | bytes 3145732
  54.9 8.7 %copy-start.1 = (bf16[2,128,2048]{2,1,0:T(8,128)(2,1)S(1)}, bf16[2,128,2048]{2,1,0:T(8,128)(2,1)}, u32[]{:S(2)}) copy-start(bf16[2,128,2048]{2,1,0:T(8,128)(2,1)} %get-tuple-element.26.refs_5_.down) | copy-start | bytes 3145732
  63.1 37.3 %copy-start.3 = (bf16[2,128,2048]{2,1,0:T(8,128)(2,1)S(1)}, bf16[2,128,2048]{2,1,0:T(8,128)(2,1)}, u32[]{:S(2)}) copy-start(bf16[2,128,2048]{2,1,0:T(8,128)(2,1)} %get-tuple-element.19.refs_6_.own_a) | copy-start | bytes 3145732
  63.1 37.3 %copy-start.4 = (bf16[2,128,2048]{2,1,0:T(8,128)(2,1)S(1)}, bf16[2,128,2048]{2,1,0:T(8,128)(2,1)}, u32[]{:S(2)}) copy-start(bf16[2,128,2048]{2,1,0:T(8,128)(2,1)} %get-tuple-element.20.refs_7_.own_b) | copy-start | bytes 3145732
  65.9 34.5 %collective-permute-start.10 = (bf16[2,128,2048]{2,1,0:T(8,128)(2,1)}, bf16[2,128,2048]{2,1,0:T(8,128)(2,1)}, u32[]{:S(2)}, u32[]{:S(2)}) collective-permute-start(bf16[2,128,2048]{2,1,0:T(8,128)(2,1)} %get-tuple-element.30), channel_id=1, source_target_pairs={{0,4},{1,5},{2,6},{3,7},{4,8},{5,9},{6,10},{7,11},{8,12},{9,13},{1... | collective-permute-start | bytes 3145736 | tf_op jit(solution)/shard_map/ppermute | solution.py:297
  66.8 33.6 %collective-permute-start.13 = (bf16[2,128,2048]{2,1,0:T(8,128)(2,1)}, bf16[2,128,2048]{2,1,0:T(8,128)(2,1)}, u32[]{:S(2)}, u32[]{:S(2)}) collective-permute-start(bf16[2,128,2048]{2,1,0:T(8,128)(2,1)} %get-tuple-element.31), channel_id=1, source_target_pairs={{0,12},{1,13},{2,14},{3,15},{4,0},{5,1},{6,2},{7,3},{8,4},{9,5},{1... | collective-permute-start | bytes 3145736 | tf_op jit(solution)/shard_map/ppermute | solution.py:297
  102.8 20.7 %collective-permute-start.14 = (bf16[128,2048]{1,0:T(8,128)(2,1)S(1)}, bf16[128,2048]{1,0:T(8,128)(2,1)S(1)}, u32[]{:S(2)}, u32[]{:S(2)}) collective-permute-start(bf16[128,2048]{1,0:T(8,128)(2,1)S(1)} %get-tuple-element.33), channel_id=1, source_target_pairs={{0,2},{1,3},{2,0},{3,1},{4,6},{5,7},{6,4},{7,5},{8,10},{9,11},{10,... | collective-permute-start | bytes 1572872 | tf_op jit(solution)/shard_map/ppermute | solution.py:297
  105.1 18.5 %collective-permute-start.15 = (bf16[128,2048]{1,0:T(8,128)(2,1)S(1)}, bf16[128,2048]{1,0:T(8,128)(2,1)S(1)}, u32[]{:S(2)}, u32[]{:S(2)}) collective-permute-start(bf16[128,2048]{1,0:T(8,128)(2,1)S(1)} %get-tuple-element.34), channel_id=1, source_target_pairs={{0,1},{1,2},{2,3},{3,0},{4,5},{5,6},{6,7},{7,4},{8,9},{9,10},{10,1... | collective-permute-start | bytes 1572872 | tf_op jit(solution)/shard_map/ppermute | solution.py:297
  105.1 18.5 %collective-permute-start.16 = (bf16[128,2048]{1,0:T(8,128)(2,1)S(1)}, bf16[128,2048]{1,0:T(8,128)(2,1)S(1)}, u32[]{:S(2)}, u32[]{:S(2)}) collective-permute-start(bf16[128,2048]{1,0:T(8,128)(2,1)S(1)} %get-tuple-element.35), channel_id=1, source_target_pairs={{0,3},{1,0},{2,1},{3,2},{4,7},{5,4},{6,5},{7,6},{8,11},{9,8},{10,9... | collective-permute-start | bytes 1572872 | tf_op jit(solution)/shard_map/ppermute | solution.py:297

commit v6 on v5

--- a/solution.py
+++ b/solution.py
@@ -11,7 +11,6 @@
 TILE = 128
 RB = 16
 KA = 27
-GROUP = 2
 AHEAD = 3
 CUTS = 3
 SIDE = 4
@@ -110,16 +109,24 @@
         slot = lax.rem(r, AHEAD + 1)
         count = table[i, COUNT]
         left = tiles[RB + i].T
-        for k in range(0, KA, GROUP):
-            products, places = [], []
-            for s in range(k, min(k + GROUP, KA)):
+        blank = jnp.zeros((TILE, TILE), jnp.bfloat16)
+        for k in range(0, KA, 2):
+            slots = range(k, min(k + 2, KA))
+            rights, places = [], []
+            for s in slots:
                 col = jnp.clip(table[i, s], 0, 3 * RB - 1)
                 block = jnp.clip(maps[lax.shift_right_logical(col, 4), lax.bitwise_and(col, RB - 1)], 0, CBS - 1)
                 places.append(pl.multiple_of(jnp.where(s < count, block, CBS) * TILE, TILE))
-                products.append(
-                    jnp.dot(a_buf[slot, s], tiles[col], preferred_element_type=jnp.float32).astype(jnp.bfloat16)
-                )
-            terms = jnp.dot(left, jnp.concatenate(products, axis=1) if len(products) > 1 else products[0], preferred_element_type=jnp.float32)
+                rights.append(tiles[col])
+            if len(rights) == 2:
+                fine = jnp.concatenate([a_buf[slot, s] for s in slots], axis=1)
+                coarse = jnp.concatenate([
+                    jnp.concatenate([rights[0], blank], axis=1), jnp.concatenate([blank, rights[1]], axis=1)
+                ], axis=0)
+            else:
+                fine, coarse = a_buf[slot, k], rights[0]
+            products = jnp.dot(fine, coarse, preferred_element_type=jnp.float32).astype(jnp.bfloat16)
+            terms = jnp.dot(left, products, preferred_element_type=jnp.float32)
             for n, place in enumerate(places):
                 acc[:, pl.ds(place, TILE)] += terms[:, n * TILE:(n + 1) * TILE]
         return 0
@@ -245,16 +252,16 @@
     )(table, *parts, high, low)
 
 
-def held_back(first, second, after_this):
+def held_back(value, after_this):
     anywhere = pl.BlockSpec(memory_space=pl.ANY)
     return pl.pallas_call(
         lambda *refs: None,
-        out_shape=[jax.ShapeDtypeStruct(value.shape, value.dtype) for value in (first, second)],
-        in_specs=[anywhere] * 3,
-        out_specs=[anywhere] * 2,
-        input_output_aliases={0: 0, 1: 1},
+        out_shape=jax.ShapeDtypeStruct(value.shape, value.dtype),
+        in_specs=[anywhere] * 2,
+        out_specs=anywhere,
+        input_output_aliases={0: 0},
         cost_estimate=cost(1),
-    )(first, second, after_this)
+    )(value, after_this)
 
 
 def joined_body(up, from_far_a, down, from_far_b, _, up_out, down_out):
@@ -370,7 +377,7 @@
     prolong_high = lax.reduce_precision(prolong, 8, 7)
     prolong_low = (prolong - prolong_high).astype(jnp.bfloat16)
     prolong_high = prolong_high.astype(jnp.bfloat16)
-    far_a, far_b = held_back(far_a, far_b, prolong_high)
+    far_a = held_back(far_a, prolong_high)
     parts = (far_a, far_b, up_b, down_a, up_a, down_b, own_a, own_b)
     from_far_a, from_far_b = send(far_a, 0, 1), send(far_b, 0, -1)
     from_up_b, from_down_a = send(up_b, 0, 1), send(down_a, 0, -1)

time: 126 us -> 128 us (1.016)
  Pallas kernels: 33.9 us -> 36.7 us
    pallas_call x1, Pallas kernels: 18.2 us -> 21 us  [galerkin(): pl.pallas_call(galerkin_body, out_shape=[jax.ShapeDtypeStruct((2, TILE, W...]
  transfers between devices with their start and end apart: 17 -> 17, of which waited for: 2 -> 2; matrix products, arithmetic and copies ran while one was open for 2% -> 2% of each run, Pallas kernels for 25% -> 27%
where the time goes in v6:
time: 128 us
  blocking collectives  47.2 us (37%)
  Pallas kernels  36.7 us (29%)
  starting transfers between devices  27.7 us (22%)
  other arithmetic  7.27 us (6%)
  waiting for transfers between devices  5.34 us (4%)
  local copies, waits for them, and re-layouts  3.33 us (3%)
    all_to_all x1, blocking collectives, share_out(): return jnp.sum(lax.all_to_all(pieces, ('sect', 'rows'), 0, 0), axis=0)  30.7 us
    ppermute x15, starting transfers between devices, send(): return lax.ppermute(value, ('sect', 'rows'), STEPS[second][by])  23.8 us
    pallas_call x1, Pallas kernels, galerkin(): pl.pallas_call(galerkin_body, out_shape=[jax.ShapeDtypeStruct((2, TILE, W...  21 us
    all_to_all x1, blocking collectives, bring_back(): lax.all_to_all(jnp.broadcast_to(piece[None], (128,) + piece.shape), ('sec...  16.4 us
    pallas_call x1, Pallas kernels, coarsest_term(): pl.pallas_call(coarsest_body, out_shape=jax.ShapeDtypeStruct((C2, C2), jn...  8.14 us
    ppermute x15, waiting for transfers between devices, send(): return lax.ppermute(value, ('sect', 'rows'), STEPS[second][by])  5.34 us
    pallas_call x1, Pallas kernels, row_plan(): pl.pallas_call(plan_body, out_shape=jax.ShapeDtypeStruct((RB + 1, 32), jn...  2.91 us
    unnamed x15, local copies, waits for them, and re-layouts  2.65 us
  transfers between devices with their start and end apart: 17, of which 2 were waited for; matrix products, arithmetic and copies ran while one was open for 2% of the time, Pallas kernels for 27%

profile of v6, /device:TPU:1, one launch (start us, length us, event | category | flops | bytes accessed | tf_op | source)
XLA Modules:
  0.0 128.3 jit_solution(12236690072543982119)
XLA Ops:
  0.6 0.7 subtract_bitcast_fusion
  1.3 1.1 fusion.2.own_ref
  2.4 1.3 %collective-permute-start.1 = (bf16[17,128,128]{2,1,0:T(8,128)(2,1)S(1)}, bf16[17,128,128]{2,1,0:T(8,128)(2,1)S(1)}, u32[]{:S(2)}, u32[]{:S(2)}) collective-permute-start(bf16[17,128,128]{2,1,0:T(8,128)(2,1)S(1)} %fusion.2.own_ref), channel_id=1, source_target_pairs={{1,0},{2,1},{3,2},{4,3},{5,4},{6,5},{7,6},{8,7},{9,8},{10,9},{11,1... | collective-permute-start | bytes 1671176 | tf_op jit(solution)/shard_map/ppermute | solution.py:368
  3.7 0.9 multiply_convert_fusion
  4.6 4.6 %collective-permute-start.3 = (f16[128,256]{1,0:T(8,128)(2,1)S(1)}, f16[128,256]{1,0:T(8,128)(2,1)S(1)}, u32[]{:S(2)}, u32[]{:S(2)}) collective-permute-start(f16[128,256]{1,0:T(8,128)(2,1)S(1)} %multiply_convert_fusion), channel_id=1, source_target_pairs={{0,8},{1,9},{2,10},{3,11},{4,12},{5,13},{6,14},{7,15},{8,0},{9,1},... | collective-permute-start | bytes 196616 | tf_op jit(solution)/shard_map/ppermute | solution.py:304
  9.2 0.6 collective-permute-start.2
  9.8 0.8 collective-permute-start.4
  10.7 2.6 %collective-permute-start = (bf16[17,128,128]{2,1,0:T(8,128)(2,1)S(1)}, bf16[17,128,128]{2,1,0:T(8,128)(2,1)S(1)}, u32[]{:S(2)}, u32[]{:S(2)}) collective-permute-start(bf16[17,128,128]{2,1,0:T(8,128)(2,1)S(1)} %fusion.2.own_ref), channel_id=1, source_target_pairs={{0,1},{1,2},{2,3},{3,4},{4,5},{5,6},{6,7},{7,8},{8,9},{9,10},{10,1... | collective-permute-start | bytes 1671176 | tf_op jit(solution)/shard_map/ppermute | solution.py:368
  13.3 0.9 fusion.6
  14.3 0.6 stack.61.info
  14.9 2.9 %shard_map.77.table = s32[17,32]{1,0:T(8,128)} custom-call(s32[16,27]{1,0:T(8,128)} %cols.1, s32[16]{0:T(128)} %counts.1, s32[16]{0:T(128)} %own_map.1, s32[8]{0:T(128)} %stack.61.info), custom_call_target="tpu_custom_call" | custom-call | bytes 11100000 | tf_op jit(solution)/shard_map/pallas_call | solution.py:64
  17.8 0.0 collective-permute-done.3
  17.8 4.8 %collective-permute-done.2 = f16[128,256]{1,0:T(8,128)(2,1)S(1)} collective-permute-done((f16[128,256]{1,0:T(8,128)(2,1)S(1)}, f16[128,256]{1,0:T(8,128)(2,1)S(1)}, u32[]{:S(2)}, u32[]{:S(2)}) %collective-permute-start.2) | collective-permute-done | bytes 65568 | tf_op jit(solution)/shard_map/ppermute | solution.py:304
  22.6 0.0 collective-permute-done.4
  22.6 0.1 fusion.5
  22.7 2.8 %collective-permute-start.6 = (f16[4,128,256]{2,1,0:T(8,128)(2,1)S(1)}, f16[4,128,256]{2,1,0:T(8,128)(2,1)S(1)}, u32[]{:S(2)}, u32[]{:S(2)}) collective-permute-start(f16[4,128,256]{2,1,0:T(8,128)(2,1)S(1)} %get-tuple-element.35), channel_id=1, source_target_pairs={{0,2},{1,3},{2,0},{3,1},{4,6},{5,7},{6,4},{7,5},{8,10},{9,11},{10,... | collective-permute-start | bytes 786440 | tf_op jit(solution)/shard_map/ppermute | solution.py:304
  25.5 0.9 collective-permute-start.5
  26.4 0.6 collective-permute-start.7
  27.0 0.0 collective-permute-done.1.right_ref
  27.0 0.0 collective-permute-done.left_ref
  27.0 0.0 copy-start.5
  27.0 0.7 copy-done.5
  27.7 21.0 %shard_map.78 = (bf16[2,128,2048]{2,1,0:T(8,128)(2,1)}, bf16[2,128,2048]{2,1,0:T(8,128)(2,1)}, bf16[2,128,2048]{2,1,0:T(8,128)(2,1)}, bf16[2,128,2048]{2,1,0:T(8...) custom-call(s32[17,32]{1,0:T(8,128)S(1)} %copy-done.5, ...), custom_call_target="tpu_custom_call" | custom-call | bytes 74000000 | tf_op jit(solution)/shard_map/pallas_call | solution.py:162
  48.7 0.0 collective-permute-done.6
  48.7 0.0 collective-permute-done.5
  48.7 0.0 collective-permute-done.7
  48.7 0.3 convert_multiply_fusion
  49.1 1.8 %fusion = (bf16[16,128,256]{2,1,0:T(8,128)(2,1)}, bf16[16,128,256]{2,1,0:T(8,128)(2,1)}) fusion(f32[4,4,128,256]{3,2,1,0:T(8,128)S(1)} %convert_multiply_fusion), kind=kLoop, calls=%fused_computation.2 | loop fusion | flops 2097152 | bytes 4194304 | tf_op jit(solution)/shard_map/convert_element_type | solution.py:378
  50.9 0.0 copy-start.6
  51.0 0.0 collective-permute-start.8
  51.0 3.6 %collective-permute-start.9 = (bf16[2,128,2048]{2,1,0:T(8,128)(2,1)}, bf16[2,128,2048]{2,1,0:T(8,128)(2,1)S(1)}, u32[]{:S(2)}, u32[]{:S(2)}) collective-permute-start(bf16[2,128,2048]{2,1,0:T(8,128)(2,1)} %get-tuple-element.23.refs_1_), channel_id=1, source_target_pairs={{0,12},{1,13},{2,14},{3,15},{4,0},{5,1},{6,2},{7,3},{8,4},{9,5},{1... | collective-permute-start | bytes 3145736 | tf_op jit(solution)/shard_map/ppermute | solution.py:304
  54.6 0.0 collective-permute-start.11
  54.6 2.7 %collective-permute-start.12 = (bf16[2,128,2048]{2,1,0:T(8,128)(2,1)}, bf16[2,128,2048]{2,1,0:T(8,128)(2,1)}, u32[]{:S(2)}, u32[]{:S(2)}) collective-permute-start(bf16[2,128,2048]{2,1,0:T(8,128)(2,1)} %get-tuple-element.25.refs_3_), channel_id=1, source_target_pairs={{0,12},{1,13},{2,14},{3,15},{4,0},{5,1},{6,2},{7,3},{8,4},{9,5},{1... | collective-permute-start | bytes 3145736 | tf_op jit(solution)/shard_map/ppermute | solution.py:304
  57.2 0.0 copy-done.6
  57.2 0.0 copy-start.2
  57.2 1.2 copy-done.2
  58.5 8.1 %shard_map.80._ = f32[256,256]{1,0:T(8,128)S(1)} custom-call(s32[17,32]{1,0:T(8,128)S(1)} %copy-done.6, bf16[2,128,2048]{2,1,0:T(8,128)(2,1)S(1)} %copy-done.2, bf16[2,128,2048]{2,1,0:T(8,128)(2,1)} %get-tuple-element.23.refs_1_, bf16[2,128,2048]{2,1,0:T(8,128)(2,1)} %get-tuple-element.24.refs_2_, bf16[2,128,2048]{2,1,0:T(8,128)(2,1)} %get-tuple-element.25.refs_3_, ...), custom_call_target="tpu_custom_call" | custom-call | bytes 22200000 | tf_op jit(solution)/shard_map/pallas_call | solution.py:230
  66.6 0.0 copy-start.3
  66.6 0.0 copy-start.4
  66.6 0.5 collective-permute-done.8.from_far_a
  67.2 0.0 collective-permute-done.9.from_far_b
  67.2 0.0 copy-done
  67.2 0.0 copy-done.1
  67.2 2.3 %shard_map.81 = (bf16[2,128,2048]{2,1,0:T(8,128)(2,1)}, bf16[2,128,2048]{2,1,0:T(8,128)(2,1)}) custom-call(bf16[2,128,2048]{2,1,0:T(8,128)(2,1)S(1)} %copy-done, bf16[2,128,2048]{2,1,0:T(8,128)(2,1)S(1)} %collective-permute-done.8.from_far_a, bf16[2,128,2048]{2,1,0:T(8,128)(2,1)S(1)} %copy-done.1, ...), custom_call_target="tpu_custom_call" | custom-call | bytes 7400000 | tf_op jit(solution)/shard_map/pallas_call | solution.py:275
  69.5 0.8 collective-permute-start.10
  70.4 1.9 %collective-permute-start.13 = (bf16[2,128,2048]{2,1,0:T(8,128)(2,1)}, bf16[2,128,2048]{2,1,0:T(8,128)(2,1)}, u32[]{:S(2)}, u32[]{:S(2)}) collective-permute-start(bf16[2,128,2048]{2,1,0:T(8,128)(2,1)} %get-tuple-element.27), channel_id=1, source_target_pairs={{0,12},{1,13},{2,14},{3,15},{4,0},{5,1},{6,2},{7,3},{8,4},{9,5},{1... | collective-permute-start | bytes 3145736 | tf_op jit(solution)/shard_map/ppermute | solution.py:304
  72.2 30.7 %all_to_all.10 = f32[128,4,128]{2,1,0:T(4,128)S(1)} all-to-all(f32[128,4,128]{2,1,0:T(4,128)S(1)} %bitcast.44), channel_id=1, replica_groups=mesh['sect'=8,'rows'=16] {'sect','rows'}, dimensions={0} | all-to-all | bytes 524288 | tf_op jit(solution)/shard_map/all_to_all | solution.py:313
  103.0 0.1 reduce_sum.9._
  103.1 0.0 collective-permute-done.11.up_b
  103.1 0.0 collective-permute-done.12.down_a
  103.1 0.0 collective-permute-done.10.up_a
  103.1 0.0 collective-permute-done.13.down_b
  103.1 0.0 copy-done.3
  103.2 0.0 copy-done.4
  103.2 2.4 %shard_map.82 = (bf16[128,2048]{1,0:T(8,128)(2,1)S(1)}, bf16[128,2048]{1,0:T(8,128)(2,1)S(1)}, bf16[128,2048]{1,0:T(8,128)(2,1)S(1)}, f32[128,2048]{1,0:T(8,128)S(1)}) custom-call(bf16[2,128,2048]{2,1,0:T(8,128)(2,1)S(1)} %copy-done.3, bf16[2,128,2048]{2,1,0:T(8,128)(2,1)S(1)} %copy-done.4, bf16[2,128,2048]{2,1,0:T(8,128)(2,1)} %collective-permute-done.10.up_a, ...), custom_call_target="tpu_custom_call" | custom-call | bytes 11100000 | tf_op jit(solution)/shard_map/pallas_call | solution.py:343
  105.5 1.7 %collective-permute-start.14 = (bf16[128,2048]{1,0:T(8,128)(2,1)S(1)}, bf16[128,2048]{1,0:T(8,128)(2,1)S(1)}, u32[]{:S(2)}, u32[]{:S(2)}) collective-permute-start(bf16[128,2048]{1,0:T(8,128)(2,1)S(1)} %get-tuple-element.29), channel_id=1, source_target_pairs={{0,2},{1,3},{2,0},{3,1},{4,6},{5,7},{6,4},{7,5},{8,10},{9,11},{10,... | collective-permute-start | bytes 1572872 | tf_op jit(solution)/shard_map/ppermute | solution.py:304
  107.2 1.3 collective-permute-start.15
  108.5 1.4 %collective-permute-start.16 = (bf16[128,2048]{1,0:T(8,128)(2,1)S(1)}, bf16[128,2048]{1,0:T(8,128)(2,1)S(1)}, u32[]{:S(2)}, u32[]{:S(2)}) collective-permute-start(bf16[128,2048]{1,0:T(8,128)(2,1)S(1)} %get-tuple-element.31), channel_id=1, source_target_pairs={{0,3},{1,0},{2,1},{3,2},{4,7},{5,4},{6,5},{7,6},{8,11},{9,8},{10,9... | collective-permute-start | bytes 1572872 | tf_op jit(solution)/shard_map/ppermute | solution.py:304
  109.9 16.4 %all_to_all.11 = f32[128,4,128]{2,1,0:T(4,128)S(1)} all-to-all(f32[128,4,128]{2,1,0:T(4,128)S(1)} %broadcast_in_dim.10), channel_id=1, replica_groups=mesh['sect'=8,'rows'=16] {'sect','rows'}, dimensions={0} | all-to-all | bytes 524288 | tf_op jit(solution)/shard_map/all_to_all | solution.py:317
  126.4 0.0 collective-permute-done.14
  126.4 0.0 collective-permute-done.15
  126.4 0.0 collective-permute-done.16
  126.4 1.2 add_add_fusion
  127.6 0.7 copy.11
  (8 shorter events, 0.1 us)
Async XLA Ops:
  2.4 24.6 %collective-permute-start.1 = (bf16[17,128,128]{2,1,0:T(8,128)(2,1)S(1)}, bf16[17,128,128]{2,1,0:T(8,128)(2,1)S(1)}, u32[]{:S(2)}, u32[]{:S(2)}) collective-permute-start(bf16[17,128,128]{2,1,0:T(8,128)(2,1)S(1)} %fusion.2.own_ref), channel_id=1, source_target_pairs={{1,0},{2,1},{3,2},{4,3},{5,4},{6,5},{7,6},{8,7},{9,8},{10,9},{11,1... | collective-permute-start | bytes 1671176 | tf_op jit(solution)/shard_map/ppermute | solution.py:368
  4.6 13.2 %collective-permute-start.3 = (f16[128,256]{1,0:T(8,128)(2,1)S(1)}, f16[128,256]{1,0:T(8,128)(2,1)S(1)}, u32[]{:S(2)}, u32[]{:S(2)}) collective-permute-start(f16[128,256]{1,0:T(8,128)(2,1)S(1)} %multiply_convert_fusion), channel_id=1, source_target_pairs={{0,8},{1,9},{2,10},{3,11},{4,12},{5,13},{6,14},{7,15},{8,0},{9,1},... | collective-permute-start | bytes 196616 | tf_op jit(solution)/shard_map/ppermute | solution.py:304
  9.2 13.4 %collective-permute-start.2 = (f16[128,256]{1,0:T(8,128)(2,1)S(1)}, f16[128,256]{1,0:T(8,128)(2,1)S(1)}, u32[]{:S(2)}, u32[]{:S(2)}) collective-permute-start(f16[128,256]{1,0:T(8,128)(2,1)S(1)} %multiply_convert_fusion), channel_id=1, source_target_pairs={{0,12},{1,13},{2,14},{3,15},{4,0},{5,1},{6,2},{7,3},{8,4},{9,5},{1... | collective-permute-start | bytes 196616 | tf_op jit(solution)/shard_map/ppermute | solution.py:304
  9.8 12.8 %collective-permute-start.4 = (f16[128,256]{1,0:T(8,128)(2,1)S(1)}, f16[128,256]{1,0:T(8,128)(2,1)S(1)}, u32[]{:S(2)}, u32[]{:S(2)}) collective-permute-start(f16[128,256]{1,0:T(8,128)(2,1)S(1)} %multiply_convert_fusion), channel_id=1, source_target_pairs={{0,4},{1,5},{2,6},{3,7},{4,8},{5,9},{6,10},{7,11},{8,12},{9,13},{1... | collective-permute-start | bytes 196616 | tf_op jit(solution)/shard_map/ppermute | solution.py:304
  10.7 16.3 %collective-permute-start = (bf16[17,128,128]{2,1,0:T(8,128)(2,1)S(1)}, bf16[17,128,128]{2,1,0:T(8,128)(2,1)S(1)}, u32[]{:S(2)}, u32[]{:S(2)}) collective-permute-start(bf16[17,128,128]{2,1,0:T(8,128)(2,1)S(1)} %fusion.2.own_ref), channel_id=1, source_target_pairs={{0,1},{1,2},{2,3},{3,4},{4,5},{5,6},{6,7},{7,8},{8,9},{9,10},{10,1... | collective-permute-start | bytes 1671176 | tf_op jit(solution)/shard_map/ppermute | solution.py:368
  22.7 26.0 %collective-permute-start.6 = (f16[4,128,256]{2,1,0:T(8,128)(2,1)S(1)}, f16[4,128,256]{2,1,0:T(8,128)(2,1)S(1)}, u32[]{:S(2)}, u32[]{:S(2)}) collective-permute-start(f16[4,128,256]{2,1,0:T(8,128)(2,1)S(1)} %get-tuple-element.35), channel_id=1, source_target_pairs={{0,2},{1,3},{2,0},{3,1},{4,6},{5,7},{6,4},{7,5},{8,10},{9,11},{10,... | collective-permute-start | bytes 786440 | tf_op jit(solution)/shard_map/ppermute | solution.py:304
  25.5 23.2 %collective-permute-start.5 = (f16[4,128,256]{2,1,0:T(8,128)(2,1)S(1)}, f16[4,128,256]{2,1,0:T(8,128)(2,1)S(1)}, u32[]{:S(2)}, u32[]{:S(2)}) collective-permute-start(f16[4,128,256]{2,1,0:T(8,128)(2,1)S(1)} %get-tuple-element.35), channel_id=1, source_target_pairs={{0,3},{1,0},{2,1},{3,2},{4,7},{5,4},{6,5},{7,6},{8,11},{9,8},{10,9... | collective-permute-start | bytes 786440 | tf_op jit(solution)/shard_map/ppermute | solution.py:304
  26.4 22.4 %collective-permute-start.7 = (f16[4,128,256]{2,1,0:T(8,128)(2,1)S(1)}, f16[4,128,256]{2,1,0:T(8,128)(2,1)S(1)}, u32[]{:S(2)}, u32[]{:S(2)}) collective-permute-start(f16[4,128,256]{2,1,0:T(8,128)(2,1)S(1)} %get-tuple-element.35), channel_id=1, source_target_pairs={{0,1},{1,2},{2,3},{3,0},{4,5},{5,6},{6,7},{7,4},{8,9},{9,10},{10,1... | collective-permute-start | bytes 786440 | tf_op jit(solution)/shard_map/ppermute | solution.py:304
  27.0 0.7 copy-start.5
  50.9 6.3 %copy-start.6 = (s32[17,32]{1,0:T(8,128)S(1)}, s32[17,32]{1,0:T(8,128)}, u32[]{:S(2)}) copy-start(s32[17,32]{1,0:T(8,128)} %shard_map.77.table) | copy-start | bytes 6532
  51.0 16.2 %collective-permute-start.8 = (bf16[2,128,2048]{2,1,0:T(8,128)(2,1)}, bf16[2,128,2048]{2,1,0:T(8,128)(2,1)S(1)}, u32[]{:S(2)}, u32[]{:S(2)}) collective-permute-start(bf16[2,128,2048]{2,1,0:T(8,128)(2,1)} %shard_map.79.refs_0_), channel_id=1, source_target_pairs={{0,4},{1,5},{2,6},{3,7},{4,8},{5,9},{6,10},{7,11},{8,12},{9,13},{1... | collective-permute-start | bytes 3145736 | tf_op jit(solution)/shard_map/ppermute | solution.py:304
  51.0 16.2 %collective-permute-start.9 = (bf16[2,128,2048]{2,1,0:T(8,128)(2,1)}, bf16[2,128,2048]{2,1,0:T(8,128)(2,1)S(1)}, u32[]{:S(2)}, u32[]{:S(2)}) collective-permute-start(bf16[2,128,2048]{2,1,0:T(8,128)(2,1)} %get-tuple-element.23.refs_1_), channel_id=1, source_target_pairs={{0,12},{1,13},{2,14},{3,15},{4,0},{5,1},{6,2},{7,3},{8,4},{9,5},{1... | collective-permute-start | bytes 3145736 | tf_op jit(solution)/shard_map/ppermute | solution.py:304
  54.6 48.6 %collective-permute-start.11 = (bf16[2,128,2048]{2,1,0:T(8,128)(2,1)}, bf16[2,128,2048]{2,1,0:T(8,128)(2,1)S(1)}, u32[]{:S(2)}, u32[]{:S(2)}) collective-permute-start(bf16[2,128,2048]{2,1,0:T(8,128)(2,1)} %get-tuple-element.24.refs_2_), channel_id=1, source_target_pairs={{0,4},{1,5},{2,6},{3,7},{4,8},{5,9},{6,10},{7,11},{8,12},{9,13},{1... | collective-permute-start | bytes 3145736 | tf_op jit(solution)/shard_map/ppermute | solution.py:304
  54.6 48.6 %collective-permute-start.12 = (bf16[2,128,2048]{2,1,0:T(8,128)(2,1)}, bf16[2,128,2048]{2,1,0:T(8,128)(2,1)}, u32[]{:S(2)}, u32[]{:S(2)}) collective-permute-start(bf16[2,128,2048]{2,1,0:T(8,128)(2,1)} %get-tuple-element.25.refs_3_), channel_id=1, source_target_pairs={{0,12},{1,13},{2,14},{3,15},{4,0},{5,1},{6,2},{7,3},{8,4},{9,5},{1... | collective-permute-start | bytes 3145736 | tf_op jit(solution)/shard_map/ppermute | solution.py:304
  57.2 1.2 copy-start.2
  58.5 8.7 %copy-start = (bf16[2,128,2048]{2,1,0:T(8,128)(2,1)S(1)}, bf16[2,128,2048]{2,1,0:T(8,128)(2,1)}, u32[]{:S(2)}) copy-start(bf16[2,128,2048]{2,1,0:T(8,128)(2,1)} %get-tuple-element.19.refs_4_.up) | copy-start | bytes 3145732
  58.5 8.7 %copy-start.1 = (bf16[2,128,2048]{2,1,0:T(8,128)(2,1)S(1)}, bf16[2,128,2048]{2,1,0:T(8,128)(2,1)}, u32[]{:S(2)}) copy-start(bf16[2,128,2048]{2,1,0:T(8,128)(2,1)} %get-tuple-element.22.refs_5_.down) | copy-start | bytes 3145732
  66.6 36.5 %copy-start.3 = (bf16[2,128,2048]{2,1,0:T(8,128)(2,1)S(1)}, bf16[2,128,2048]{2,1,0:T(8,128)(2,1)}, u32[]{:S(2)}) copy-start(bf16[2,128,2048]{2,1,0:T(8,128)(2,1)} %get-tuple-element.17.refs_6_.own_a) | copy-start | bytes 3145732
  66.6 36.5 %copy-start.4 = (bf16[2,128,2048]{2,1,0:T(8,128)(2,1)S(1)}, bf16[2,128,2048]{2,1,0:T(8,128)(2,1)}, u32[]{:S(2)}) copy-start(bf16[2,128,2048]{2,1,0:T(8,128)(2,1)} %get-tuple-element.18.refs_7_.own_b) | copy-start | bytes 3145732
  69.5 33.6 %collective-permute-start.10 = (bf16[2,128,2048]{2,1,0:T(8,128)(2,1)}, bf16[2,128,2048]{2,1,0:T(8,128)(2,1)}, u32[]{:S(2)}, u32[]{:S(2)}) collective-permute-start(bf16[2,128,2048]{2,1,0:T(8,128)(2,1)} %get-tuple-element.26), channel_id=1, source_target_pairs={{0,4},{1,5},{2,6},{3,7},{4,8},{5,9},{6,10},{7,11},{8,12},{9,13},{1... | collective-permute-start | bytes 3145736 | tf_op jit(solution)/shard_map/ppermute | solution.py:304
  70.4 32.8 %collective-permute-start.13 = (bf16[2,128,2048]{2,1,0:T(8,128)(2,1)}, bf16[2,128,2048]{2,1,0:T(8,128)(2,1)}, u32[]{:S(2)}, u32[]{:S(2)}) collective-permute-start(bf16[2,128,2048]{2,1,0:T(8,128)(2,1)} %get-tuple-element.27), channel_id=1, source_target_pairs={{0,12},{1,13},{2,14},{3,15},{4,0},{5,1},{6,2},{7,3},{8,4},{9,5},{1... | collective-permute-start | bytes 3145736 | tf_op jit(solution)/shard_map/ppermute | solution.py:304
  105.5 20.8 %collective-permute-start.14 = (bf16[128,2048]{1,0:T(8,128)(2,1)S(1)}, bf16[128,2048]{1,0:T(8,128)(2,1)S(1)}, u32[]{:S(2)}, u32[]{:S(2)}) collective-permute-start(bf16[128,2048]{1,0:T(8,128)(2,1)S(1)} %get-tuple-element.29), channel_id=1, source_target_pairs={{0,2},{1,3},{2,0},{3,1},{4,6},{5,7},{6,4},{7,5},{8,10},{9,11},{10,... | collective-permute-start | bytes 1572872 | tf_op jit(solution)/shard_map/ppermute | solution.py:304
  107.2 19.1 %collective-permute-start.15 = (bf16[128,2048]{1,0:T(8,128)(2,1)S(1)}, bf16[128,2048]{1,0:T(8,128)(2,1)S(1)}, u32[]{:S(2)}, u32[]{:S(2)}) collective-permute-start(bf16[128,2048]{1,0:T(8,128)(2,1)S(1)} %get-tuple-element.30), channel_id=1, source_target_pairs={{0,1},{1,2},{2,3},{3,0},{4,5},{5,6},{6,7},{7,4},{8,9},{9,10},{10,1... | collective-permute-start | bytes 1572872 | tf_op jit(solution)/shard_map/ppermute | solution.py:304
  108.5 17.9 %collective-permute-start.16 = (bf16[128,2048]{1,0:T(8,128)(2,1)S(1)}, bf16[128,2048]{1,0:T(8,128)(2,1)S(1)}, u32[]{:S(2)}, u32[]{:S(2)}) collective-permute-start(bf16[128,2048]{1,0:T(8,128)(2,1)S(1)} %get-tuple-element.31), channel_id=1, source_target_pairs={{0,3},{1,0},{2,1},{3,2},{4,7},{5,4},{6,5},{7,6},{8,11},{9,8},{10,9... | collective-permute-start | bytes 1572872 | tf_op jit(solution)/shard_map/ppermute | solution.py:304

commit v7 on v5

--- a/solution.py
+++ b/solution.py
@@ -14,6 +14,7 @@
 GROUP = 2
 AHEAD = 3
 CUTS = 3
+STAGES = 4
 SIDE = 4
 WIDTH = CBS * TILE
 C2 = 256
@@ -85,15 +86,15 @@
             for n in range(CUTS)
         ]
 
-    for r in range(AHEAD):
-        for copy in fetch(r):
-            copy.start()
     loads = [
         pltpu.make_async_copy(src.at[pl.ds(0, RB)], tiles.at[pl.ds(n * RB, RB)], p_sem.at[n])
         for n, src in enumerate((left_ref, own_ref, right_ref))
     ]
     for load in loads:
         load.start()
+    for r in range(AHEAD):
+        for copy in fetch(r):
+            copy.start()
     acc[...] = jnp.zeros_like(acc)
     for load in loads:
         load.wait()
@@ -124,30 +125,30 @@
                 acc[:, pl.ds(place, TILE)] += terms[:, n * TILE:(n + 1) * TILE]
         return 0
 
-    def leave(n, half):
-        return pltpu.make_async_copy(stage.at[half], outs[n].at[half], out_sem.at[half])
+    def leave(n, half, slot):
+        return pltpu.make_async_copy(stage.at[slot], outs[n].at[half], out_sem.at[slot])
 
     def block(t, _):
-        pair, half = lax.div(t, 2), lax.rem(t, 2)
+        pair, half, slot = lax.div(t, 2), lax.rem(t, 2), lax.rem(t, STAGES)
         lax.fori_loop(table[t, STARTS], table[t + 1, STARTS], row, 0)
 
-        @pl.when(pair > 0)
+        @pl.when(t >= STAGES)
         def _():
-            leave(0, half).wait()
+            leave(0, 0, slot).wait()
 
         for first in range(0, WIDTH, TILE):
             columns = pl.ds(first, TILE)
-            stage[half, :, columns] = acc[:, columns].astype(jnp.bfloat16)
+            stage[slot, :, columns] = acc[:, columns].astype(jnp.bfloat16)
             acc[:, columns] = jnp.zeros((TILE, TILE), jnp.float32)
         for n in range(PAIRS):
             @pl.when(pair == n)
             def _(n=n):
-                leave(n, half).start()
+                leave(n, half, slot).start()
         return 0
 
     lax.fori_loop(0, 2 * PAIRS, block, 0)
-    for half in range(2):
-        leave(0, half).wait()
+    for slot in range(STAGES):
+        leave(0, 0, slot).wait()
 
 
 def galerkin(table, maps, a_tiles, left, own, right):
@@ -165,10 +166,10 @@
                 pltpu.VMEM((AHEAD + 1, KA, TILE, TILE), jnp.bfloat16),
                 pltpu.VMEM((3 * RB, TILE, TILE), jnp.bfloat16),
                 pltpu.VMEM((TILE, WIDTH + TILE), jnp.float32),
-                pltpu.VMEM((2, TILE, WIDTH), jnp.bfloat16),
+                pltpu.VMEM((STAGES, TILE, WIDTH), jnp.bfloat16),
                 pltpu.SemaphoreType.DMA((AHEAD + 1, CUTS)),
                 pltpu.SemaphoreType.DMA((3,)),
-                pltpu.SemaphoreType.DMA((2,)),
+                pltpu.SemaphoreType.DMA((STAGES,)),
             ],
         ),
         compiler_params=pltpu.CompilerParams(vmem_limit_bytes=52 * 1024 * 1024),
@@ -370,7 +371,8 @@
     prolong_high = lax.reduce_precision(prolong, 8, 7)
     prolong_low = (prolong - prolong_high).astype(jnp.bfloat16)
     prolong_high = prolong_high.astype(jnp.bfloat16)
-    far_a, far_b = held_back(far_a, far_b, prolong_high)
+    square_held = jnp.sum(square[1:, 0, :8, :TILE].astype(jnp.float32) * scale, axis=0)
+    far_a, far_b = held_back(far_a, far_b, square_held)
     parts = (far_a, far_b, up_b, down_a, up_a, down_b, own_a, own_b)
     from_far_a, from_far_b = send(far_a, 0, 1), send(far_b, 0, -1)
     from_up_b, from_down_a = send(up_b, 0, 1), send(down_a, 0, -1)

time: 126 us -> 122 us (0.968)
  blocking collectives: 47.3 us -> 44.5 us
    all_to_all x1, blocking collectives: 31.6 us -> 27.6 us  [share_out(): return jnp.sum(lax.all_to_all(pieces, ('sect', 'rows'), 0, 0), axis=0)]
  transfers between devices with their start and end apart: 17 -> 17, of which waited for: 2 -> 1; matrix products, arithmetic and copies ran while one was open for 2% -> 4% of each run, Pallas kernels for 25% -> 26%
where the time goes in v7:
time: 122 us
  blocking collectives  44.5 us (36%)
  Pallas kernels  34 us (28%)
  starting transfers between devices  27.7 us (23%)
  other arithmetic  7.9 us (6%)
  waiting for transfers between devices  4.76 us (4%)
  local copies, waits for them, and re-layouts  2.16 us (2%)
    all_to_all x1, blocking collectives, share_out(): return jnp.sum(lax.all_to_all(pieces, ('sect', 'rows'), 0, 0), axis=0)  27.6 us
    ppermute x15, starting transfers between devices, send(): return lax.ppermute(value, ('sect', 'rows'), STEPS[second][by])  23.8 us
    pallas_call x1, Pallas kernels, galerkin(): pl.pallas_call(galerkin_body, out_shape=[jax.ShapeDtypeStruct((2, TILE, W...  18.3 us
    all_to_all x1, blocking collectives, bring_back(): lax.all_to_all(jnp.broadcast_to(piece[None], (128,) + piece.shape), ('sec...  16.9 us
    pallas_call x1, Pallas kernels, coarsest_term(): pl.pallas_call(coarsest_body, out_shape=jax.ShapeDtypeStruct((C2, C2), jn...  8.16 us
    ppermute x15, waiting for transfers between devices, send(): return lax.ppermute(value, ('sect', 'rows'), STEPS[second][by])  4.75 us
    pallas_call x1, Pallas kernels, row_plan(): pl.pallas_call(plan_body, out_shape=jax.ShapeDtypeStruct((RB + 1, 32), jn...  2.91 us
    ppermute x1, starting transfers between devices, per_device(): lax.ppermute(own, 'rows', up)  2.62 us
  transfers between devices with their start and end apart: 17, of which 1 were waited for; matrix products, arithmetic and copies ran while one was open for 4% of the time, Pallas kernels for 26%

profile of v7, /device:TPU:1, one launch (start us, length us, event | category | flops | bytes accessed | tf_op | source)
XLA Modules:
  0.0 121.9 jit_solution(5581511029209231966)
XLA Ops:
  0.6 0.7 subtract_bitcast_fusion
  1.3 1.1 fusion.2.own_ref
  2.4 1.3 %collective-permute-start.1 = (bf16[17,128,128]{2,1,0:T(8,128)(2,1)S(1)}, bf16[17,128,128]{2,1,0:T(8,128)(2,1)S(1)}, u32[]{:S(2)}, u32[]{:S(2)}) collective-permute-start(bf16[17,128,128]{2,1,0:T(8,128)(2,1)S(1)} %fusion.2.own_ref), channel_id=1, source_target_pairs={{1,0},{2,1},{3,2},{4,3},{5,4},{6,5},{7,6},{8,7},{9,8},{10,9},{11,1... | collective-permute-start | bytes 1671176 | tf_op jit(solution)/shard_map/ppermute | solution.py:362
  3.7 0.9 multiply_convert_fusion
  4.6 4.6 %collective-permute-start.3 = (f16[128,256]{1,0:T(8,128)(2,1)S(1)}, f16[128,256]{1,0:T(8,128)(2,1)S(1)}, u32[]{:S(2)}, u32[]{:S(2)}) collective-permute-start(f16[128,256]{1,0:T(8,128)(2,1)S(1)} %multiply_convert_fusion), channel_id=1, source_target_pairs={{0,8},{1,9},{2,10},{3,11},{4,12},{5,13},{6,14},{7,15},{8,0},{9,1},... | collective-permute-start | bytes 196616 | tf_op jit(solution)/shard_map/ppermute | solution.py:298
  9.2 0.6 collective-permute-start.2
  9.8 0.8 collective-permute-start.4
  10.7 2.6 %collective-permute-start = (bf16[17,128,128]{2,1,0:T(8,128)(2,1)S(1)}, bf16[17,128,128]{2,1,0:T(8,128)(2,1)S(1)}, u32[]{:S(2)}, u32[]{:S(2)}) collective-permute-start(bf16[17,128,128]{2,1,0:T(8,128)(2,1)S(1)} %fusion.2.own_ref), channel_id=1, source_target_pairs={{0,1},{1,2},{2,3},{3,4},{4,5},{5,6},{6,7},{7,8},{8,9},{9,10},{10,1... | collective-permute-start | bytes 1671176 | tf_op jit(solution)/shard_map/ppermute | solution.py:362
  13.3 0.9 fusion.8
  14.3 0.7 stack.63.info
  15.0 2.9 %shard_map.77.table = s32[17,32]{1,0:T(8,128)} custom-call(s32[16,27]{1,0:T(8,128)} %cols.1, s32[16]{0:T(128)} %counts.1, s32[16]{0:T(128)} %own_map.1, s32[8]{0:T(128)} %stack.63.info), custom_call_target="tpu_custom_call" | custom-call | bytes 11100000 | tf_op jit(solution)/shard_map/pallas_call | solution.py:66
  17.9 0.0 collective-permute-done.3
  17.9 4.7 %collective-permute-done.2 = f16[128,256]{1,0:T(8,128)(2,1)S(1)} collective-permute-done((f16[128,256]{1,0:T(8,128)(2,1)S(1)}, f16[128,256]{1,0:T(8,128)(2,1)S(1)}, u32[]{:S(2)}, u32[]{:S(2)}) %collective-permute-start.2) | collective-permute-done | bytes 65568 | tf_op jit(solution)/shard_map/ppermute | solution.py:298
  22.6 0.0 collective-permute-done.4
  22.6 0.1 fusion.7
  22.7 1.3 %collective-permute-start.7 = (f16[4,128,256]{2,1,0:T(8,128)(2,1)S(1)}, f16[4,128,256]{2,1,0:T(8,128)(2,1)S(1)}, u32[]{:S(2)}, u32[]{:S(2)}) collective-permute-start(f16[4,128,256]{2,1,0:T(8,128)(2,1)S(1)} %get-tuple-element.39), channel_id=1, source_target_pairs={{0,1},{1,2},{2,3},{3,0},{4,5},{5,6},{6,7},{7,4},{8,9},{9,10},{10,1... | collective-permute-start | bytes 786440 | tf_op jit(solution)/shard_map/ppermute | solution.py:298
  24.0 1.6 %collective-permute-start.6 = (f16[4,128,256]{2,1,0:T(8,128)(2,1)S(1)}, f16[4,128,256]{2,1,0:T(8,128)(2,1)S(1)}, u32[]{:S(2)}, u32[]{:S(2)}) collective-permute-start(f16[4,128,256]{2,1,0:T(8,128)(2,1)S(1)} %get-tuple-element.39), channel_id=1, source_target_pairs={{0,2},{1,3},{2,0},{3,1},{4,6},{5,7},{6,4},{7,5},{8,10},{9,11},{10,... | collective-permute-start | bytes 786440 | tf_op jit(solution)/shard_map/ppermute | solution.py:298
  25.6 2.0 %collective-permute-start.5 = (f16[4,128,256]{2,1,0:T(8,128)(2,1)S(1)}, f16[4,128,256]{2,1,0:T(8,128)(2,1)S(1)}, u32[]{:S(2)}, u32[]{:S(2)}) collective-permute-start(f16[4,128,256]{2,1,0:T(8,128)(2,1)S(1)} %get-tuple-element.39), channel_id=1, source_target_pairs={{0,3},{1,0},{2,1},{3,2},{4,7},{5,4},{6,5},{7,6},{8,11},{9,8},{10,9... | collective-permute-start | bytes 786440 | tf_op jit(solution)/shard_map/ppermute | solution.py:298
  27.6 0.0 collective-permute-done.1.right_ref
  27.6 0.0 collective-permute-done.left_ref
  27.6 0.0 copy-start.5
  27.6 0.7 copy-done.5
  28.3 18.3 %shard_map.78 = (bf16[2,128,2048]{2,1,0:T(8,128)(2,1)}, bf16[2,128,2048]{2,1,0:T(8,128)(2,1)}, bf16[2,128,2048]{2,1,0:T(8,128)(2,1)}, bf16[2,128,2048]{2,1,0:T(8...) custom-call(s32[17,32]{1,0:T(8,128)S(1)} %copy-done.5, ...), custom_call_target="tpu_custom_call" | custom-call | bytes 74000000 | tf_op jit(solution)/shard_map/pallas_call | solution.py:156
  46.6 0.0 collective-permute-done.7
  46.7 0.0 collective-permute-done.6
  46.7 0.0 collective-permute-done.5
  46.7 0.6 fusion.3.refs_2_
  47.3 0.0 collective-permute-start.8
  47.3 3.1 %collective-permute-start.9 = (bf16[2,128,2048]{2,1,0:T(8,128)(2,1)}, bf16[2,128,2048]{2,1,0:T(8,128)(2,1)S(1)}, u32[]{:S(2)}, u32[]{:S(2)}) collective-permute-start(bf16[2,128,2048]{2,1,0:T(8,128)(2,1)} %get-tuple-element.27.refs_1_), channel_id=1, source_target_pairs={{0,12},{1,13},{2,14},{3,15},{4,0},{5,1},{6,2},{7,3},{8,4},{9,5},{1... | collective-permute-start | bytes 3145736 | tf_op jit(solution)/shard_map/ppermute | solution.py:298
  50.4 0.0 collective-permute-start.11
  50.4 2.7 %collective-permute-start.12 = (bf16[2,128,2048]{2,1,0:T(8,128)(2,1)}, bf16[2,128,2048]{2,1,0:T(8,128)(2,1)}, u32[]{:S(2)}, u32[]{:S(2)}) collective-permute-start(bf16[2,128,2048]{2,1,0:T(8,128)(2,1)} %get-tuple-element.29.refs_3_), channel_id=1, source_target_pairs={{0,12},{1,13},{2,14},{3,15},{4,0},{5,1},{6,2},{7,3},{8,4},{9,5},{1... | collective-permute-start | bytes 3145736 | tf_op jit(solution)/shard_map/ppermute | solution.py:298
  53.1 0.3 convert_multiply_fusion
  53.4 0.0 copy-start.2
  53.5 0.0 copy-start.6
  53.5 1.9 %fusion = (bf16[16,128,256]{2,1,0:T(8,128)(2,1)}, bf16[16,128,256]{2,1,0:T(8,128)(2,1)}) fusion(f32[4,4,128,256]{3,2,1,0:T(8,128)S(1)} %convert_multiply_fusion), kind=kLoop, calls=%fused_computation.2 | loop fusion | flops 2097152 | bytes 4194304 | tf_op jit(solution)/shard_map/convert_element_type | solution.py:372
  55.3 0.0 copy-done.2
  55.3 0.0 copy-done.6
  55.3 0.0 copy-start.1
  55.4 8.2 %shard_map.80._ = f32[256,256]{1,0:T(8,128)S(1)} custom-call(s32[17,32]{1,0:T(8,128)S(1)} %copy-done.6, bf16[2,128,2048]{2,1,0:T(8,128)(2,1)S(1)} %copy-done.2, bf16[2,128,2048]{2,1,0:T(8,128)(2,1)} %get-tuple-element.27.refs_1_, bf16[2,128,2048]{2,1,0:T(8,128)(2,1)} %get-tuple-element.28.refs_2_, bf16[2,128,2048]{2,1,0:T(8,128)(2,1)} %get-tuple-element.29.refs_3_, ...), custom_call_target="tpu_custom_call" | custom-call | bytes 22200000 | tf_op jit(solution)/shard_map/pallas_call | solution.py:224
  63.5 0.0 copy-start.3
  63.5 0.0 copy-start.4
  63.5 0.0 collective-permute-done.8.from_far_a
  63.6 0.0 collective-permute-done.9.from_far_b
  63.6 0.0 copy-done
  63.6 0.0 copy-done.1
  63.6 2.3 %shard_map.81 = (bf16[2,128,2048]{2,1,0:T(8,128)(2,1)}, bf16[2,128,2048]{2,1,0:T(8,128)(2,1)}) custom-call(bf16[2,128,2048]{2,1,0:T(8,128)(2,1)S(1)} %copy-done, bf16[2,128,2048]{2,1,0:T(8,128)(2,1)S(1)} %collective-permute-done.8.from_far_a, bf16[2,128,2048]{2,1,0:T(8,128)(2,1)S(1)} %copy-done.1, ...), custom_call_target="tpu_custom_call" | custom-call | bytes 7400000 | tf_op jit(solution)/shard_map/pallas_call | solution.py:269
  65.9 0.4 collective-permute-start.10
  66.2 2.3 %collective-permute-start.13 = (bf16[2,128,2048]{2,1,0:T(8,128)(2,1)}, bf16[2,128,2048]{2,1,0:T(8,128)(2,1)}, u32[]{:S(2)}, u32[]{:S(2)}) collective-permute-start(bf16[2,128,2048]{2,1,0:T(8,128)(2,1)} %get-tuple-element.31), channel_id=1, source_target_pairs={{0,12},{1,13},{2,14},{3,15},{4,0},{5,1},{6,2},{7,3},{8,4},{9,5},{1... | collective-permute-start | bytes 3145736 | tf_op jit(solution)/shard_map/ppermute | solution.py:298
  68.5 27.6 %all_to_all.10 = f32[128,4,128]{2,1,0:T(4,128)S(1)} all-to-all(f32[128,4,128]{2,1,0:T(4,128)S(1)} %bitcast.50), channel_id=1, replica_groups=mesh['sect'=8,'rows'=16] {'sect','rows'}, dimensions={0} | all-to-all | bytes 524288 | tf_op jit(solution)/shard_map/all_to_all | solution.py:307
  96.1 0.1 reduce_sum.19._
  96.3 0.0 collective-permute-done.11.up_b
  96.3 0.0 collective-permute-done.12.down_a
  96.3 0.0 collective-permute-done.10.up_a
  96.3 0.0 collective-permute-done.13.down_b
  96.3 2.4 %shard_map.82 = (bf16[128,2048]{1,0:T(8,128)(2,1)S(1)}, bf16[128,2048]{1,0:T(8,128)(2,1)S(1)}, bf16[128,2048]{1,0:T(8,128)(2,1)S(1)}, f32[128,2048]{1,0:T(8,128)S(1)}) custom-call(bf16[2,128,2048]{2,1,0:T(8,128)(2,1)S(1)} %copy-done.3, bf16[2,128,2048]{2,1,0:T(8,128)(2,1)S(1)} %copy-done.4, bf16[2,128,2048]{2,1,0:T(8,128)(2,1)} %collective-permute-done.10.up_a, ...), custom_call_target="tpu_custom_call" | custom-call | bytes 11100000 | tf_op jit(solution)/shard_map/pallas_call | solution.py:337
  98.7 1.6 %collective-permute-start.14 = (bf16[128,2048]{1,0:T(8,128)(2,1)S(1)}, bf16[128,2048]{1,0:T(8,128)(2,1)S(1)}, u32[]{:S(2)}, u32[]{:S(2)}) collective-permute-start(bf16[128,2048]{1,0:T(8,128)(2,1)S(1)} %get-tuple-element.33), channel_id=1, source_target_pairs={{0,2},{1,3},{2,0},{3,1},{4,6},{5,7},{6,4},{7,5},{8,10},{9,11},{10,... | collective-permute-start | bytes 1572872 | tf_op jit(solution)/shard_map/ppermute | solution.py:298
  100.3 0.8 collective-permute-start.15
  101.2 1.8 %collective-permute-start.16 = (bf16[128,2048]{1,0:T(8,128)(2,1)S(1)}, bf16[128,2048]{1,0:T(8,128)(2,1)S(1)}, u32[]{:S(2)}, u32[]{:S(2)}) collective-permute-start(bf16[128,2048]{1,0:T(8,128)(2,1)S(1)} %get-tuple-element.35), channel_id=1, source_target_pairs={{0,3},{1,0},{2,1},{3,2},{4,7},{5,4},{6,5},{7,6},{8,11},{9,8},{10,9... | collective-permute-start | bytes 1572872 | tf_op jit(solution)/shard_map/ppermute | solution.py:298
  103.1 16.9 %all_to_all.11 = f32[128,4,128]{2,1,0:T(4,128)S(1)} all-to-all(f32[128,4,128]{2,1,0:T(4,128)S(1)} %broadcast_in_dim.5), channel_id=1, replica_groups=mesh['sect'=8,'rows'=16] {'sect','rows'}, dimensions={0} | all-to-all | bytes 524288 | tf_op jit(solution)/shard_map/all_to_all | solution.py:311
  119.9 0.0 collective-permute-done.14
  119.9 0.0 collective-permute-done.15
  119.9 0.0 collective-permute-done.16
  119.9 1.3 %add_add_fusion = f32[128,2048]{1,0:T(8,128)} fusion(f32[128,2048]{1,0:T(8,128)S(1)} %get-tuple-element.32, bf16[128,2048]{1,0:T(8,128)(2,1)S(1)} %collective-permute-done.16, bf16[128,2048]{1,0:T(8,128)(2,1)S(1)} %collective-permute-done.15, bf16[128,2048]{1,0:T(8,128)(2,1)S(1)} %collective-permute-done.14), kind=kLoop, calls=%fused_computation.6 | loop fusion | flops 1572864 | bytes 3670016 | tf_op jit(solution)/shard_map/add | solution.py:387
  121.2 0.7 copy.13
  (9 shorter events, 0.1 us)
Async XLA Ops:
  2.4 25.2 %collective-permute-start.1 = (bf16[17,128,128]{2,1,0:T(8,128)(2,1)S(1)}, bf16[17,128,128]{2,1,0:T(8,128)(2,1)S(1)}, u32[]{:S(2)}, u32[]{:S(2)}) collective-permute-start(bf16[17,128,128]{2,1,0:T(8,128)(2,1)S(1)} %fusion.2.own_ref), channel_id=1, source_target_pairs={{1,0},{2,1},{3,2},{4,3},{5,4},{6,5},{7,6},{8,7},{9,8},{10,9},{11,1... | collective-permute-start | bytes 1671176 | tf_op jit(solution)/shard_map/ppermute | solution.py:362
  4.6 13.3 %collective-permute-start.3 = (f16[128,256]{1,0:T(8,128)(2,1)S(1)}, f16[128,256]{1,0:T(8,128)(2,1)S(1)}, u32[]{:S(2)}, u32[]{:S(2)}) collective-permute-start(f16[128,256]{1,0:T(8,128)(2,1)S(1)} %multiply_convert_fusion), channel_id=1, source_target_pairs={{0,8},{1,9},{2,10},{3,11},{4,12},{5,13},{6,14},{7,15},{8,0},{9,1},... | collective-permute-start | bytes 196616 | tf_op jit(solution)/shard_map/ppermute | solution.py:298
  9.2 13.4 %collective-permute-start.2 = (f16[128,256]{1,0:T(8,128)(2,1)S(1)}, f16[128,256]{1,0:T(8,128)(2,1)S(1)}, u32[]{:S(2)}, u32[]{:S(2)}) collective-permute-start(f16[128,256]{1,0:T(8,128)(2,1)S(1)} %multiply_convert_fusion), channel_id=1, source_target_pairs={{0,12},{1,13},{2,14},{3,15},{4,0},{5,1},{6,2},{7,3},{8,4},{9,5},{1... | collective-permute-start | bytes 196616 | tf_op jit(solution)/shard_map/ppermute | solution.py:298
  9.8 12.8 %collective-permute-start.4 = (f16[128,256]{1,0:T(8,128)(2,1)S(1)}, f16[128,256]{1,0:T(8,128)(2,1)S(1)}, u32[]{:S(2)}, u32[]{:S(2)}) collective-permute-start(f16[128,256]{1,0:T(8,128)(2,1)S(1)} %multiply_convert_fusion), channel_id=1, source_target_pairs={{0,4},{1,5},{2,6},{3,7},{4,8},{5,9},{6,10},{7,11},{8,12},{9,13},{1... | collective-permute-start | bytes 196616 | tf_op jit(solution)/shard_map/ppermute | solution.py:298
  10.7 16.9 %collective-permute-start = (bf16[17,128,128]{2,1,0:T(8,128)(2,1)S(1)}, bf16[17,128,128]{2,1,0:T(8,128)(2,1)S(1)}, u32[]{:S(2)}, u32[]{:S(2)}) collective-permute-start(bf16[17,128,128]{2,1,0:T(8,128)(2,1)S(1)} %fusion.2.own_ref), channel_id=1, source_target_pairs={{0,1},{1,2},{2,3},{3,4},{4,5},{5,6},{6,7},{7,8},{8,9},{9,10},{10,1... | collective-permute-start | bytes 1671176 | tf_op jit(solution)/shard_map/ppermute | solution.py:362
  22.7 24.0 %collective-permute-start.7 = (f16[4,128,256]{2,1,0:T(8,128)(2,1)S(1)}, f16[4,128,256]{2,1,0:T(8,128)(2,1)S(1)}, u32[]{:S(2)}, u32[]{:S(2)}) collective-permute-start(f16[4,128,256]{2,1,0:T(8,128)(2,1)S(1)} %get-tuple-element.39), channel_id=1, source_target_pairs={{0,1},{1,2},{2,3},{3,0},{4,5},{5,6},{6,7},{7,4},{8,9},{9,10},{10,1... | collective-permute-start | bytes 786440 | tf_op jit(solution)/shard_map/ppermute | solution.py:298
  24.0 22.7 %collective-permute-start.6 = (f16[4,128,256]{2,1,0:T(8,128)(2,1)S(1)}, f16[4,128,256]{2,1,0:T(8,128)(2,1)S(1)}, u32[]{:S(2)}, u32[]{:S(2)}) collective-permute-start(f16[4,128,256]{2,1,0:T(8,128)(2,1)S(1)} %get-tuple-element.39), channel_id=1, source_target_pairs={{0,2},{1,3},{2,0},{3,1},{4,6},{5,7},{6,4},{7,5},{8,10},{9,11},{10,... | collective-permute-start | bytes 786440 | tf_op jit(solution)/shard_map/ppermute | solution.py:298
  25.6 21.1 %collective-permute-start.5 = (f16[4,128,256]{2,1,0:T(8,128)(2,1)S(1)}, f16[4,128,256]{2,1,0:T(8,128)(2,1)S(1)}, u32[]{:S(2)}, u32[]{:S(2)}) collective-permute-start(f16[4,128,256]{2,1,0:T(8,128)(2,1)S(1)} %get-tuple-element.39), channel_id=1, source_target_pairs={{0,3},{1,0},{2,1},{3,2},{4,7},{5,4},{6,5},{7,6},{8,11},{9,8},{10,9... | collective-permute-start | bytes 786440 | tf_op jit(solution)/shard_map/ppermute | solution.py:298
  27.6 0.7 copy-start.5
  47.3 16.3 %collective-permute-start.8 = (bf16[2,128,2048]{2,1,0:T(8,128)(2,1)}, bf16[2,128,2048]{2,1,0:T(8,128)(2,1)S(1)}, u32[]{:S(2)}, u32[]{:S(2)}) collective-permute-start(bf16[2,128,2048]{2,1,0:T(8,128)(2,1)} %get-tuple-element.25.refs_0_), channel_id=1, source_target_pairs={{0,4},{1,5},{2,6},{3,7},{4,8},{5,9},{6,10},{7,11},{8,12},{9,13},{1... | collective-permute-start | bytes 3145736 | tf_op jit(solution)/shard_map/ppermute | solution.py:298
  47.3 16.3 %collective-permute-start.9 = (bf16[2,128,2048]{2,1,0:T(8,128)(2,1)}, bf16[2,128,2048]{2,1,0:T(8,128)(2,1)S(1)}, u32[]{:S(2)}, u32[]{:S(2)}) collective-permute-start(bf16[2,128,2048]{2,1,0:T(8,128)(2,1)} %get-tuple-element.27.refs_1_), channel_id=1, source_target_pairs={{0,12},{1,13},{2,14},{3,15},{4,0},{5,1},{6,2},{7,3},{8,4},{9,5},{1... | collective-permute-start | bytes 3145736 | tf_op jit(solution)/shard_map/ppermute | solution.py:298
  50.4 45.9 %collective-permute-start.11 = (bf16[2,128,2048]{2,1,0:T(8,128)(2,1)}, bf16[2,128,2048]{2,1,0:T(8,128)(2,1)S(1)}, u32[]{:S(2)}, u32[]{:S(2)}) collective-permute-start(bf16[2,128,2048]{2,1,0:T(8,128)(2,1)} %get-tuple-element.28.refs_2_), channel_id=1, source_target_pairs={{0,4},{1,5},{2,6},{3,7},{4,8},{5,9},{6,10},{7,11},{8,12},{9,13},{1... | collective-permute-start | bytes 3145736 | tf_op jit(solution)/shard_map/ppermute | solution.py:298
  50.4 45.9 %collective-permute-start.12 = (bf16[2,128,2048]{2,1,0:T(8,128)(2,1)}, bf16[2,128,2048]{2,1,0:T(8,128)(2,1)}, u32[]{:S(2)}, u32[]{:S(2)}) collective-permute-start(bf16[2,128,2048]{2,1,0:T(8,128)(2,1)} %get-tuple-element.29.refs_3_), channel_id=1, source_target_pairs={{0,12},{1,13},{2,14},{3,15},{4,0},{5,1},{6,2},{7,3},{8,4},{9,5},{1... | collective-permute-start | bytes 3145736 | tf_op jit(solution)/shard_map/ppermute | solution.py:298
  53.4 1.9 %copy-start.2 = (bf16[2,128,2048]{2,1,0:T(8,128)(2,1)S(1)}, bf16[2,128,2048]{2,1,0:T(8,128)(2,1)}, u32[]{:S(2)}) copy-start(bf16[2,128,2048]{2,1,0:T(8,128)(2,1)} %get-tuple-element.25.refs_0_) | copy-start | bytes 3145732
  53.5 1.9 %copy-start.6 = (s32[17,32]{1,0:T(8,128)S(1)}, s32[17,32]{1,0:T(8,128)}, u32[]{:S(2)}) copy-start(s32[17,32]{1,0:T(8,128)} %shard_map.77.table) | copy-start | bytes 6532
  55.3 8.2 %copy-start = (bf16[2,128,2048]{2,1,0:T(8,128)(2,1)S(1)}, bf16[2,128,2048]{2,1,0:T(8,128)(2,1)}, u32[]{:S(2)}) copy-start(bf16[2,128,2048]{2,1,0:T(8,128)(2,1)} %get-tuple-element.21.refs_4_.up) | copy-start | bytes 3145732
  55.3 8.2 %copy-start.1 = (bf16[2,128,2048]{2,1,0:T(8,128)(2,1)S(1)}, bf16[2,128,2048]{2,1,0:T(8,128)(2,1)}, u32[]{:S(2)}) copy-start(bf16[2,128,2048]{2,1,0:T(8,128)(2,1)} %get-tuple-element.26.refs_5_.down) | copy-start | bytes 3145732
  63.5 32.8 %copy-start.3 = (bf16[2,128,2048]{2,1,0:T(8,128)(2,1)S(1)}, bf16[2,128,2048]{2,1,0:T(8,128)(2,1)}, u32[]{:S(2)}) copy-start(bf16[2,128,2048]{2,1,0:T(8,128)(2,1)} %get-tuple-element.19.refs_6_.own_a) | copy-start | bytes 3145732
  63.5 32.8 %copy-start.4 = (bf16[2,128,2048]{2,1,0:T(8,128)(2,1)S(1)}, bf16[2,128,2048]{2,1,0:T(8,128)(2,1)}, u32[]{:S(2)}) copy-start(bf16[2,128,2048]{2,1,0:T(8,128)(2,1)} %get-tuple-element.20.refs_7_.own_b) | copy-start | bytes 3145732
  65.9 30.4 %collective-permute-start.10 = (bf16[2,128,2048]{2,1,0:T(8,128)(2,1)}, bf16[2,128,2048]{2,1,0:T(8,128)(2,1)}, u32[]{:S(2)}, u32[]{:S(2)}) collective-permute-start(bf16[2,128,2048]{2,1,0:T(8,128)(2,1)} %get-tuple-element.30), channel_id=1, source_target_pairs={{0,4},{1,5},{2,6},{3,7},{4,8},{5,9},{6,10},{7,11},{8,12},{9,13},{1... | collective-permute-start | bytes 3145736 | tf_op jit(solution)/shard_map/ppermute | solution.py:298
  66.2 30.1 %collective-permute-start.13 = (bf16[2,128,2048]{2,1,0:T(8,128)(2,1)}, bf16[2,128,2048]{2,1,0:T(8,128)(2,1)}, u32[]{:S(2)}, u32[]{:S(2)}) collective-permute-start(bf16[2,128,2048]{2,1,0:T(8,128)(2,1)} %get-tuple-element.31), channel_id=1, source_target_pairs={{0,12},{1,13},{2,14},{3,15},{4,0},{5,1},{6,2},{7,3},{8,4},{9,5},{1... | collective-permute-start | bytes 3145736 | tf_op jit(solution)/shard_map/ppermute | solution.py:298
  98.7 21.2 %collective-permute-start.14 = (bf16[128,2048]{1,0:T(8,128)(2,1)S(1)}, bf16[128,2048]{1,0:T(8,128)(2,1)S(1)}, u32[]{:S(2)}, u32[]{:S(2)}) collective-permute-start(bf16[128,2048]{1,0:T(8,128)(2,1)S(1)} %get-tuple-element.33), channel_id=1, source_target_pairs={{0,2},{1,3},{2,0},{3,1},{4,6},{5,7},{6,4},{7,5},{8,10},{9,11},{10,... | collective-permute-start | bytes 1572872 | tf_op jit(solution)/shard_map/ppermute | solution.py:298
  100.3 19.6 %collective-permute-start.15 = (bf16[128,2048]{1,0:T(8,128)(2,1)S(1)}, bf16[128,2048]{1,0:T(8,128)(2,1)S(1)}, u32[]{:S(2)}, u32[]{:S(2)}) collective-permute-start(bf16[128,2048]{1,0:T(8,128)(2,1)S(1)} %get-tuple-element.34), channel_id=1, source_target_pairs={{0,1},{1,2},{2,3},{3,0},{4,5},{5,6},{6,7},{7,4},{8,9},{9,10},{10,1... | collective-permute-start | bytes 1572872 | tf_op jit(solution)/shard_map/ppermute | solution.py:298
  101.2 18.7 %collective-permute-start.16 = (bf16[128,2048]{1,0:T(8,128)(2,1)S(1)}, bf16[128,2048]{1,0:T(8,128)(2,1)S(1)}, u32[]{:S(2)}, u32[]{:S(2)}) collective-permute-start(bf16[128,2048]{1,0:T(8,128)(2,1)S(1)} %get-tuple-element.35), channel_id=1, source_target_pairs={{0,3},{1,0},{2,1},{3,2},{4,7},{5,4},{6,5},{7,6},{8,11},{9,8},{10,9... | collective-permute-start | bytes 1572872 | tf_op jit(solution)/shard_map/ppermute | solution.py:298

commit v8 on v7

--- a/solution.py
+++ b/solution.py
@@ -28,6 +28,7 @@
 SEQUENCE = FAR + NEXT_ALONE + NEXT_JOINED + OWN
 PAIRS = len(SEQUENCE) // 2
 COUNT, ORDER, STARTS, INFO = KA, KA + 1, KA + 2, KA + 3
+MAPS = RB + 1
 Q_SCALE = 2.0**20
 
 
@@ -72,7 +73,7 @@
     )(*operands)
 
 
-def galerkin_body(table, maps, a_ref, left_ref, own_ref, right_ref, *rest):
+def galerkin_body(table, a_ref, left_ref, own_ref, right_ref, *rest):
     outs, (scale_ref, a_buf, tiles, acc, stage, a_sem, p_sem, out_sem) = rest[:PAIRS], rest[PAIRS:]
     scale_ref[...] = jnp.full(scale_ref.shape, 1.0 / Q_SCALE, jnp.float32)
 
@@ -115,7 +116,7 @@
             products, places = [], []
             for s in range(k, min(k + GROUP, KA)):
                 col = jnp.clip(table[i, s], 0, 3 * RB - 1)
-                block = jnp.clip(maps[lax.shift_right_logical(col, 4), lax.bitwise_and(col, RB - 1)], 0, CBS - 1)
+                block = jnp.clip(table[MAPS + lax.shift_right_logical(col, 4), lax.bitwise_and(col, RB - 1)], 0, CBS - 1)
                 places.append(pl.multiple_of(jnp.where(s < count, block, CBS) * TILE, TILE))
                 products.append(
                     jnp.dot(a_buf[slot, s], tiles[col], preferred_element_type=jnp.float32).astype(jnp.bfloat16)
@@ -151,14 +152,14 @@
         leave(0, 0, slot).wait()
 
 
-def galerkin(table, maps, a_tiles, left, own, right):
+def galerkin(table, a_tiles, left, own, right):
     anywhere = pl.BlockSpec(memory_space=pl.ANY)
     return pl.pallas_call(
         galerkin_body,
         out_shape=[jax.ShapeDtypeStruct((2, TILE, WIDTH), jnp.bfloat16)] * PAIRS
         + [jax.ShapeDtypeStruct((1, TILE), jnp.float32)],
         grid_spec=pltpu.PrefetchScalarGridSpec(
-            num_scalar_prefetch=2,
+            num_scalar_prefetch=1,
             grid=(1,),
             in_specs=[pl.BlockSpec(memory_space=pltpu.HBM)] + [anywhere] * 3,
             out_specs=[anywhere] * PAIRS + [pl.BlockSpec((1, TILE), lambda j, *_: (0, 0))],
@@ -174,7 +175,7 @@
         ),
         compiler_params=pltpu.CompilerParams(vmem_limit_bytes=52 * 1024 * 1024),
         cost_estimate=cost(20),
-    )(table, maps, a_tiles, left, own, right)
+    )(table, a_tiles, left, own, right)
 
 
 def coarsest_body(table, *refs):
@@ -330,7 +331,7 @@
 
 
 def reduced(own_a, own_b, up_a, up_b, down_a, down_b, after_this):
-    rows = 64
+    rows = 32
     pair = pl.BlockSpec((2, rows, WIDTH), lambda j: (0, j, 0))
     one = pl.BlockSpec((rows, WIDTH), lambda j: (j, 0))
     shape = (TILE, WIDTH)
@@ -364,8 +365,8 @@
 
     line = around((p_coarse * Q_SCALE).astype(jnp.float16), 0)
     square = around(line, 1)
-    table = row_plan(a_cols, a_count, coarse_map, info)
-    *parts, scale = galerkin(table, maps, a_tiles, left, own, right)
+    table = jnp.concatenate([row_plan(a_cols, a_count, coarse_map, info), jnp.pad(maps, ((0, 0), (0, 32 - RB)))], axis=0)
+    *parts, scale = galerkin(table, a_tiles, left, own, right)
     far_a, far_b, up_b, down_a, up_a, down_b, own_a, own_b = parts
     prolong = square.reshape(CBS, TILE, C2).astype(jnp.float32) * scale[0, 0]
     prolong_high = lax.reduce_precision(prolong, 8, 7)

time: 122 us -> 123 us (level)
  transfers between devices with their start and end apart: 17 -> 17, of which waited for: 1 -> 1; matrix products, arithmetic and copies ran while one was open for 4% -> 5% of each run, Pallas kernels for 26% -> 26%
where the time goes in v8:
time: 123 us
  blocking collectives  44.8 us (36%)
  Pallas kernels  34.8 us (28%)
  starting transfers between devices  27.4 us (22%)
  other arithmetic  8.59 us (7%)
  waiting for transfers between devices  4.83 us (4%)
  local copies, waits for them, and re-layouts  1.37 us (1%)
    all_to_all x1, blocking collectives, share_out(): return jnp.sum(lax.all_to_all(pieces, ('sect', 'rows'), 0, 0), axis=0)  27.6 us
    ppermute x15, starting transfers between devices, send(): return lax.ppermute(value, ('sect', 'rows'), STEPS[second][by])  23.5 us
    pallas_call x1, Pallas kernels, galerkin(): pl.pallas_call(galerkin_body, out_shape=[jax.ShapeDtypeStruct((2, TILE, W...  18.3 us
    all_to_all x1, blocking collectives, bring_back(): lax.all_to_all(jnp.broadcast_to(piece[None], (128,) + piece.shape), ('sec...  17.1 us
    pallas_call x1, Pallas kernels, coarsest_term(): pl.pallas_call(coarsest_body, out_shape=jax.ShapeDtypeStruct((C2, C2), jn...  8.16 us
    ppermute x15, waiting for transfers between devices, send(): return lax.ppermute(value, ('sect', 'rows'), STEPS[second][by])  4.83 us
    pallas_call x1, Pallas kernels, reduced(): pl.pallas_call(reduced_body, out_shape=[jax.ShapeDtypeStruct(shape, jnp.b...  3.07 us
    pallas_call x1, Pallas kernels, row_plan(): pl.pallas_call(plan_body, out_shape=jax.ShapeDtypeStruct((RB + 1, 32), jn...  2.91 us
  transfers between devices with their start and end apart: 17, of which 1 were waited for; matrix products, arithmetic and copies ran while one was open for 5% of the time, Pallas kernels for 26%

profile of v8, /device:TPU:1, one launch (start us, length us, event | category | flops | bytes accessed | tf_op | source)
XLA Modules:
  0.0 122.6 jit_solution(6868961681497361527)
XLA Ops:
  0.6 0.7 subtract_bitcast_fusion
  1.3 1.1 fusion.2.own_ref
  2.4 1.3 %collective-permute-start.1 = (bf16[17,128,128]{2,1,0:T(8,128)(2,1)S(1)}, bf16[17,128,128]{2,1,0:T(8,128)(2,1)S(1)}, u32[]{:S(2)}, u32[]{:S(2)}) collective-permute-start(bf16[17,128,128]{2,1,0:T(8,128)(2,1)S(1)} %fusion.2.own_ref), channel_id=1, source_target_pairs={{1,0},{2,1},{3,2},{4,3},{5,4},{6,5},{7,6},{8,7},{9,8},{10,9},{11,1... | collective-permute-start | bytes 1671176 | tf_op jit(solution)/shard_map/ppermute | solution.py:363
  3.7 0.9 multiply_convert_fusion
  4.6 4.6 %collective-permute-start.3 = (f16[128,256]{1,0:T(8,128)(2,1)S(1)}, f16[128,256]{1,0:T(8,128)(2,1)S(1)}, u32[]{:S(2)}, u32[]{:S(2)}) collective-permute-start(f16[128,256]{1,0:T(8,128)(2,1)S(1)} %multiply_convert_fusion), channel_id=1, source_target_pairs={{0,8},{1,9},{2,10},{3,11},{4,12},{5,13},{6,14},{7,15},{8,0},{9,1},... | collective-permute-start | bytes 196616 | tf_op jit(solution)/shard_map/ppermute | solution.py:299
  9.2 0.6 collective-permute-start.2
  9.8 0.8 collective-permute-start.4
  10.7 2.6 %collective-permute-start = (bf16[17,128,128]{2,1,0:T(8,128)(2,1)S(1)}, bf16[17,128,128]{2,1,0:T(8,128)(2,1)S(1)}, u32[]{:S(2)}, u32[]{:S(2)}) collective-permute-start(bf16[17,128,128]{2,1,0:T(8,128)(2,1)S(1)} %fusion.2.own_ref), channel_id=1, source_target_pairs={{0,1},{1,2},{2,3},{3,4},{4,5},{5,6},{6,7},{7,8},{8,9},{9,10},{10,1... | collective-permute-start | bytes 1671176 | tf_op jit(solution)/shard_map/ppermute | solution.py:363
  13.3 0.9 fusion.8
  14.3 0.6 stack.63.info
  14.9 2.9 %shard_map.77 = s32[17,32]{1,0:T(8,128)} custom-call(s32[16,27]{1,0:T(8,128)} %cols.1, s32[16]{0:T(128)} %counts.1, s32[16]{0:T(128)} %own_map.1, s32[8]{0:T(128)} %stack.63.info), custom_call_target="tpu_custom_call" | custom-call | bytes 11100000 | tf_op jit(solution)/shard_map/pallas_call | solution.py:67
  17.8 0.0 collective-permute-done.3
  17.8 4.8 %collective-permute-done.2 = f16[128,256]{1,0:T(8,128)(2,1)S(1)} collective-permute-done((f16[128,256]{1,0:T(8,128)(2,1)S(1)}, f16[128,256]{1,0:T(8,128)(2,1)S(1)}, u32[]{:S(2)}, u32[]{:S(2)}) %collective-permute-start.2) | collective-permute-done | bytes 65568 | tf_op jit(solution)/shard_map/ppermute | solution.py:299
  22.6 0.0 collective-permute-done.4
  22.6 0.1 fusion.7
  22.7 1.3 %collective-permute-start.7 = (f16[4,128,256]{2,1,0:T(8,128)(2,1)S(1)}, f16[4,128,256]{2,1,0:T(8,128)(2,1)S(1)}, u32[]{:S(2)}, u32[]{:S(2)}) collective-permute-start(f16[4,128,256]{2,1,0:T(8,128)(2,1)S(1)} %get-tuple-element.39), channel_id=1, source_target_pairs={{0,1},{1,2},{2,3},{3,0},{4,5},{5,6},{6,7},{7,4},{8,9},{9,10},{10,1... | collective-permute-start | bytes 786440 | tf_op jit(solution)/shard_map/ppermute | solution.py:299
  24.0 1.6 %collective-permute-start.6 = (f16[4,128,256]{2,1,0:T(8,128)(2,1)S(1)}, f16[4,128,256]{2,1,0:T(8,128)(2,1)S(1)}, u32[]{:S(2)}, u32[]{:S(2)}) collective-permute-start(f16[4,128,256]{2,1,0:T(8,128)(2,1)S(1)} %get-tuple-element.39), channel_id=1, source_target_pairs={{0,2},{1,3},{2,0},{3,1},{4,6},{5,7},{6,4},{7,5},{8,10},{9,11},{10,... | collective-permute-start | bytes 786440 | tf_op jit(solution)/shard_map/ppermute | solution.py:299
  25.6 2.0 %collective-permute-start.5 = (f16[4,128,256]{2,1,0:T(8,128)(2,1)S(1)}, f16[4,128,256]{2,1,0:T(8,128)(2,1)S(1)}, u32[]{:S(2)}, u32[]{:S(2)}) collective-permute-start(f16[4,128,256]{2,1,0:T(8,128)(2,1)S(1)} %get-tuple-element.39), channel_id=1, source_target_pairs={{0,3},{1,0},{2,1},{3,2},{4,7},{5,4},{6,5},{7,6},{8,11},{9,8},{10,9... | collective-permute-start | bytes 786440 | tf_op jit(solution)/shard_map/ppermute | solution.py:299
  27.6 0.0 collective-permute-done.1.right_ref
  27.6 0.0 collective-permute-done.left_ref
  27.6 0.7 pad_add_fusion.table
  28.3 18.3 %shard_map.78 = (bf16[2,128,2048]{2,1,0:T(8,128)(2,1)}, bf16[2,128,2048]{2,1,0:T(8,128)(2,1)}, bf16[2,128,2048]{2,1,0:T(8,128)(2,1)}, bf16[2,128,2048]{2,1,0:T(8...) custom-call(s32[20,32]{1,0:T(8,128)S(1)} %pad_add_fusion.table, ...), custom_call_target="tpu_custom_call" | custom-call | bytes 74000000 | tf_op jit(solution)/shard_map/pallas_call | solution.py:157
  46.7 0.0 collective-permute-done.7
  46.7 0.0 collective-permute-done.6
  46.7 0.0 collective-permute-done.5
  46.7 0.6 fusion.3.refs_2_
  47.3 0.0 collective-permute-start.8
  47.3 3.1 %collective-permute-start.9 = (bf16[2,128,2048]{2,1,0:T(8,128)(2,1)}, bf16[2,128,2048]{2,1,0:T(8,128)(2,1)S(1)}, u32[]{:S(2)}, u32[]{:S(2)}) collective-permute-start(bf16[2,128,2048]{2,1,0:T(8,128)(2,1)} %get-tuple-element.27.refs_1_), channel_id=1, source_target_pairs={{0,12},{1,13},{2,14},{3,15},{4,0},{5,1},{6,2},{7,3},{8,4},{9,5},{1... | collective-permute-start | bytes 3145736 | tf_op jit(solution)/shard_map/ppermute | solution.py:299
  50.4 0.0 collective-permute-start.11
  50.4 2.7 %collective-permute-start.12 = (bf16[2,128,2048]{2,1,0:T(8,128)(2,1)}, bf16[2,128,2048]{2,1,0:T(8,128)(2,1)}, u32[]{:S(2)}, u32[]{:S(2)}) collective-permute-start(bf16[2,128,2048]{2,1,0:T(8,128)(2,1)} %get-tuple-element.29.refs_3_), channel_id=1, source_target_pairs={{0,12},{1,13},{2,14},{3,15},{4,0},{5,1},{6,2},{7,3},{8,4},{9,5},{1... | collective-permute-start | bytes 3145736 | tf_op jit(solution)/shard_map/ppermute | solution.py:299
  53.1 0.3 convert_multiply_fusion
  53.5 0.0 copy-start.2
  53.5 1.8 %fusion = (bf16[16,128,256]{2,1,0:T(8,128)(2,1)}, bf16[16,128,256]{2,1,0:T(8,128)(2,1)}) fusion(f32[4,4,128,256]{3,2,1,0:T(8,128)S(1)} %convert_multiply_fusion), kind=kLoop, calls=%fused_computation.2 | loop fusion | flops 2097152 | bytes 4194304 | tf_op jit(solution)/shard_map/convert_element_type | solution.py:373
  55.3 0.0 copy-done.2
  55.3 0.0 copy-start
  55.3 0.0 copy-start.1
  55.3 8.2 %shard_map.80._ = f32[256,256]{1,0:T(8,128)S(1)} custom-call(s32[20,32]{1,0:T(8,128)S(1)} %pad_add_fusion.table, bf16[2,128,2048]{2,1,0:T(8,128)(2,1)S(1)} %copy-done.2, bf16[2,128,2048]{2,1,0:T(8,128)(2,1)} %get-tuple-element.27.refs_1_, bf16[2,128,2048]{2,1,0:T(8,128)(2,1)} %get-tuple-element.28.refs_2_, bf16[2,128,2048]{2,1,0:T(8,128)(2,1)} %get-tuple-element.29.refs_3_, ...), custom_call_target="tpu_custom_call" | custom-call | bytes 22200000 | tf_op jit(solution)/shard_map/pallas_call | solution.py:225
  63.5 0.0 copy-start.3
  63.5 0.0 copy-start.4
  63.5 0.0 collective-permute-done.8.from_far_a
  63.5 0.0 collective-permute-done.9.from_far_b
  63.5 0.0 copy-done
  63.5 0.0 copy-done.1
  63.5 2.3 %shard_map.81 = (bf16[2,128,2048]{2,1,0:T(8,128)(2,1)}, bf16[2,128,2048]{2,1,0:T(8,128)(2,1)}) custom-call(bf16[2,128,2048]{2,1,0:T(8,128)(2,1)S(1)} %copy-done, bf16[2,128,2048]{2,1,0:T(8,128)(2,1)S(1)} %collective-permute-done.8.from_far_a, bf16[2,128,2048]{2,1,0:T(8,128)(2,1)S(1)} %copy-done.1, ...), custom_call_target="tpu_custom_call" | custom-call | bytes 7400000 | tf_op jit(solution)/shard_map/pallas_call | solution.py:270
  65.8 0.4 collective-permute-start.10
  66.3 2.2 %collective-permute-start.13 = (bf16[2,128,2048]{2,1,0:T(8,128)(2,1)}, bf16[2,128,2048]{2,1,0:T(8,128)(2,1)}, u32[]{:S(2)}, u32[]{:S(2)}) collective-permute-start(bf16[2,128,2048]{2,1,0:T(8,128)(2,1)} %get-tuple-element.31), channel_id=1, source_target_pairs={{0,12},{1,13},{2,14},{3,15},{4,0},{5,1},{6,2},{7,3},{8,4},{9,5},{1... | collective-permute-start | bytes 3145736 | tf_op jit(solution)/shard_map/ppermute | solution.py:299
  68.5 27.6 %all_to_all.10 = f32[128,4,128]{2,1,0:T(4,128)S(1)} all-to-all(f32[128,4,128]{2,1,0:T(4,128)S(1)} %bitcast.50), channel_id=1, replica_groups=mesh['sect'=8,'rows'=16] {'sect','rows'}, dimensions={0} | all-to-all | bytes 524288 | tf_op jit(solution)/shard_map/all_to_all | solution.py:308
  96.2 0.1 reduce_sum.19._
  96.3 0.0 collective-permute-done.11.up_b
  96.3 0.0 collective-permute-done.12.down_a
  96.3 0.0 collective-permute-done.10.up_a
  96.3 0.0 collective-permute-done.13.down_b
  96.3 0.0 copy-done.3
  96.3 0.0 copy-done.4
  96.4 3.1 %shard_map.82 = (bf16[128,2048]{1,0:T(8,128)(2,1)S(1)}, bf16[128,2048]{1,0:T(8,128)(2,1)S(1)}, bf16[128,2048]{1,0:T(8,128)(2,1)S(1)}, f32[128,2048]{1,0:T(8,128)S(1)}) custom-call(bf16[2,128,2048]{2,1,0:T(8,128)(2,1)S(1)} %copy-done.3, bf16[2,128,2048]{2,1,0:T(8,128)(2,1)S(1)} %copy-done.4, bf16[2,128,2048]{2,1,0:T(8,128)(2,1)} %collective-permute-done.10.up_a, ...), custom_call_target="tpu_custom_call" | custom-call | bytes 11100000 | tf_op jit(solution)/shard_map/pallas_call | solution.py:338
  99.4 1.4 %collective-permute-start.14 = (bf16[128,2048]{1,0:T(8,128)(2,1)S(1)}, bf16[128,2048]{1,0:T(8,128)(2,1)S(1)}, u32[]{:S(2)}, u32[]{:S(2)}) collective-permute-start(bf16[128,2048]{1,0:T(8,128)(2,1)S(1)} %get-tuple-element.33), channel_id=1, source_target_pairs={{0,2},{1,3},{2,0},{3,1},{4,6},{5,7},{6,4},{7,5},{8,10},{9,11},{10,... | collective-permute-start | bytes 1572872 | tf_op jit(solution)/shard_map/ppermute | solution.py:299
  100.8 0.8 collective-permute-start.15
  101.7 1.8 %collective-permute-start.16 = (bf16[128,2048]{1,0:T(8,128)(2,1)S(1)}, bf16[128,2048]{1,0:T(8,128)(2,1)S(1)}, u32[]{:S(2)}, u32[]{:S(2)}) collective-permute-start(bf16[128,2048]{1,0:T(8,128)(2,1)S(1)} %get-tuple-element.35), channel_id=1, source_target_pairs={{0,3},{1,0},{2,1},{3,2},{4,7},{5,4},{6,5},{7,6},{8,11},{9,8},{10,9... | collective-permute-start | bytes 1572872 | tf_op jit(solution)/shard_map/ppermute | solution.py:299
  103.6 17.1 %all_to_all.11 = f32[128,4,128]{2,1,0:T(4,128)S(1)} all-to-all(f32[128,4,128]{2,1,0:T(4,128)S(1)} %broadcast_in_dim.5), channel_id=1, replica_groups=mesh['sect'=8,'rows'=16] {'sect','rows'}, dimensions={0} | all-to-all | bytes 524288 | tf_op jit(solution)/shard_map/all_to_all | solution.py:312
  120.7 0.0 collective-permute-done.14
  120.7 0.0 collective-permute-done.15
  120.7 0.0 collective-permute-done.16
  120.7 1.3 %add_add_fusion = f32[128,2048]{1,0:T(8,128)} fusion(f32[128,2048]{1,0:T(8,128)S(1)} %get-tuple-element.32, bf16[128,2048]{1,0:T(8,128)(2,1)S(1)} %collective-permute-done.16, bf16[128,2048]{1,0:T(8,128)(2,1)S(1)} %collective-permute-done.15, bf16[128,2048]{1,0:T(8,128)(2,1)S(1)} %collective-permute-done.14), kind=kLoop, calls=%fused_computation.6 | loop fusion | flops 1572864 | bytes 3670016 | tf_op jit(solution)/shard_map/add | solution.py:388
  121.9 0.7 copy.13
  (6 shorter events, 0.1 us)
Async XLA Ops:
  2.4 25.2 %collective-permute-start.1 = (bf16[17,128,128]{2,1,0:T(8,128)(2,1)S(1)}, bf16[17,128,128]{2,1,0:T(8,128)(2,1)S(1)}, u32[]{:S(2)}, u32[]{:S(2)}) collective-permute-start(bf16[17,128,128]{2,1,0:T(8,128)(2,1)S(1)} %fusion.2.own_ref), channel_id=1, source_target_pairs={{1,0},{2,1},{3,2},{4,3},{5,4},{6,5},{7,6},{8,7},{9,8},{10,9},{11,1... | collective-permute-start | bytes 1671176 | tf_op jit(solution)/shard_map/ppermute | solution.py:363
  4.6 13.2 %collective-permute-start.3 = (f16[128,256]{1,0:T(8,128)(2,1)S(1)}, f16[128,256]{1,0:T(8,128)(2,1)S(1)}, u32[]{:S(2)}, u32[]{:S(2)}) collective-permute-start(f16[128,256]{1,0:T(8,128)(2,1)S(1)} %multiply_convert_fusion), channel_id=1, source_target_pairs={{0,8},{1,9},{2,10},{3,11},{4,12},{5,13},{6,14},{7,15},{8,0},{9,1},... | collective-permute-start | bytes 196616 | tf_op jit(solution)/shard_map/ppermute | solution.py:299
  9.2 13.4 %collective-permute-start.2 = (f16[128,256]{1,0:T(8,128)(2,1)S(1)}, f16[128,256]{1,0:T(8,128)(2,1)S(1)}, u32[]{:S(2)}, u32[]{:S(2)}) collective-permute-start(f16[128,256]{1,0:T(8,128)(2,1)S(1)} %multiply_convert_fusion), channel_id=1, source_target_pairs={{0,12},{1,13},{2,14},{3,15},{4,0},{5,1},{6,2},{7,3},{8,4},{9,5},{1... | collective-permute-start | bytes 196616 | tf_op jit(solution)/shard_map/ppermute | solution.py:299
  9.8 12.8 %collective-permute-start.4 = (f16[128,256]{1,0:T(8,128)(2,1)S(1)}, f16[128,256]{1,0:T(8,128)(2,1)S(1)}, u32[]{:S(2)}, u32[]{:S(2)}) collective-permute-start(f16[128,256]{1,0:T(8,128)(2,1)S(1)} %multiply_convert_fusion), channel_id=1, source_target_pairs={{0,4},{1,5},{2,6},{3,7},{4,8},{5,9},{6,10},{7,11},{8,12},{9,13},{1... | collective-permute-start | bytes 196616 | tf_op jit(solution)/shard_map/ppermute | solution.py:299
  10.7 16.9 %collective-permute-start = (bf16[17,128,128]{2,1,0:T(8,128)(2,1)S(1)}, bf16[17,128,128]{2,1,0:T(8,128)(2,1)S(1)}, u32[]{:S(2)}, u32[]{:S(2)}) collective-permute-start(bf16[17,128,128]{2,1,0:T(8,128)(2,1)S(1)} %fusion.2.own_ref), channel_id=1, source_target_pairs={{0,1},{1,2},{2,3},{3,4},{4,5},{5,6},{6,7},{7,8},{8,9},{9,10},{10,1... | collective-permute-start | bytes 1671176 | tf_op jit(solution)/shard_map/ppermute | solution.py:363
  22.7 24.0 %collective-permute-start.7 = (f16[4,128,256]{2,1,0:T(8,128)(2,1)S(1)}, f16[4,128,256]{2,1,0:T(8,128)(2,1)S(1)}, u32[]{:S(2)}, u32[]{:S(2)}) collective-permute-start(f16[4,128,256]{2,1,0:T(8,128)(2,1)S(1)} %get-tuple-element.39), channel_id=1, source_target_pairs={{0,1},{1,2},{2,3},{3,0},{4,5},{5,6},{6,7},{7,4},{8,9},{9,10},{10,1... | collective-permute-start | bytes 786440 | tf_op jit(solution)/shard_map/ppermute | solution.py:299
  24.0 22.7 %collective-permute-start.6 = (f16[4,128,256]{2,1,0:T(8,128)(2,1)S(1)}, f16[4,128,256]{2,1,0:T(8,128)(2,1)S(1)}, u32[]{:S(2)}, u32[]{:S(2)}) collective-permute-start(f16[4,128,256]{2,1,0:T(8,128)(2,1)S(1)} %get-tuple-element.39), channel_id=1, source_target_pairs={{0,2},{1,3},{2,0},{3,1},{4,6},{5,7},{6,4},{7,5},{8,10},{9,11},{10,... | collective-permute-start | bytes 786440 | tf_op jit(solution)/shard_map/ppermute | solution.py:299
  25.6 21.1 %collective-permute-start.5 = (f16[4,128,256]{2,1,0:T(8,128)(2,1)S(1)}, f16[4,128,256]{2,1,0:T(8,128)(2,1)S(1)}, u32[]{:S(2)}, u32[]{:S(2)}) collective-permute-start(f16[4,128,256]{2,1,0:T(8,128)(2,1)S(1)} %get-tuple-element.39), channel_id=1, source_target_pairs={{0,3},{1,0},{2,1},{3,2},{4,7},{5,4},{6,5},{7,6},{8,11},{9,8},{10,9... | collective-permute-start | bytes 786440 | tf_op jit(solution)/shard_map/ppermute | solution.py:299
  47.3 16.2 %collective-permute-start.8 = (bf16[2,128,2048]{2,1,0:T(8,128)(2,1)}, bf16[2,128,2048]{2,1,0:T(8,128)(2,1)S(1)}, u32[]{:S(2)}, u32[]{:S(2)}) collective-permute-start(bf16[2,128,2048]{2,1,0:T(8,128)(2,1)} %get-tuple-element.25.refs_0_), channel_id=1, source_target_pairs={{0,4},{1,5},{2,6},{3,7},{4,8},{5,9},{6,10},{7,11},{8,12},{9,13},{1... | collective-permute-start | bytes 3145736 | tf_op jit(solution)/shard_map/ppermute | solution.py:299
  47.3 16.2 %collective-permute-start.9 = (bf16[2,128,2048]{2,1,0:T(8,128)(2,1)}, bf16[2,128,2048]{2,1,0:T(8,128)(2,1)S(1)}, u32[]{:S(2)}, u32[]{:S(2)}) collective-permute-start(bf16[2,128,2048]{2,1,0:T(8,128)(2,1)} %get-tuple-element.27.refs_1_), channel_id=1, source_target_pairs={{0,12},{1,13},{2,14},{3,15},{4,0},{5,1},{6,2},{7,3},{8,4},{9,5},{1... | collective-permute-start | bytes 3145736 | tf_op jit(solution)/shard_map/ppermute | solution.py:299
  50.4 45.9 %collective-permute-start.11 = (bf16[2,128,2048]{2,1,0:T(8,128)(2,1)}, bf16[2,128,2048]{2,1,0:T(8,128)(2,1)S(1)}, u32[]{:S(2)}, u32[]{:S(2)}) collective-permute-start(bf16[2,128,2048]{2,1,0:T(8,128)(2,1)} %get-tuple-element.28.refs_2_), channel_id=1, source_target_pairs={{0,4},{1,5},{2,6},{3,7},{4,8},{5,9},{6,10},{7,11},{8,12},{9,13},{1... | collective-permute-start | bytes 3145736 | tf_op jit(solution)/shard_map/ppermute | solution.py:299
  50.4 45.9 %collective-permute-start.12 = (bf16[2,128,2048]{2,1,0:T(8,128)(2,1)}, bf16[2,128,2048]{2,1,0:T(8,128)(2,1)}, u32[]{:S(2)}, u32[]{:S(2)}) collective-permute-start(bf16[2,128,2048]{2,1,0:T(8,128)(2,1)} %get-tuple-element.29.refs_3_), channel_id=1, source_target_pairs={{0,12},{1,13},{2,14},{3,15},{4,0},{5,1},{6,2},{7,3},{8,4},{9,5},{1... | collective-permute-start | bytes 3145736 | tf_op jit(solution)/shard_map/ppermute | solution.py:299
  53.5 1.8 %copy-start.2 = (bf16[2,128,2048]{2,1,0:T(8,128)(2,1)S(1)}, bf16[2,128,2048]{2,1,0:T(8,128)(2,1)}, u32[]{:S(2)}) copy-start(bf16[2,128,2048]{2,1,0:T(8,128)(2,1)} %get-tuple-element.25.refs_0_) | copy-start | bytes 3145732
  55.3 8.2 %copy-start = (bf16[2,128,2048]{2,1,0:T(8,128)(2,1)S(1)}, bf16[2,128,2048]{2,1,0:T(8,128)(2,1)}, u32[]{:S(2)}) copy-start(bf16[2,128,2048]{2,1,0:T(8,128)(2,1)} %get-tuple-element.21.refs_4_.up) | copy-start | bytes 3145732
  55.3 8.2 %copy-start.1 = (bf16[2,128,2048]{2,1,0:T(8,128)(2,1)S(1)}, bf16[2,128,2048]{2,1,0:T(8,128)(2,1)}, u32[]{:S(2)}) copy-start(bf16[2,128,2048]{2,1,0:T(8,128)(2,1)} %get-tuple-element.26.refs_5_.down) | copy-start | bytes 3145732
  63.5 32.9 %copy-start.3 = (bf16[2,128,2048]{2,1,0:T(8,128)(2,1)S(1)}, bf16[2,128,2048]{2,1,0:T(8,128)(2,1)}, u32[]{:S(2)}) copy-start(bf16[2,128,2048]{2,1,0:T(8,128)(2,1)} %get-tuple-element.19.refs_6_.own_a) | copy-start | bytes 3145732
  63.5 32.9 %copy-start.4 = (bf16[2,128,2048]{2,1,0:T(8,128)(2,1)S(1)}, bf16[2,128,2048]{2,1,0:T(8,128)(2,1)}, u32[]{:S(2)}) copy-start(bf16[2,128,2048]{2,1,0:T(8,128)(2,1)} %get-tuple-element.20.refs_7_.own_b) | copy-start | bytes 3145732
  65.8 30.5 %collective-permute-start.10 = (bf16[2,128,2048]{2,1,0:T(8,128)(2,1)}, bf16[2,128,2048]{2,1,0:T(8,128)(2,1)}, u32[]{:S(2)}, u32[]{:S(2)}) collective-permute-start(bf16[2,128,2048]{2,1,0:T(8,128)(2,1)} %get-tuple-element.30), channel_id=1, source_target_pairs={{0,4},{1,5},{2,6},{3,7},{4,8},{5,9},{6,10},{7,11},{8,12},{9,13},{1... | collective-permute-start | bytes 3145736 | tf_op jit(solution)/shard_map/ppermute | solution.py:299
  66.3 30.1 %collective-permute-start.13 = (bf16[2,128,2048]{2,1,0:T(8,128)(2,1)}, bf16[2,128,2048]{2,1,0:T(8,128)(2,1)}, u32[]{:S(2)}, u32[]{:S(2)}) collective-permute-start(bf16[2,128,2048]{2,1,0:T(8,128)(2,1)} %get-tuple-element.31), channel_id=1, source_target_pairs={{0,12},{1,13},{2,14},{3,15},{4,0},{5,1},{6,2},{7,3},{8,4},{9,5},{1... | collective-permute-start | bytes 3145736 | tf_op jit(solution)/shard_map/ppermute | solution.py:299
  99.4 21.2 %collective-permute-start.14 = (bf16[128,2048]{1,0:T(8,128)(2,1)S(1)}, bf16[128,2048]{1,0:T(8,128)(2,1)S(1)}, u32[]{:S(2)}, u32[]{:S(2)}) collective-permute-start(bf16[128,2048]{1,0:T(8,128)(2,1)S(1)} %get-tuple-element.33), channel_id=1, source_target_pairs={{0,2},{1,3},{2,0},{3,1},{4,6},{5,7},{6,4},{7,5},{8,10},{9,11},{10,... | collective-permute-start | bytes 1572872 | tf_op jit(solution)/shard_map/ppermute | solution.py:299
  100.8 19.8 %collective-permute-start.15 = (bf16[128,2048]{1,0:T(8,128)(2,1)S(1)}, bf16[128,2048]{1,0:T(8,128)(2,1)S(1)}, u32[]{:S(2)}, u32[]{:S(2)}) collective-permute-start(bf16[128,2048]{1,0:T(8,128)(2,1)S(1)} %get-tuple-element.34), channel_id=1, source_target_pairs={{0,1},{1,2},{2,3},{3,0},{4,5},{5,6},{6,7},{7,4},{8,9},{9,10},{10,1... | collective-permute-start | bytes 1572872 | tf_op jit(solution)/shard_map/ppermute | solution.py:299
  101.7 19.0 %collective-permute-start.16 = (bf16[128,2048]{1,0:T(8,128)(2,1)S(1)}, bf16[128,2048]{1,0:T(8,128)(2,1)S(1)}, u32[]{:S(2)}, u32[]{:S(2)}) collective-permute-start(bf16[128,2048]{1,0:T(8,128)(2,1)S(1)} %get-tuple-element.35), channel_id=1, source_target_pairs={{0,3},{1,0},{2,1},{3,2},{4,7},{5,4},{6,5},{7,6},{8,11},{9,8},{10,9... | collective-permute-start | bytes 1572872 | tf_op jit(solution)/shard_map/ppermute | solution.py:299

commit v9 on v7

--- a/solution.py
+++ b/solution.py
@@ -264,7 +264,7 @@
 
 
 def joined(up, from_far_a, down, from_far_b, after_this):
-    rows = 32
+    rows = 64
     part = pl.BlockSpec((2, rows, WIDTH), lambda j: (0, j, 0))
     return pl.pallas_call(
         joined_body,
@@ -330,7 +330,7 @@
 
 
 def reduced(own_a, own_b, up_a, up_b, down_a, down_b, after_this):
-    rows = 64
+    rows = 128
     pair = pl.BlockSpec((2, rows, WIDTH), lambda j: (0, j, 0))
     one = pl.BlockSpec((rows, WIDTH), lambda j: (j, 0))
     shape = (TILE, WIDTH)

time: 122 us -> 123 us (level)
  no operation moved by 1% of the time
where the time goes in v9:
time: 123 us; the launch traced here: 122 us
  blocking collectives  45 us (37%)
  Pallas kernels  33.9 us (28%)
  starting transfers between devices  27.5 us (22%)
  other arithmetic  7.9 us (6%)
  waiting for transfers between devices  4.76 us (4%)
  local copies, waits for them, and re-layouts  2.16 us (2%)
    all_to_all x1, blocking collectives, share_out(): return jnp.sum(lax.all_to_all(pieces, ('sect', 'rows'), 0, 0), axis=0)  28.2 us
    ppermute x15, starting transfers between devices, send(): return lax.ppermute(value, ('sect', 'rows'), STEPS[second][by])  23.6 us
    pallas_call x1, Pallas kernels, galerkin(): pl.pallas_call(galerkin_body, out_shape=[jax.ShapeDtypeStruct((2, TILE, W...  18.3 us
    all_to_all x1, blocking collectives, bring_back(): lax.all_to_all(jnp.broadcast_to(piece[None], (128,) + piece.shape), ('sec...  16.9 us
    pallas_call x1, Pallas kernels, coarsest_term(): pl.pallas_call(coarsest_body, out_shape=jax.ShapeDtypeStruct((C2, C2), jn...  8.16 us
    ppermute x15, waiting for transfers between devices, send(): return lax.ppermute(value, ('sect', 'rows'), STEPS[second][by])  4.75 us
    pallas_call x1, Pallas kernels, row_plan(): pl.pallas_call(plan_body, out_shape=jax.ShapeDtypeStruct((RB + 1, 32), jn...  2.91 us
    ppermute x1, starting transfers between devices, per_device(): lax.ppermute(own, 'rows', up)  2.62 us
  transfers between devices with their start and end apart: 17, of which 1 were waited for; matrix products, arithmetic and copies ran while one was open for 4% of the time, Pallas kernels for 26%

profile of v9, /device:TPU:1, one launch (start us, length us, event | category | flops | bytes accessed | tf_op | source)
XLA Modules:
  0.0 122.1 jit_solution(4162850601311457474)
XLA Ops:
  0.6 0.7 subtract_bitcast_fusion
  1.3 1.1 fusion.2.own_ref
  2.4 1.3 %collective-permute-start.1 = (bf16[17,128,128]{2,1,0:T(8,128)(2,1)S(1)}, bf16[17,128,128]{2,1,0:T(8,128)(2,1)S(1)}, u32[]{:S(2)}, u32[]{:S(2)}) collective-permute-start(bf16[17,128,128]{2,1,0:T(8,128)(2,1)S(1)} %fusion.2.own_ref), channel_id=1, source_target_pairs={{1,0},{2,1},{3,2},{4,3},{5,4},{6,5},{7,6},{8,7},{9,8},{10,9},{11,1... | collective-permute-start | bytes 1671176 | tf_op jit(solution)/shard_map/ppermute | solution.py:362
  3.7 0.9 multiply_convert_fusion
  4.6 4.6 %collective-permute-start.3 = (f16[128,256]{1,0:T(8,128)(2,1)S(1)}, f16[128,256]{1,0:T(8,128)(2,1)S(1)}, u32[]{:S(2)}, u32[]{:S(2)}) collective-permute-start(f16[128,256]{1,0:T(8,128)(2,1)S(1)} %multiply_convert_fusion), channel_id=1, source_target_pairs={{0,8},{1,9},{2,10},{3,11},{4,12},{5,13},{6,14},{7,15},{8,0},{9,1},... | collective-permute-start | bytes 196616 | tf_op jit(solution)/shard_map/ppermute | solution.py:298
  9.2 0.6 collective-permute-start.2
  9.8 0.8 collective-permute-start.4
  10.7 2.6 %collective-permute-start = (bf16[17,128,128]{2,1,0:T(8,128)(2,1)S(1)}, bf16[17,128,128]{2,1,0:T(8,128)(2,1)S(1)}, u32[]{:S(2)}, u32[]{:S(2)}) collective-permute-start(bf16[17,128,128]{2,1,0:T(8,128)(2,1)S(1)} %fusion.2.own_ref), channel_id=1, source_target_pairs={{0,1},{1,2},{2,3},{3,4},{4,5},{5,6},{6,7},{7,8},{8,9},{9,10},{10,1... | collective-permute-start | bytes 1671176 | tf_op jit(solution)/shard_map/ppermute | solution.py:362
  13.3 0.9 fusion.8
  14.3 0.7 stack.63.info
  15.0 2.9 %shard_map.77.table = s32[17,32]{1,0:T(8,128)} custom-call(s32[16,27]{1,0:T(8,128)} %cols.1, s32[16]{0:T(128)} %counts.1, s32[16]{0:T(128)} %own_map.1, s32[8]{0:T(128)} %stack.63.info), custom_call_target="tpu_custom_call" | custom-call | bytes 11100000 | tf_op jit(solution)/shard_map/pallas_call | solution.py:66
  17.9 0.0 collective-permute-done.3
  17.9 4.7 %collective-permute-done.2 = f16[128,256]{1,0:T(8,128)(2,1)S(1)} collective-permute-done((f16[128,256]{1,0:T(8,128)(2,1)S(1)}, f16[128,256]{1,0:T(8,128)(2,1)S(1)}, u32[]{:S(2)}, u32[]{:S(2)}) %collective-permute-start.2) | collective-permute-done | bytes 65568 | tf_op jit(solution)/shard_map/ppermute | solution.py:298
  22.6 0.0 collective-permute-done.4
  22.6 0.1 fusion.7
  22.7 1.3 %collective-permute-start.7 = (f16[4,128,256]{2,1,0:T(8,128)(2,1)S(1)}, f16[4,128,256]{2,1,0:T(8,128)(2,1)S(1)}, u32[]{:S(2)}, u32[]{:S(2)}) collective-permute-start(f16[4,128,256]{2,1,0:T(8,128)(2,1)S(1)} %get-tuple-element.39), channel_id=1, source_target_pairs={{0,1},{1,2},{2,3},{3,0},{4,5},{5,6},{6,7},{7,4},{8,9},{9,10},{10,1... | collective-permute-start | bytes 786440 | tf_op jit(solution)/shard_map/ppermute | solution.py:298
  24.0 1.6 %collective-permute-start.6 = (f16[4,128,256]{2,1,0:T(8,128)(2,1)S(1)}, f16[4,128,256]{2,1,0:T(8,128)(2,1)S(1)}, u32[]{:S(2)}, u32[]{:S(2)}) collective-permute-start(f16[4,128,256]{2,1,0:T(8,128)(2,1)S(1)} %get-tuple-element.39), channel_id=1, source_target_pairs={{0,2},{1,3},{2,0},{3,1},{4,6},{5,7},{6,4},{7,5},{8,10},{9,11},{10,... | collective-permute-start | bytes 786440 | tf_op jit(solution)/shard_map/ppermute | solution.py:298
  25.6 2.0 %collective-permute-start.5 = (f16[4,128,256]{2,1,0:T(8,128)(2,1)S(1)}, f16[4,128,256]{2,1,0:T(8,128)(2,1)S(1)}, u32[]{:S(2)}, u32[]{:S(2)}) collective-permute-start(f16[4,128,256]{2,1,0:T(8,128)(2,1)S(1)} %get-tuple-element.39), channel_id=1, source_target_pairs={{0,3},{1,0},{2,1},{3,2},{4,7},{5,4},{6,5},{7,6},{8,11},{9,8},{10,9... | collective-permute-start | bytes 786440 | tf_op jit(solution)/shard_map/ppermute | solution.py:298
  27.6 0.0 collective-permute-done.1.right_ref
  27.6 0.0 collective-permute-done.left_ref
  27.6 0.0 copy-start.5
  27.6 0.7 copy-done.5
  28.3 18.3 %shard_map.78 = (bf16[2,128,2048]{2,1,0:T(8,128)(2,1)}, bf16[2,128,2048]{2,1,0:T(8,128)(2,1)}, bf16[2,128,2048]{2,1,0:T(8,128)(2,1)}, bf16[2,128,2048]{2,1,0:T(8...) custom-call(s32[17,32]{1,0:T(8,128)S(1)} %copy-done.5, ...), custom_call_target="tpu_custom_call" | custom-call | bytes 74000000 | tf_op jit(solution)/shard_map/pallas_call | solution.py:156
  46.6 0.0 collective-permute-done.7
  46.6 0.0 collective-permute-done.6
  46.7 0.0 collective-permute-done.5
  46.7 0.6 fusion.3.refs_2_
  47.3 0.0 collective-permute-start.8
  47.3 2.9 %collective-permute-start.9 = (bf16[2,128,2048]{2,1,0:T(8,128)(2,1)}, bf16[2,128,2048]{2,1,0:T(8,128)(2,1)S(1)}, u32[]{:S(2)}, u32[]{:S(2)}) collective-permute-start(bf16[2,128,2048]{2,1,0:T(8,128)(2,1)} %get-tuple-element.27.refs_1_), channel_id=1, source_target_pairs={{0,12},{1,13},{2,14},{3,15},{4,0},{5,1},{6,2},{7,3},{8,4},{9,5},{1... | collective-permute-start | bytes 3145736 | tf_op jit(solution)/shard_map/ppermute | solution.py:298
  50.2 0.0 collective-permute-start.11
  50.2 2.7 %collective-permute-start.12 = (bf16[2,128,2048]{2,1,0:T(8,128)(2,1)}, bf16[2,128,2048]{2,1,0:T(8,128)(2,1)}, u32[]{:S(2)}, u32[]{:S(2)}) collective-permute-start(bf16[2,128,2048]{2,1,0:T(8,128)(2,1)} %get-tuple-element.29.refs_3_), channel_id=1, source_target_pairs={{0,12},{1,13},{2,14},{3,15},{4,0},{5,1},{6,2},{7,3},{8,4},{9,5},{1... | collective-permute-start | bytes 3145736 | tf_op jit(solution)/shard_map/ppermute | solution.py:298
  52.8 0.3 convert_multiply_fusion
  53.2 0.0 copy-start.2
  53.2 0.0 copy-start.6
  53.2 1.9 %fusion = (bf16[16,128,256]{2,1,0:T(8,128)(2,1)}, bf16[16,128,256]{2,1,0:T(8,128)(2,1)}) fusion(f32[4,4,128,256]{3,2,1,0:T(8,128)S(1)} %convert_multiply_fusion), kind=kLoop, calls=%fused_computation.2 | loop fusion | flops 2097152 | bytes 4194304 | tf_op jit(solution)/shard_map/convert_element_type | solution.py:372
  55.1 0.0 copy-done.2
  55.1 0.0 copy-done.6
  55.1 0.0 copy-start.1
  55.1 8.2 %shard_map.80._ = f32[256,256]{1,0:T(8,128)S(1)} custom-call(s32[17,32]{1,0:T(8,128)S(1)} %copy-done.6, bf16[2,128,2048]{2,1,0:T(8,128)(2,1)S(1)} %copy-done.2, bf16[2,128,2048]{2,1,0:T(8,128)(2,1)} %get-tuple-element.27.refs_1_, bf16[2,128,2048]{2,1,0:T(8,128)(2,1)} %get-tuple-element.28.refs_2_, bf16[2,128,2048]{2,1,0:T(8,128)(2,1)} %get-tuple-element.29.refs_3_, ...), custom_call_target="tpu_custom_call" | custom-call | bytes 22200000 | tf_op jit(solution)/shard_map/pallas_call | solution.py:224
  63.3 0.0 copy-start.3
  63.3 0.0 copy-start.4
  63.3 0.0 collective-permute-done.8.from_far_a
  63.3 0.0 collective-permute-done.9.from_far_b
  63.3 0.0 copy-done
  63.3 0.0 copy-done.1
  63.3 1.9 %shard_map.81 = (bf16[2,128,2048]{2,1,0:T(8,128)(2,1)}, bf16[2,128,2048]{2,1,0:T(8,128)(2,1)}) custom-call(bf16[2,128,2048]{2,1,0:T(8,128)(2,1)S(1)} %copy-done, bf16[2,128,2048]{2,1,0:T(8,128)(2,1)S(1)} %collective-permute-done.8.from_far_a, bf16[2,128,2048]{2,1,0:T(8,128)(2,1)S(1)} %copy-done.1, ...), custom_call_target="tpu_custom_call" | custom-call | bytes 7400000 | tf_op jit(solution)/shard_map/pallas_call | solution.py:269
  65.3 0.4 collective-permute-start.10
  65.6 2.3 %collective-permute-start.13 = (bf16[2,128,2048]{2,1,0:T(8,128)(2,1)}, bf16[2,128,2048]{2,1,0:T(8,128)(2,1)}, u32[]{:S(2)}, u32[]{:S(2)}) collective-permute-start(bf16[2,128,2048]{2,1,0:T(8,128)(2,1)} %get-tuple-element.31), channel_id=1, source_target_pairs={{0,12},{1,13},{2,14},{3,15},{4,0},{5,1},{6,2},{7,3},{8,4},{9,5},{1... | collective-permute-start | bytes 3145736 | tf_op jit(solution)/shard_map/ppermute | solution.py:298
  67.9 28.2 %all_to_all.10 = f32[128,4,128]{2,1,0:T(4,128)S(1)} all-to-all(f32[128,4,128]{2,1,0:T(4,128)S(1)} %bitcast.50), channel_id=1, replica_groups=mesh['sect'=8,'rows'=16] {'sect','rows'}, dimensions={0} | all-to-all | bytes 524288 | tf_op jit(solution)/shard_map/all_to_all | solution.py:307
  96.1 0.1 reduce_sum.19._
  96.3 0.0 collective-permute-done.11.up_b
  96.3 0.0 collective-permute-done.12.down_a
  96.3 0.0 collective-permute-done.10.up_a
  96.3 0.0 collective-permute-done.13.down_b
  96.3 2.6 %shard_map.82 = (bf16[128,2048]{1,0:T(8,128)(2,1)S(1)}, bf16[128,2048]{1,0:T(8,128)(2,1)S(1)}, bf16[128,2048]{1,0:T(8,128)(2,1)S(1)}, f32[128,2048]{1,0:T(8,128)S(1)}) custom-call(bf16[2,128,2048]{2,1,0:T(8,128)(2,1)S(1)} %copy-done.3, bf16[2,128,2048]{2,1,0:T(8,128)(2,1)S(1)} %copy-done.4, bf16[2,128,2048]{2,1,0:T(8,128)(2,1)} %collective-permute-done.10.up_a, ...), custom_call_target="tpu_custom_call" | custom-call | bytes 11100000 | tf_op jit(solution)/shard_map/pallas_call | solution.py:337
  98.9 1.7 %collective-permute-start.14 = (bf16[128,2048]{1,0:T(8,128)(2,1)S(1)}, bf16[128,2048]{1,0:T(8,128)(2,1)S(1)}, u32[]{:S(2)}, u32[]{:S(2)}) collective-permute-start(bf16[128,2048]{1,0:T(8,128)(2,1)S(1)} %get-tuple-element.33), channel_id=1, source_target_pairs={{0,2},{1,3},{2,0},{3,1},{4,6},{5,7},{6,4},{7,5},{8,10},{9,11},{10,... | collective-permute-start | bytes 1572872 | tf_op jit(solution)/shard_map/ppermute | solution.py:298
  100.6 0.8 collective-permute-start.15
  101.4 1.8 %collective-permute-start.16 = (bf16[128,2048]{1,0:T(8,128)(2,1)S(1)}, bf16[128,2048]{1,0:T(8,128)(2,1)S(1)}, u32[]{:S(2)}, u32[]{:S(2)}) collective-permute-start(bf16[128,2048]{1,0:T(8,128)(2,1)S(1)} %get-tuple-element.35), channel_id=1, source_target_pairs={{0,3},{1,0},{2,1},{3,2},{4,7},{5,4},{6,5},{7,6},{8,11},{9,8},{10,9... | collective-permute-start | bytes 1572872 | tf_op jit(solution)/shard_map/ppermute | solution.py:298
  103.3 16.9 %all_to_all.11 = f32[128,4,128]{2,1,0:T(4,128)S(1)} all-to-all(f32[128,4,128]{2,1,0:T(4,128)S(1)} %broadcast_in_dim.5), channel_id=1, replica_groups=mesh['sect'=8,'rows'=16] {'sect','rows'}, dimensions={0} | all-to-all | bytes 524288 | tf_op jit(solution)/shard_map/all_to_all | solution.py:311
  120.1 0.0 collective-permute-done.14
  120.1 0.0 collective-permute-done.15
  120.1 0.0 collective-permute-done.16
  120.1 1.3 %add_add_fusion = f32[128,2048]{1,0:T(8,128)} fusion(f32[128,2048]{1,0:T(8,128)S(1)} %get-tuple-element.32, bf16[128,2048]{1,0:T(8,128)(2,1)S(1)} %collective-permute-done.16, bf16[128,2048]{1,0:T(8,128)(2,1)S(1)} %collective-permute-done.15, bf16[128,2048]{1,0:T(8,128)(2,1)S(1)} %collective-permute-done.14), kind=kLoop, calls=%fused_computation.6 | loop fusion | flops 1572864 | bytes 3670016 | tf_op jit(solution)/shard_map/add | solution.py:387
  121.4 0.7 copy.13
  (9 shorter events, 0.1 us)
Async XLA Ops:
  2.4 25.2 %collective-permute-start.1 = (bf16[17,128,128]{2,1,0:T(8,128)(2,1)S(1)}, bf16[17,128,128]{2,1,0:T(8,128)(2,1)S(1)}, u32[]{:S(2)}, u32[]{:S(2)}) collective-permute-start(bf16[17,128,128]{2,1,0:T(8,128)(2,1)S(1)} %fusion.2.own_ref), channel_id=1, source_target_pairs={{1,0},{2,1},{3,2},{4,3},{5,4},{6,5},{7,6},{8,7},{9,8},{10,9},{11,1... | collective-permute-start | bytes 1671176 | tf_op jit(solution)/shard_map/ppermute | solution.py:362
  4.6 13.3 %collective-permute-start.3 = (f16[128,256]{1,0:T(8,128)(2,1)S(1)}, f16[128,256]{1,0:T(8,128)(2,1)S(1)}, u32[]{:S(2)}, u32[]{:S(2)}) collective-permute-start(f16[128,256]{1,0:T(8,128)(2,1)S(1)} %multiply_convert_fusion), channel_id=1, source_target_pairs={{0,8},{1,9},{2,10},{3,11},{4,12},{5,13},{6,14},{7,15},{8,0},{9,1},... | collective-permute-start | bytes 196616 | tf_op jit(solution)/shard_map/ppermute | solution.py:298
  9.2 13.4 %collective-permute-start.2 = (f16[128,256]{1,0:T(8,128)(2,1)S(1)}, f16[128,256]{1,0:T(8,128)(2,1)S(1)}, u32[]{:S(2)}, u32[]{:S(2)}) collective-permute-start(f16[128,256]{1,0:T(8,128)(2,1)S(1)} %multiply_convert_fusion), channel_id=1, source_target_pairs={{0,12},{1,13},{2,14},{3,15},{4,0},{5,1},{6,2},{7,3},{8,4},{9,5},{1... | collective-permute-start | bytes 196616 | tf_op jit(solution)/shard_map/ppermute | solution.py:298
  9.8 12.8 %collective-permute-start.4 = (f16[128,256]{1,0:T(8,128)(2,1)S(1)}, f16[128,256]{1,0:T(8,128)(2,1)S(1)}, u32[]{:S(2)}, u32[]{:S(2)}) collective-permute-start(f16[128,256]{1,0:T(8,128)(2,1)S(1)} %multiply_convert_fusion), channel_id=1, source_target_pairs={{0,4},{1,5},{2,6},{3,7},{4,8},{5,9},{6,10},{7,11},{8,12},{9,13},{1... | collective-permute-start | bytes 196616 | tf_op jit(solution)/shard_map/ppermute | solution.py:298
  10.7 16.9 %collective-permute-start = (bf16[17,128,128]{2,1,0:T(8,128)(2,1)S(1)}, bf16[17,128,128]{2,1,0:T(8,128)(2,1)S(1)}, u32[]{:S(2)}, u32[]{:S(2)}) collective-permute-start(bf16[17,128,128]{2,1,0:T(8,128)(2,1)S(1)} %fusion.2.own_ref), channel_id=1, source_target_pairs={{0,1},{1,2},{2,3},{3,4},{4,5},{5,6},{6,7},{7,8},{8,9},{9,10},{10,1... | collective-permute-start | bytes 1671176 | tf_op jit(solution)/shard_map/ppermute | solution.py:362
  22.7 23.9 %collective-permute-start.7 = (f16[4,128,256]{2,1,0:T(8,128)(2,1)S(1)}, f16[4,128,256]{2,1,0:T(8,128)(2,1)S(1)}, u32[]{:S(2)}, u32[]{:S(2)}) collective-permute-start(f16[4,128,256]{2,1,0:T(8,128)(2,1)S(1)} %get-tuple-element.39), channel_id=1, source_target_pairs={{0,1},{1,2},{2,3},{3,0},{4,5},{5,6},{6,7},{7,4},{8,9},{9,10},{10,1... | collective-permute-start | bytes 786440 | tf_op jit(solution)/shard_map/ppermute | solution.py:298
  24.0 22.7 %collective-permute-start.6 = (f16[4,128,256]{2,1,0:T(8,128)(2,1)S(1)}, f16[4,128,256]{2,1,0:T(8,128)(2,1)S(1)}, u32[]{:S(2)}, u32[]{:S(2)}) collective-permute-start(f16[4,128,256]{2,1,0:T(8,128)(2,1)S(1)} %get-tuple-element.39), channel_id=1, source_target_pairs={{0,2},{1,3},{2,0},{3,1},{4,6},{5,7},{6,4},{7,5},{8,10},{9,11},{10,... | collective-permute-start | bytes 786440 | tf_op jit(solution)/shard_map/ppermute | solution.py:298
  25.6 21.1 %collective-permute-start.5 = (f16[4,128,256]{2,1,0:T(8,128)(2,1)S(1)}, f16[4,128,256]{2,1,0:T(8,128)(2,1)S(1)}, u32[]{:S(2)}, u32[]{:S(2)}) collective-permute-start(f16[4,128,256]{2,1,0:T(8,128)(2,1)S(1)} %get-tuple-element.39), channel_id=1, source_target_pairs={{0,3},{1,0},{2,1},{3,2},{4,7},{5,4},{6,5},{7,6},{8,11},{9,8},{10,9... | collective-permute-start | bytes 786440 | tf_op jit(solution)/shard_map/ppermute | solution.py:298
  27.6 0.7 copy-start.5
  47.3 16.0 %collective-permute-start.8 = (bf16[2,128,2048]{2,1,0:T(8,128)(2,1)}, bf16[2,128,2048]{2,1,0:T(8,128)(2,1)S(1)}, u32[]{:S(2)}, u32[]{:S(2)}) collective-permute-start(bf16[2,128,2048]{2,1,0:T(8,128)(2,1)} %get-tuple-element.25.refs_0_), channel_id=1, source_target_pairs={{0,4},{1,5},{2,6},{3,7},{4,8},{5,9},{6,10},{7,11},{8,12},{9,13},{1... | collective-permute-start | bytes 3145736 | tf_op jit(solution)/shard_map/ppermute | solution.py:298
  47.3 16.1 %collective-permute-start.9 = (bf16[2,128,2048]{2,1,0:T(8,128)(2,1)}, bf16[2,128,2048]{2,1,0:T(8,128)(2,1)S(1)}, u32[]{:S(2)}, u32[]{:S(2)}) collective-permute-start(bf16[2,128,2048]{2,1,0:T(8,128)(2,1)} %get-tuple-element.27.refs_1_), channel_id=1, source_target_pairs={{0,12},{1,13},{2,14},{3,15},{4,0},{5,1},{6,2},{7,3},{8,4},{9,5},{1... | collective-permute-start | bytes 3145736 | tf_op jit(solution)/shard_map/ppermute | solution.py:298
  50.2 46.1 %collective-permute-start.11 = (bf16[2,128,2048]{2,1,0:T(8,128)(2,1)}, bf16[2,128,2048]{2,1,0:T(8,128)(2,1)S(1)}, u32[]{:S(2)}, u32[]{:S(2)}) collective-permute-start(bf16[2,128,2048]{2,1,0:T(8,128)(2,1)} %get-tuple-element.28.refs_2_), channel_id=1, source_target_pairs={{0,4},{1,5},{2,6},{3,7},{4,8},{5,9},{6,10},{7,11},{8,12},{9,13},{1... | collective-permute-start | bytes 3145736 | tf_op jit(solution)/shard_map/ppermute | solution.py:298
  50.2 46.1 %collective-permute-start.12 = (bf16[2,128,2048]{2,1,0:T(8,128)(2,1)}, bf16[2,128,2048]{2,1,0:T(8,128)(2,1)}, u32[]{:S(2)}, u32[]{:S(2)}) collective-permute-start(bf16[2,128,2048]{2,1,0:T(8,128)(2,1)} %get-tuple-element.29.refs_3_), channel_id=1, source_target_pairs={{0,12},{1,13},{2,14},{3,15},{4,0},{5,1},{6,2},{7,3},{8,4},{9,5},{1... | collective-permute-start | bytes 3145736 | tf_op jit(solution)/shard_map/ppermute | solution.py:298
  53.2 1.9 %copy-start.2 = (bf16[2,128,2048]{2,1,0:T(8,128)(2,1)S(1)}, bf16[2,128,2048]{2,1,0:T(8,128)(2,1)}, u32[]{:S(2)}) copy-start(bf16[2,128,2048]{2,1,0:T(8,128)(2,1)} %get-tuple-element.25.refs_0_) | copy-start | bytes 3145732
  53.2 1.9 %copy-start.6 = (s32[17,32]{1,0:T(8,128)S(1)}, s32[17,32]{1,0:T(8,128)}, u32[]{:S(2)}) copy-start(s32[17,32]{1,0:T(8,128)} %shard_map.77.table) | copy-start | bytes 6532
  55.1 8.2 %copy-start = (bf16[2,128,2048]{2,1,0:T(8,128)(2,1)S(1)}, bf16[2,128,2048]{2,1,0:T(8,128)(2,1)}, u32[]{:S(2)}) copy-start(bf16[2,128,2048]{2,1,0:T(8,128)(2,1)} %get-tuple-element.21.refs_4_.up) | copy-start | bytes 3145732
  55.1 8.2 %copy-start.1 = (bf16[2,128,2048]{2,1,0:T(8,128)(2,1)S(1)}, bf16[2,128,2048]{2,1,0:T(8,128)(2,1)}, u32[]{:S(2)}) copy-start(bf16[2,128,2048]{2,1,0:T(8,128)(2,1)} %get-tuple-element.26.refs_5_.down) | copy-start | bytes 3145732
  63.3 33.0 %copy-start.3 = (bf16[2,128,2048]{2,1,0:T(8,128)(2,1)S(1)}, bf16[2,128,2048]{2,1,0:T(8,128)(2,1)}, u32[]{:S(2)}) copy-start(bf16[2,128,2048]{2,1,0:T(8,128)(2,1)} %get-tuple-element.19.refs_6_.own_a) | copy-start | bytes 3145732
  63.3 33.0 %copy-start.4 = (bf16[2,128,2048]{2,1,0:T(8,128)(2,1)S(1)}, bf16[2,128,2048]{2,1,0:T(8,128)(2,1)}, u32[]{:S(2)}) copy-start(bf16[2,128,2048]{2,1,0:T(8,128)(2,1)} %get-tuple-element.20.refs_7_.own_b) | copy-start | bytes 3145732
  65.3 31.0 %collective-permute-start.10 = (bf16[2,128,2048]{2,1,0:T(8,128)(2,1)}, bf16[2,128,2048]{2,1,0:T(8,128)(2,1)}, u32[]{:S(2)}, u32[]{:S(2)}) collective-permute-start(bf16[2,128,2048]{2,1,0:T(8,128)(2,1)} %get-tuple-element.30), channel_id=1, source_target_pairs={{0,4},{1,5},{2,6},{3,7},{4,8},{5,9},{6,10},{7,11},{8,12},{9,13},{1... | collective-permute-start | bytes 3145736 | tf_op jit(solution)/shard_map/ppermute | solution.py:298
  65.6 30.6 %collective-permute-start.13 = (bf16[2,128,2048]{2,1,0:T(8,128)(2,1)}, bf16[2,128,2048]{2,1,0:T(8,128)(2,1)}, u32[]{:S(2)}, u32[]{:S(2)}) collective-permute-start(bf16[2,128,2048]{2,1,0:T(8,128)(2,1)} %get-tuple-element.31), channel_id=1, source_target_pairs={{0,12},{1,13},{2,14},{3,15},{4,0},{5,1},{6,2},{7,3},{8,4},{9,5},{1... | collective-permute-start | bytes 3145736 | tf_op jit(solution)/shard_map/ppermute | solution.py:298
  98.9 21.2 %collective-permute-start.14 = (bf16[128,2048]{1,0:T(8,128)(2,1)S(1)}, bf16[128,2048]{1,0:T(8,128)(2,1)S(1)}, u32[]{:S(2)}, u32[]{:S(2)}) collective-permute-start(bf16[128,2048]{1,0:T(8,128)(2,1)S(1)} %get-tuple-element.33), channel_id=1, source_target_pairs={{0,2},{1,3},{2,0},{3,1},{4,6},{5,7},{6,4},{7,5},{8,10},{9,11},{10,... | collective-permute-start | bytes 1572872 | tf_op jit(solution)/shard_map/ppermute | solution.py:298
  100.6 19.6 %collective-permute-start.15 = (bf16[128,2048]{1,0:T(8,128)(2,1)S(1)}, bf16[128,2048]{1,0:T(8,128)(2,1)S(1)}, u32[]{:S(2)}, u32[]{:S(2)}) collective-permute-start(bf16[128,2048]{1,0:T(8,128)(2,1)S(1)} %get-tuple-element.34), channel_id=1, source_target_pairs={{0,1},{1,2},{2,3},{3,0},{4,5},{5,6},{6,7},{7,4},{8,9},{9,10},{10,1... | collective-permute-start | bytes 1572872 | tf_op jit(solution)/shard_map/ppermute | solution.py:298
  101.4 18.7 %collective-permute-start.16 = (bf16[128,2048]{1,0:T(8,128)(2,1)S(1)}, bf16[128,2048]{1,0:T(8,128)(2,1)S(1)}, u32[]{:S(2)}, u32[]{:S(2)}) collective-permute-start(bf16[128,2048]{1,0:T(8,128)(2,1)S(1)} %get-tuple-element.35), channel_id=1, source_target_pairs={{0,3},{1,0},{2,1},{3,2},{4,7},{5,4},{6,5},{7,6},{8,11},{9,8},{10,9... | collective-permute-start | bytes 1572872 | tf_op jit(solution)/shard_map/ppermute | solution.py:298
